TPU v7x, 512 devices: a whole 4x8x8 slice. The times are simulated.
512 devices in a mesh: loop: 32 (over z_hi, x, core), mp: 16 (over z_lo, y).
Axes of the slice: x: 4, y: 8, z: 8 (z_hi: 4, z_lo: 2; z = z_hi * 2 + z_lo), core: 2. Of those that a mesh axis runs over, the one named last changes fastest.
Arguments:
- img_emb: bfloat16 [65536, 1536], P(('loop', 'mp')), may hold values from -0.15625 to 0.15625
- txt_emb: bfloat16 [65536, 1536], P(('loop', 'mp')), may hold values from -0.15625 to 0.15625
- hidden: bfloat16 [65536, 6144], P('loop', 'mp'), may hold values from -6 to 6
- positives: int32 [65536], P(('loop', 'mp')), may hold values from 0 to 65535, as said below
Outputs:
- text_grad: bfloat16 [65536, 1536], P(('loop', 'mp'))
- weight_grad: float32 [6144, 1536], P(('mp', 'loop'))
Inputs may be any that keep to these rules, and one draw needn't show every extreme that they name: `positives`: the positive of an image row in block (g, m) is a text row of block ((g - k) mod 32, m) for some k < 4.
All inputs are finite; a program needn't handle non-finite values.
Results may differ from a plain program's by a relative error of at most 0.0059.
Values may be sent and summed in bfloat16 or wider, within the bound.
No kernel may reach another device: no remote copies, remote signals or barrier semaphores. Data moves between devices by JAX's collectives and lax.ppermute only.
A program may use at most 64 MiB of HBM per device.

v0:
```python
import math

import jax
import jax.numpy as jnp
from jax import lax
from jax.sharding import PartitionSpec as P

STEPS = 4


SCALE_T = 10.0
BIAS_T = -1.0
EPSILON = 1e-06


def passed_along(x, axis, by):
    size = lax.axis_size(axis)
    return lax.ppermute(x, axis, [(i, (i + by) % size) for i in range(size)])


def normalize(values):
    widened = values.astype(jnp.float32)
    inverse = lax.rsqrt(jnp.sum(widened * widened, axis=1, keepdims=True) + EPSILON)
    return (widened * inverse, inverse)


def backward_norm(unit_rows, inverse, upstream):
    return (upstream - unit_rows * jnp.sum(unit_rows * upstream, axis=1, keepdims=True)) * inverse


def pair_terms(image_low, text_low, positives, first_col):
    scores = (
        SCALE_T
        * lax.dot_general(
            image_low, text_low, (((1,), (1,)), ((), ())), preferred_element_type=jnp.float32
        )
        + BIAS_T
    )
    columns = first_col + lax.broadcasted_iota(jnp.int32, scores.shape, 1)
    target = (positives[:, None] == columns).astype(jnp.float32)
    coefficient = (jax.nn.sigmoid(scores) - target).astype(jnp.bfloat16)
    image_part = SCALE_T * jnp.dot(coefficient, text_low, preferred_element_type=jnp.float32)
    text_part = SCALE_T * lax.dot_general(
        coefficient, image_low, (((0,), (0,)), ((), ())), preferred_element_type=jnp.float32
    )
    return (image_part, text_part)


def local(img_emb, txt_emb, hidden, positives):
    loop_index = lax.axis_index("loop")
    model_index = lax.axis_index("mp")
    groups = lax.axis_size("loop")
    splits = lax.axis_size("mp")
    row_count = img_emb.shape[0]
    image_unit, image_inv = normalize(img_emb)
    text_unit, text_inv = normalize(txt_emb)
    image_low = image_unit.astype(jnp.bfloat16)
    text_low = text_unit.astype(jnp.bfloat16)
    blocks_held = [text_low]
    current = text_low
    for offset in range(1, STEPS):
        current = passed_along(current, "loop", 1)
        blocks_held.append(current)
    image_total = jnp.zeros(img_emb.shape, jnp.float32)
    text_parts = []
    for offset in range(STEPS):
        owner = (loop_index - offset) % groups
        first_col = (owner * splits + model_index) * row_count
        image_part, text_part = pair_terms(image_low, blocks_held[offset], positives, first_col)
        image_total = image_total + image_part
        text_parts.append(text_part)
    text_total = text_parts[STEPS - 1]
    for offset in range(STEPS - 2, -1, -1):
        text_total = passed_along(text_total, "loop", -1) + text_parts[offset]
    image_grad = backward_norm(image_unit, image_inv, image_total).astype(jnp.bfloat16)
    text_grad = backward_norm(text_unit, text_inv, text_total).astype(jnp.bfloat16)
    gathered = lax.all_gather(image_grad, "mp", axis=0, tiled=True)
    weight_share = lax.psum_scatter(
        lax.dot_general(
            hidden, gathered, (((0,), (0,)), ((), ())), preferred_element_type=jnp.float32
        ),
        "loop",
        scatter_dimension=0,
        tiled=True,
    )
    batch_rows = row_count * splits * groups
    return (text_grad, weight_share / math.sqrt(batch_rows))


def solution(mesh):
    in_specs = (
        P(("loop", "mp"), None),
        P(("loop", "mp"), None),
        P("loop", "mp"),
        P(("loop", "mp")),
    )
    out_specs = (P(("loop", "mp"), None), P(("mp", "loop"), None))
    return jax.shard_map(local, mesh=mesh, in_specs=in_specs, out_specs=out_specs, check_vma=False)
```

profile of v0, /device:TPU:1, one launch (start us, length us, event | category | flops | bytes accessed | tf_op | source)
XLA Modules:
  0.0 474.9 jit_solution(10071461757545407224)
XLA Ops:
  7.2 1.3 fusion.45
  8.5 1.1 fusion.32
  9.7 4.5 collective-permute-start
  14.3 1.2 fusion.40
  15.5 1.3 fusion.29
  17.1 2.6 collective-permute-done
  19.7 3.6 collective-permute-start.1
  23.9 9.2 %collective-permute-done.1 = bf16[128,1536]{1,0:T(8,128)(2,1)S(1)} collective-permute-done((bf16[128,1536]{1,0:T(8,128)(2,1)S(1)}, bf16[128,1536]{1,0:T(8,128)(2,1)S(1)}, u32[]{:S(2)}, u32[]{:S(2)}) %collective-permute-start.1) | collective-permute-done | bytes 393248 | tf_op jit(solution)/shard_map/ppermute | solution.py:18
  33.1 1.9 collective-permute-start.2
  35.7 12.5 %collective-permute-done.2 = bf16[128,1536]{1,0:T(8,128)(2,1)S(1)} collective-permute-done((bf16[128,1536]{1,0:T(8,128)(2,1)S(1)}, bf16[128,1536]{1,0:T(8,128)(2,1)S(1)}, u32[]{:S(2)}, u32[]{:S(2)}) %collective-permute-start.2) | collective-permute-done | bytes 393248 | tf_op jit(solution)/shard_map/ppermute | solution.py:18
  48.9 1.0 fusion.39
  50.3 12.2 %collective-permute-start.3 = (f32[128,1536]{1,0:T(8,128)S(1)}, f32[128,1536]{1,0:T(8,128)S(1)}, u32[]{:S(2)}, u32[]{:S(2)}) collective-permute-start(f32[128,1536]{1,0:T(8,128)S(1)} %convolution_multiply_fusion.3), channel_id=1, source_target_pairs={{0,496},{16,0},{32,16},{48,32},{64,48},{80,64},{96,80},{112,96},{1... | collective-permute-start | bytes 2359304 | tf_op jit(solution)/shard_map/ppermute | solution.py:18
  62.6 1.9 collective-permute-done.3
  64.8 11.6 %collective-permute-start.4 = (f32[128,1536]{1,0:T(8,128)S(1)}, f32[128,1536]{1,0:T(8,128)}, u32[]{:S(2)}, u32[]{:S(2)}) collective-permute-start(f32[128,1536]{1,0:T(8,128)S(1)} %fusion.1), channel_id=1, source_target_pairs={{0,496},{16,0},{32,16},{48,32},{64,48},{80,64},{96,80},{112,96},{1... | collective-permute-start | bytes 2359304 | tf_op jit(solution)/shard_map/ppermute | solution.py:18
  76.4 76.0 %all-gather.2.cloned.1.call-done = bf16[2048,1536]{1,0:T(8,128)(2,1)} async-done(((bf16[128,1536]{1,0:T(8,128)(2,1)}), bf16[2048,1536]{1,0:T(8,128)(2,1)}) %all-gather.2.cloned.1.call-update) | async-done | bytes 6291472 | tf_op jit(solution)/shard_map/all_gather | solution.py:77
  152.4 7.7 %convolution_bitcast_fusion = f32[384,1536]{0,1:T(8,128)} fusion(bf16[2048,1536]{1,0:T(8,128)(2,1)} %all-gather.2.cloned.1.call-done, bf16[2048,384]{1,0:T(8,128)(2,1)S(1)} %copy-done), kind=kOutput, calls=%fused_computation | convolution fusion | flops 2415919104 | bytes 10223616 | tf_op jit(solution)/shard_map/dot_general | solution.py:79
  160.5 2.1 add.137
  162.6 7.3 %collective-permute-start.5 = (f32[128,1536]{1,0:T(8,128)}, f32[128,1536]{1,0:T(8,128)S(1)}, u32[]{:S(2)}, u32[]{:S(2)}) collective-permute-start(f32[128,1536]{1,0:T(8,128)} %add.137), channel_id=1, source_target_pairs={{0,496},{16,0},{32,16},{48,32},{64,48},{80,64},{96,80},{112,96},{1... | collective-permute-start | bytes 2359304 | tf_op jit(solution)/shard_map/ppermute | solution.py:18
  169.9 1.3 dynamic-slice
  172.1 4.0 collective-permute-done.5
  176.3 1.0 fusion.44
  177.4 288.1 %all-reduce.3.cloned.1.call-done = f32[384,1536]{0,1:T(8,128)} async-done(((f32[384,1536]{0,1:T(8,128)}), f32[384,1536]{0,1:T(8,128)}) %all-reduce.3.cloned.1.call-update) | async-done | bytes 2359312
  465.5 1.7 dynamic-slice_multiply_fusion
  467.2 0.9 copy.7
  (31 shorter events, 3.9 us)
Async XLA Ops:
  7.2 145.2 %copy-start = (bf16[2048,384]{1,0:T(8,128)(2,1)S(1)}, bf16[2048,384]{1,0:T(8,128)(2,1)}, u32[]{:S(2)}) copy-start(bf16[2048,384]{1,0:T(8,128)(2,1)} %param.6) | copy-start | bytes 4718596
  7.2 16.1 %copy-start.1 = (bf16[128,1536]{1,0:T(8,128)(2,1)S(1)}, bf16[128,1536]{1,0:T(8,128)(2,1)}, u32[]{:S(2)}) copy-start(bf16[128,1536]{1,0:T(8,128)(2,1)} %param.4) | copy-start | bytes 1179652
  7.2 16.1 %copy-start.3 = (s32[128]{0:T(128)S(1)}, s32[128]{0:T(128)}, u32[]{:S(2)}) copy-start(s32[128]{0:T(128)} %param.7) | copy-start | bytes 1540
  7.2 145.2 %all-gather.2.cloned.1.call-start = ((), (), s32[]{:S(2)}) async-start(), calls=%async_computation | async-start | bytes 6684672 | tf_op jit(solution)/shard_map/all_gather | solution.py:77
  9.7 10.0 %collective-permute-start = (bf16[128,1536]{1,0:T(8,128)(2,1)S(1)}, bf16[128,1536]{1,0:T(8,128)(2,1)S(1)}, u32[]{:S(2)}, u32[]{:S(2)}) collective-permute-start(bf16[128,1536]{1,0:T(8,128)(2,1)S(1)} %fusion.32), channel_id=1, source_target_pairs={{0,16},{16,32},{32,48},{48,64},{64,80},{80,96},{96,112},{112,128},... | collective-permute-start | bytes 1179656 | tf_op jit(solution)/shard_map/ppermute | solution.py:18
  19.7 13.4 %collective-permute-start.1 = (bf16[128,1536]{1,0:T(8,128)(2,1)S(1)}, bf16[128,1536]{1,0:T(8,128)(2,1)S(1)}, u32[]{:S(2)}, u32[]{:S(2)}) collective-permute-start(bf16[128,1536]{1,0:T(8,128)(2,1)S(1)} %collective-permute-done), channel_id=1, source_target_pairs={{0,16},{16,32},{32,48},{48,64},{64,80},{80,96},{96,112},{112,128},... | collective-permute-start | bytes 1179656 | tf_op jit(solution)/shard_map/ppermute | solution.py:18
  33.1 15.0 %collective-permute-start.2 = (bf16[128,1536]{1,0:T(8,128)(2,1)S(1)}, bf16[128,1536]{1,0:T(8,128)(2,1)S(1)}, u32[]{:S(2)}, u32[]{:S(2)}) collective-permute-start(bf16[128,1536]{1,0:T(8,128)(2,1)S(1)} %collective-permute-done.1), channel_id=1, source_target_pairs={{0,16},{16,32},{32,48},{48,64},{64,80},{80,96},{96,112},{112,128},... | collective-permute-start | bytes 1179656 | tf_op jit(solution)/shard_map/ppermute | solution.py:18
  50.0 415.6 %all-reduce.3.cloned.1.call-start = ((), (), s32[]{:S(2)}) async-start(), calls=%async_computation.1 | async-start | bytes 4718592
  50.3 14.1 %collective-permute-start.3 = (f32[128,1536]{1,0:T(8,128)S(1)}, f32[128,1536]{1,0:T(8,128)S(1)}, u32[]{:S(2)}, u32[]{:S(2)}) collective-permute-start(f32[128,1536]{1,0:T(8,128)S(1)} %convolution_multiply_fusion.3), channel_id=1, source_target_pairs={{0,496},{16,0},{32,16},{48,32},{64,48},{80,64},{96,80},{112,96},{1... | collective-permute-start | bytes 2359304 | tf_op jit(solution)/shard_map/ppermute | solution.py:18
  64.8 95.7 %collective-permute-start.4 = (f32[128,1536]{1,0:T(8,128)S(1)}, f32[128,1536]{1,0:T(8,128)}, u32[]{:S(2)}, u32[]{:S(2)}) collective-permute-start(f32[128,1536]{1,0:T(8,128)S(1)} %fusion.1), channel_id=1, source_target_pairs={{0,496},{16,0},{32,16},{48,32},{64,48},{80,64},{96,80},{112,96},{1... | collective-permute-start | bytes 2359304 | tf_op jit(solution)/shard_map/ppermute | solution.py:18
  160.1 16.0 %copy-start.2 = (bf16[128,1536]{1,0:T(8,128)(2,1)S(1)}, bf16[128,1536]{1,0:T(8,128)(2,1)}, u32[]{:S(2)}) copy-start(bf16[128,1536]{1,0:T(8,128)(2,1)} %param.5) | copy-start | bytes 1179652
  162.6 13.5 %collective-permute-start.5 = (f32[128,1536]{1,0:T(8,128)}, f32[128,1536]{1,0:T(8,128)S(1)}, u32[]{:S(2)}, u32[]{:S(2)}) collective-permute-start(f32[128,1536]{1,0:T(8,128)} %add.137), channel_id=1, source_target_pairs={{0,496},{16,0},{32,16},{48,32},{64,48},{80,64},{96,80},{112,96},{1... | collective-permute-start | bytes 2359304 | tf_op jit(solution)/shard_map/ppermute | solution.py:18
Sparse Core Ops, SparseCore 0:
  50.1 102.2 all-gather.1
  160.2 305.2 all-reduce.2
where the time goes:
time: 475 us
  waiting for transfers between devices  394 us (83%)
  starting transfers between devices  41.2 us (9%)
  between operations  15 us (3%)
  matrix products  12.5 us (3%)
  other arithmetic  9.75 us (2%)
    unnamed x3, waiting for transfers between devices  288 us
    all_gather x1, waiting for transfers between devices, local(): gathered = lax.all_gather(image_grad, 'mp', axis=0, tiled=True)  76 us
    ppermute x6, starting transfers between devices, passed_along(): return lax.ppermute(x, axis, [(i, (i + by) % size) for i in range(size)])  41.1 us
    ppermute x6, waiting for transfers between devices, passed_along(): return lax.ppermute(x, axis, [(i, (i + by) % size) for i in range(size)])  30.1 us
  transfers between devices with their start and end apart: 8, of which 7 were waited for; matrix products, arithmetic and copies ran while one was open for 4% of the time, Pallas kernels for 0%

commit v1 on v0

v1 whole, which is shorter than its diff:
```python
import math

import jax
import jax.numpy as jnp
from jax import lax
from jax.sharding import PartitionSpec as P

SCALE_T = 10.0
BIAS_T = -1.0
EPSILON = 1e-06

Z_HI, X, CORE, Z_LO, Y = 4, 4, 2, 2, 8


def moved(value, where):
    pairs = []
    for source in range(Z_HI * X * CORE * Z_LO * Y):
        rest, y = divmod(source, Y)
        rest, z_lo = divmod(rest, Z_LO)
        rest, core = divmod(rest, CORE)
        z_hi, x = divmod(rest, X)
        a, b, c, d, e = where(z_hi, x, core, z_lo, y)
        pairs.append((source, ((((a % Z_HI) * X + b % X) * CORE + c % CORE) * Z_LO + d % Z_LO) * Y + e % Y))
    return lax.ppermute(value, ("loop", "mp"), pairs)


def next_chip(by):
    def where(z_hi, x, core, z_lo, y):
        chip = z_hi * X + x + by
        return chip // X, chip % X, core, z_lo, y

    return where


def cross(sign):
    def where(z_hi, x, core, z_lo, y):
        chip = z_hi * X + x
        if sign > 0:
            chip += 2 * core
        else:
            chip -= 2 * (1 - core)
        return chip // X, chip % X, 1 - core, z_lo, y

    return where


def other_core(z_hi, x, core, z_lo, y):
    return z_hi, x, 1 - core, z_lo, y


def other_z_lo(z_hi, x, core, z_lo, y):
    return z_hi, x, core, 1 - z_lo, y


def normalize(values):
    widened = values.astype(jnp.float32)
    inverse = lax.rsqrt(jnp.sum(widened * widened, axis=1, keepdims=True) + EPSILON)
    return (widened * inverse, inverse)


def backward_norm(unit_rows, inverse, upstream):
    return (upstream - unit_rows * jnp.sum(unit_rows * upstream, axis=1, keepdims=True)) * inverse


def pair_terms(image_low, text_low, positives, first_col):
    scores = (
        SCALE_T
        * lax.dot_general(
            image_low, text_low, (((1,), (1,)), ((), ())), preferred_element_type=jnp.float32
        )
        + BIAS_T
    )
    columns = first_col + lax.broadcasted_iota(jnp.int32, scores.shape, 1)
    target = (positives[:, None] == columns).astype(jnp.float32)
    coefficient = (jax.nn.sigmoid(scores) - target).astype(jnp.bfloat16)
    image_part = SCALE_T * jnp.dot(coefficient, text_low, preferred_element_type=jnp.float32)
    text_part = SCALE_T * lax.dot_general(
        coefficient, image_low, (((0,), (0,)), ((), ())), preferred_element_type=jnp.float32
    )
    return (image_part, text_part)


def local(img_emb, txt_emb, hidden, positives):
    bf16 = jnp.bfloat16
    loop_index = lax.axis_index("loop")
    model_index = lax.axis_index("mp")
    core = loop_index % CORE
    x = (loop_index // CORE) % X
    z_hi = loop_index // (CORE * X)
    z_lo = model_index // Y
    groups = lax.axis_size("loop")
    splits = lax.axis_size("mp")
    rows, width = img_emb.shape
    half = width // Z_LO
    units = hidden.shape[1]
    share = units // groups

    text_unit, text_inv = normalize(txt_emb)
    text_low = text_unit.astype(bf16)
    two_back = moved(text_low, next_chip(1))
    crossed = moved(text_low, cross(1))
    swapped = moved(two_back, other_core)
    image_unit, image_inv = normalize(img_emb)
    image_low = image_unit.astype(bf16)

    hidden_other = moved(hidden, other_z_lo)
    place = lax.broadcasted_iota(jnp.int32, (units, Z_LO * units), 1)
    block = CORE * X * Z_HI
    at_core = (place // (Z_LO * units // CORE) + core) % CORE
    at_x = (place // (Z_LO * units // (CORE * X)) + x) % X
    at_z = (place // (Z_LO * share) + z_hi) % Z_HI
    unit = ((at_z * X + at_x) * CORE + at_core) * share + place % share
    here = lax.broadcasted_iota(jnp.int32, place.shape, 0) == unit
    which = (place // share) % Z_LO
    hidden_both = jnp.dot(
        hidden, (here & (which == 0)).astype(bf16), preferred_element_type=bf16
    ) + jnp.dot(hidden_other, (here & (which == 1)).astype(bf16), preferred_element_type=bf16)
    hidden_both = hidden_both.reshape(Z_LO, Y, rows, Z_LO * units).transpose(1, 0, 2, 3)
    hidden_both = hidden_both.reshape(Z_LO * Y * rows, Z_LO * units)

    image_total = jnp.zeros(img_emb.shape, jnp.float32)
    text_parts = []
    far = jnp.where(core == 0, 3, 1)
    for text_block, offset in ((text_low, 0), (two_back, 2), (crossed, far), (swapped, 4 - far)):
        owner = (loop_index - offset) % groups
        first_col = (owner * splits + model_index) * rows
        image_part, text_part = pair_terms(image_low, text_block, positives, first_col)
        image_total = image_total + image_part
        text_parts.append(text_part)
    image_grad = backward_norm(image_unit, image_inv, image_total).astype(bf16)

    left, right = image_grad[:, :half], image_grad[:, half:]
    first = z_lo == 0
    mine = jnp.where(first, left, right)
    theirs = moved(jnp.where(first, right, left), other_z_lo)
    both = jnp.where(first, jnp.stack([mine, theirs]), jnp.stack([theirs, mine]))
    gathered = lax.all_gather(
        both.reshape(Z_LO * rows, half),
        "mp",
        axis=0,
        tiled=True,
        axis_index_groups=[list(range(Y)), list(range(Y, Z_LO * Y))],
    )

    back = moved(text_parts[3].astype(bf16), other_core)
    back_two = moved((text_parts[1] + back.astype(jnp.float32)).astype(bf16), next_chip(-1))
    back_cross = moved(text_parts[2].astype(bf16), cross(-1))
    text_total = text_parts[0] + back_two.astype(jnp.float32) + back_cross.astype(jnp.float32)
    text_grad = backward_norm(text_unit, text_inv, text_total).astype(bf16)

    total = lax.dot_general(
        hidden_both, gathered, (((0,), (0,)), ((), ())), preferred_element_type=jnp.float32
    )
    part = total.shape[0] // CORE
    total = total[:part] + moved(total[part:].astype(bf16), other_core).astype(jnp.float32)
    part = part // X
    pieces = [
        moved(
            total[part * k : part * (k + 1)].astype(bf16),
            lambda z_hi, x, core, z_lo, y, k=k: (z_hi, x + k, core, z_lo, y),
        )
        for k in range(1, X)
    ]
    total = total[:part] + sum(piece.astype(jnp.float32) for piece in pieces)
    part = part // Z_HI
    pieces = [
        moved(
            total[part * k : part * (k + 1)].astype(bf16),
            lambda z_hi, x, core, z_lo, y, k=k: (z_hi + k, x, core, z_lo, y),
        )
        for k in range(1, Z_HI)
    ]
    total = total[:part] + sum(piece.astype(jnp.float32) for piece in pieces)
    total = total / math.sqrt(rows * splits * groups)
    own = total[:share]
    rest = moved(total[share:], other_z_lo)
    weight_share = jnp.where(
        first, jnp.concatenate([own, rest], axis=1), jnp.concatenate([rest, own], axis=1)
    )
    return (text_grad, weight_share)


def solution(mesh):
    in_specs = (
        P(("loop", "mp"), None),
        P(("loop", "mp"), None),
        P("loop", "mp"),
        P(("loop", "mp")),
    )
    out_specs = (P(("loop", "mp"), None), P(("mp", "loop"), None))
    return jax.shard_map(local, mesh=mesh, in_specs=in_specs, out_specs=out_specs, check_vma=False)
```

time: 475 us -> 179 us (0.38)
  waiting for transfers between devices: 394 us -> 72.1 us
  starting transfers between devices: 41.2 us -> 67.1 us
    unnamed x3 -> x1, waiting for transfers between devices: 288 us -> 0.02 us
    all_gather x1, waiting for transfers between devices: 76 us -> 2.27 us  [local(): lax.all_gather(both.reshape(Z_LO * rows, half), 'mp', axis=0, tiled=True,...]
    ppermute x6 -> x16, waiting for transfers between devices: 30.1 us -> 69.8 us  [moved(): return lax.ppermute(value, ('loop', 'mp'), pairs)]
    ppermute x6 -> x16, starting transfers between devices: 41.1 us -> 67.1 us  [moved(): return lax.ppermute(value, ('loop', 'mp'), pairs)]
  transfers between devices with their start and end apart: 8 -> 17, of which waited for: 7 -> 8; matrix products, arithmetic and copies ran while one was open for 4% -> 8% of each run, Pallas kernels for 0% -> 0%
where the time goes in v1:
time: 179 us; the launch traced here: 178 us
  waiting for transfers between devices  72.1 us (40%)
  starting transfers between devices  67.1 us (37%)
  between operations  14.8 us (8%)
  matrix products  13.9 us (8%)
  other arithmetic  5.68 us (3%)
  local copies, waits for them, and re-layouts  4.92 us (3%)
    ppermute x16, waiting for transfers between devices, moved(): return lax.ppermute(value, ('loop', 'mp'), pairs)  69.8 us
    ppermute x16, starting transfers between devices, moved(): return lax.ppermute(value, ('loop', 'mp'), pairs)  67.1 us
    dot_general x1, matrix products, local(): lax.dot_general(hidden_both, gathered, (((0,), (0,)), ((), ())), preferre...  5.56 us
    unnamed x2, matrix products  4.34 us
  transfers between devices with their start and end apart: 17, of which 8 were waited for; matrix products, arithmetic and copies ran while one was open for 8% of the time, Pallas kernels for 0%

profile of v1, /device:TPU:1, one launch (start us, length us, event | category | flops | bytes accessed | tf_op | source)
XLA Modules:
  0.0 178.5 jit_solution(16993825713948412352)
XLA Ops:
  9.6 6.0 %collective-permute-start.4 = (bf16[128,1536]{1,0:T(8,128)(2,1)S(1)}, bf16[128,1536]{1,0:T(8,128)(2,1)S(1)}, u32[]{:S(2)}, u32[]{:S(2)}) collective-permute-start(bf16[128,1536]{1,0:T(8,128)(2,1)S(1)} %fusion.44), channel_id=1, source_target_pairs={{0,16},{1,17},{2,18},{3,19},{4,20},{5,21},{6,22},{7,23},{8,24},{9,... | collective-permute-start | bytes 1179656 | tf_op jit(solution)/shard_map/ppermute | solution.py:24
  15.6 2.2 %collective-permute-start = (bf16[128,1536]{1,0:T(8,128)(2,1)S(1)}, bf16[128,1536]{1,0:T(8,128)(2,1)S(1)}, u32[]{:S(2)}, u32[]{:S(2)}) collective-permute-start(bf16[128,1536]{1,0:T(8,128)(2,1)S(1)} %fusion.44), channel_id=1, source_target_pairs={{0,32},{1,33},{2,34},{3,35},{4,36},{5,37},{6,38},{7,39},{8,40},{9,... | collective-permute-start | bytes 1179656 | tf_op jit(solution)/shard_map/ppermute | solution.py:24
  18.8 20.2 %collective-permute-done = bf16[128,1536]{1,0:T(8,128)(2,1)S(1)} collective-permute-done((bf16[128,1536]{1,0:T(8,128)(2,1)S(1)}, bf16[128,1536]{1,0:T(8,128)(2,1)S(1)}, u32[]{:S(2)}, u32[]{:S(2)}) %collective-permute-start) | collective-permute-done | bytes 393248 | tf_op jit(solution)/shard_map/ppermute | solution.py:24
  44.0 13.6 %collective-permute-start.7 = (bf16[128,768]{1,0:T(8,128)(2,1)S(1)}, bf16[128,768]{1,0:T(8,128)(2,1)S(1)}, u32[]{:S(2)}, u32[]{:S(2)}) collective-permute-start(bf16[128,768]{1,0:T(8,128)(2,1)S(1)} %get-tuple-element.10), channel_id=1, source_target_pairs={{0,8},{1,9},{2,10},{3,11},{4,12},{5,13},{6,14},{7,15},{8,0},{9,1},... | collective-permute-start | bytes 589832 | tf_op jit(solution)/shard_map/ppermute | solution.py:24
  57.6 4.9 %collective-permute-done.7 = bf16[128,768]{1,0:T(8,128)(2,1)S(1)} collective-permute-done((bf16[128,768]{1,0:T(8,128)(2,1)S(1)}, bf16[128,768]{1,0:T(8,128)(2,1)S(1)}, u32[]{:S(2)}, u32[]{:S(2)}) %collective-permute-start.7) | collective-permute-done | bytes 196640 | tf_op jit(solution)/shard_map/ppermute | solution.py:24
  63.3 3.0 %collective-permute-start.6 = (bf16[2048,384]{1,0:T(8,128)(2,1)S(1)}, bf16[2048,384]{1,0:T(8,128)(2,1)S(1)}, u32[]{:S(2)}, u32[]{:S(2)}) collective-permute-start(bf16[2048,384]{1,0:T(8,128)(2,1)S(1)} %copy-done.10), channel_id=1, source_target_pairs={{0,8},{1,9},{2,10},{3,11},{4,12},{5,13},{6,14},{7,15},{8,0},{9,1},... | collective-permute-start | bytes 4718600 | tf_op jit(solution)/shard_map/ppermute | solution.py:24
  66.5 2.2 %convolution_convert_fusion.1 = bf16[768,2048]{1,0:T(8,128)(2,1)S(1)} fusion(bf16[2048,384]{1,0:T(8,128)(2,1)S(1)} %copy-done.10, s32[768]{0:T(1024)S(1)} %get-tuple-element.23, s32[768]{0:T(1024)S(1)} %get-tuple-element.30, pred[768]{0:T(1024)(128)(4,1)S(1)} %get-tuple-element.24, s32[768]{0:T(1024)S(1)} %get-tuple-element.28, ...), kind=kOutput, calls=%fused_computation.1 | convolution fusion | flops 1227816960 | bytes 4753164
  68.7 31.6 %collective-permute-done.6 = bf16[2048,384]{1,0:T(8,128)(2,1)S(1)} collective-permute-done((bf16[2048,384]{1,0:T(8,128)(2,1)S(1)}, bf16[2048,384]{1,0:T(8,128)(2,1)S(1)}, u32[]{:S(2)}, u32[]{:S(2)}) %collective-permute-start.6) | collective-permute-done | bytes 1572896 | tf_op jit(solution)/shard_map/ppermute | solution.py:24
  100.3 2.2 %add_bitcast_fusion = bf16[96,8,16,128]{3,1,2,0:T(8,128)(2,1)S(1)} fusion(bf16[768,2048]{1,0:T(8,128)(2,1)S(1)} %convolution_convert_fusion.1, bf16[2048,384]{1,0:T(8,128)(2,1)S(1)} %collective-permute-done.6, s32[768]{0:T(1024)S(1)} %get-tuple-element.23, s32[768]{0:T(1024)S(1)} %get-tuple-element.30, pred[768]{0:T(1024)(128)(4,1)S(1)} %get-tuple-element.24, ...), kind=kOutput, calls=%fused_computation.2 | convolution fusion | flops 1229389824 | bytes 7898892
  103.5 3.5 %copy.6 = bf16[2,8,128,768]{3,2,0,1:T(8,128)(2,1)} copy(bf16[2,8,128,768]{2,1,0,3:T(8,128)(2,1)S(1)} %bitcast.34) | data formatting | bytes 6291456 | tf_op jit(solution)/shard_map/reshape | solution.py:118
  107.0 2.3 %all-gather.2.cloned.1.call-done = bf16[2048,768]{1,0:T(8,128)(2,1)} async-done(((bf16[256,768]{1,0:T(8,128)(2,1)}), bf16[2048,768]{1,0:T(8,128)(2,1)}) %all-gather.2.cloned.1.call-update) | async-done | bytes 3145744 | tf_op jit(solution)/shard_map/all_gather | solution.py:137
  109.3 5.6 %fusion.105 = f32[768,768]{1,0:T(8,128)S(1)} fusion(bf16[2048,768]{1,0:T(8,128)(2,1)} %bitcast.35, bf16[2048,768]{1,0:T(8,128)(2,1)} %all-gather.2.cloned.1.call-done), kind=kOutput, calls=%fused_computation.158 | convolution fusion | flops 2415919104 | bytes 8650752 | tf_op jit(solution)/shard_map/dot_general | solution.py:151
  114.9 3.2 %collective-permute-start.8 = (bf16[384,768]{1,0:T(8,128)(2,1)S(1)}, bf16[384,768]{1,0:T(8,128)(2,1)S(1)}, u32[]{:S(2)}, u32[]{:S(2)}) collective-permute-start(bf16[384,768]{1,0:T(8,128)(2,1)S(1)} %slice.87), channel_id=1, source_target_pairs={{0,16},{1,17},{2,18},{3,19},{4,20},{5,21},{6,22},{7,23},{8,24},{9,... | collective-permute-start | bytes 1769480 | tf_op jit(solution)/shard_map/ppermute | solution.py:24
  118.5 1.9 %collective-permute-start.5 = (bf16[128,1536]{1,0:T(8,128)(2,1)S(1)}, bf16[128,1536]{1,0:T(8,128)(2,1)S(1)}, u32[]{:S(2)}, u32[]{:S(2)}) collective-permute-start(bf16[128,1536]{1,0:T(8,128)(2,1)S(1)} %fusion.2), channel_id=1, source_target_pairs={{0,464},{1,465},{2,466},{3,467},{4,468},{5,469},{6,470},{7,471},{8... | collective-permute-start | bytes 1179656 | tf_op jit(solution)/shard_map/ppermute | solution.py:24
  120.8 9.1 %collective-permute-start.2 = (bf16[128,1536]{1,0:T(8,128)(2,1)S(1)}, bf16[128,1536]{1,0:T(8,128)(2,1)S(1)}, u32[]{:S(2)}, u32[]{:S(2)}) collective-permute-start(bf16[128,1536]{1,0:T(8,128)(2,1)S(1)} %fusion.1), channel_id=1, source_target_pairs={{0,16},{1,17},{2,18},{3,19},{4,20},{5,21},{6,22},{7,23},{8,24},{9,... | collective-permute-start | bytes 1179656 | tf_op jit(solution)/shard_map/ppermute | solution.py:24
  130.1 1.9 %collective-permute-start.11 = (bf16[96,768]{1,0:T(8,128)(2,1)S(1)}, bf16[96,768]{1,0:T(8,128)(2,1)S(1)}, u32[]{:S(2)}, u32[]{:S(2)}) collective-permute-start(bf16[96,768]{1,0:T(8,128)(2,1)S(1)} %get-tuple-element.7), channel_id=1, source_target_pairs={{0,96},{1,97},{2,98},{3,99},{4,100},{5,101},{6,102},{7,103},{8,104... | collective-permute-start | bytes 442376 | tf_op jit(solution)/shard_map/ppermute | solution.py:24
  132.0 4.0 %collective-permute-start.10 = (bf16[96,768]{1,0:T(8,128)(2,1)S(1)}, bf16[96,768]{1,0:T(8,128)(2,1)S(1)}, u32[]{:S(2)}, u32[]{:S(2)}) collective-permute-start(bf16[96,768]{1,0:T(8,128)(2,1)S(1)} %get-tuple-element.8), channel_id=1, source_target_pairs={{0,64},{1,65},{2,66},{3,67},{4,68},{5,69},{6,70},{7,71},{8,72},{9,... | collective-permute-start | bytes 442376 | tf_op jit(solution)/shard_map/ppermute | solution.py:24
  136.0 2.1 %collective-permute-start.9 = (bf16[96,768]{1,0:T(8,128)(2,1)S(1)}, bf16[96,768]{1,0:T(8,128)(2,1)S(1)}, u32[]{:S(2)}, u32[]{:S(2)}) collective-permute-start(bf16[96,768]{1,0:T(8,128)(2,1)S(1)} %get-tuple-element.6), channel_id=1, source_target_pairs={{0,32},{1,33},{2,34},{3,35},{4,36},{5,37},{6,38},{7,39},{8,40},{9,... | collective-permute-start | bytes 442376 | tf_op jit(solution)/shard_map/ppermute | solution.py:24
  138.4 6.0 %collective-permute-start.3 = (bf16[128,1536]{1,0:T(8,128)(2,1)S(1)}, bf16[128,1536]{1,0:T(8,128)(2,1)S(1)}, u32[]{:S(2)}, u32[]{:S(2)}) collective-permute-start(bf16[128,1536]{1,0:T(8,128)(2,1)S(1)} %add_convert_fusion), channel_id=1, source_target_pairs={{0,480},{1,481},{2,482},{3,483},{4,484},{5,485},{6,486},{7,487},{8... | collective-permute-start | bytes 1179656 | tf_op jit(solution)/shard_map/ppermute | solution.py:24
  144.6 3.2 %collective-permute-start.14 = (bf16[24,768]{1,0:T(8,128)(2,1)S(1)}, bf16[24,768]{1,0:T(8,128)(2,1)S(1)}, u32[]{:S(2)}, u32[]{:S(2)}) collective-permute-start(bf16[24,768]{1,0:T(8,128)(2,1)S(1)} %get-tuple-element.12), channel_id=1, source_target_pairs={{0,384},{1,385},{2,386},{3,387},{4,388},{5,389},{6,390},{7,391},{8... | collective-permute-start | bytes 110600 | tf_op jit(solution)/shard_map/ppermute | solution.py:24
  147.8 4.5 %collective-permute-start.13 = (bf16[24,768]{1,0:T(8,128)(2,1)S(1)}, bf16[24,768]{1,0:T(8,128)(2,1)S(1)}, u32[]{:S(2)}, u32[]{:S(2)}) collective-permute-start(bf16[24,768]{1,0:T(8,128)(2,1)S(1)} %get-tuple-element.13), channel_id=1, source_target_pairs={{0,256},{1,257},{2,258},{3,259},{4,260},{5,261},{6,262},{7,263},{8... | collective-permute-start | bytes 110600 | tf_op jit(solution)/shard_map/ppermute | solution.py:24
  152.4 2.4 %collective-permute-start.12 = (bf16[24,768]{1,0:T(8,128)(2,1)S(1)}, bf16[24,768]{1,0:T(8,128)(2,1)S(1)}, u32[]{:S(2)}, u32[]{:S(2)}) collective-permute-start(bf16[24,768]{1,0:T(8,128)(2,1)S(1)} %get-tuple-element.11), channel_id=1, source_target_pairs={{0,128},{1,129},{2,130},{3,131},{4,132},{5,133},{6,134},{7,135},{8... | collective-permute-start | bytes 110600 | tf_op jit(solution)/shard_map/ppermute | solution.py:24
  154.8 8.7 %collective-permute-done.3 = bf16[128,1536]{1,0:T(8,128)(2,1)S(1)} collective-permute-done((bf16[128,1536]{1,0:T(8,128)(2,1)S(1)}, bf16[128,1536]{1,0:T(8,128)(2,1)S(1)}, u32[]{:S(2)}, u32[]{:S(2)}) %collective-permute-start.3) | collective-permute-done | bytes 393248 | tf_op jit(solution)/shard_map/ppermute | solution.py:24
  164.0 2.1 %collective-permute-done.14 = bf16[24,768]{1,0:T(8,128)(2,1)S(1)} collective-permute-done((bf16[24,768]{1,0:T(8,128)(2,1)S(1)}, bf16[24,768]{1,0:T(8,128)(2,1)S(1)}, u32[]{:S(2)}, u32[]{:S(2)}) %collective-permute-start.14) | collective-permute-done | bytes 36896 | tf_op jit(solution)/shard_map/ppermute | solution.py:24
  (81 shorter events, 17.3 us)
Async XLA Ops:
  7.2 10.8 %copy-start = (bf16[128,1536]{1,0:T(8,128)(2,1)S(1)}, bf16[128,1536]{1,0:T(8,128)(2,1)}, u32[]{:S(2)}) copy-start(bf16[128,1536]{1,0:T(8,128)(2,1)} %param.4) | copy-start | bytes 1179652
  7.2 11.0 %copy-start.11 = (s32[128]{0:T(128)S(1)}, s32[128]{0:T(128)}, u32[]{:S(2)}) copy-start(s32[128]{0:T(128)} %param.7) | copy-start | bytes 1540
  7.2 102.1 %all-gather.2.cloned.1.call-start = ((), (), s32[]{:S(2)}) async-start(), calls=%async_computation | async-start | bytes 3538944 | tf_op jit(solution)/shard_map/all_gather | solution.py:137
  9.6 32.0 %collective-permute-start.4 = (bf16[128,1536]{1,0:T(8,128)(2,1)S(1)}, bf16[128,1536]{1,0:T(8,128)(2,1)S(1)}, u32[]{:S(2)}, u32[]{:S(2)}) collective-permute-start(bf16[128,1536]{1,0:T(8,128)(2,1)S(1)} %fusion.44), channel_id=1, source_target_pairs={{0,16},{1,17},{2,18},{3,19},{4,20},{5,21},{6,22},{7,23},{8,24},{9,... | collective-permute-start | bytes 1179656 | tf_op jit(solution)/shard_map/ppermute | solution.py:24
  15.6 23.4 %collective-permute-start = (bf16[128,1536]{1,0:T(8,128)(2,1)S(1)}, bf16[128,1536]{1,0:T(8,128)(2,1)S(1)}, u32[]{:S(2)}, u32[]{:S(2)}) collective-permute-start(bf16[128,1536]{1,0:T(8,128)(2,1)S(1)} %fusion.44), channel_id=1, source_target_pairs={{0,32},{1,33},{2,34},{3,35},{4,36},{5,37},{6,38},{7,39},{8,40},{9,... | collective-permute-start | bytes 1179656 | tf_op jit(solution)/shard_map/ppermute | solution.py:24
  18.5 22.8 %copy-start.2 = (bf16[128,128]{1,0:T(8,128)(2,1)}, bf16[128,128]{1,0:T(8,128)(2,1)S(1)}, u32[]{:S(2)}) copy-start(bf16[128,128]{1,0:T(8,128)(2,1)S(1)} %fusion.38) | copy-start | bytes 98308
  39.1 3.6 %collective-permute-start.1 = (bf16[128,1536]{1,0:T(8,128)(2,1)S(1)}, bf16[128,1536]{1,0:T(8,128)(2,1)S(1)}, u32[]{:S(2)}, u32[]{:S(2)}) collective-permute-start(bf16[128,1536]{1,0:T(8,128)(2,1)S(1)} %collective-permute-done), channel_id=1, source_target_pairs={{0,16},{1,17},{2,18},{3,19},{4,20},{5,21},{6,22},{7,23},{8,24},{9,... | collective-permute-start | bytes 1179656 | tf_op jit(solution)/shard_map/ppermute | solution.py:24
  43.9 19.4 %copy-start.10 = (bf16[2048,384]{1,0:T(8,128)(2,1)S(1)}, bf16[2048,384]{1,0:T(8,128)(2,1)}, u32[]{:S(2)}) copy-start(bf16[2048,384]{1,0:T(8,128)(2,1)} %param.6) | copy-start | bytes 4718596
  44.0 18.5 %collective-permute-start.7 = (bf16[128,768]{1,0:T(8,128)(2,1)S(1)}, bf16[128,768]{1,0:T(8,128)(2,1)S(1)}, u32[]{:S(2)}, u32[]{:S(2)}) collective-permute-start(bf16[128,768]{1,0:T(8,128)(2,1)S(1)} %get-tuple-element.10), channel_id=1, source_target_pairs={{0,8},{1,9},{2,10},{3,11},{4,12},{5,13},{6,14},{7,15},{8,0},{9,1},... | collective-permute-start | bytes 589832 | tf_op jit(solution)/shard_map/ppermute | solution.py:24
  63.3 36.9 %collective-permute-start.6 = (bf16[2048,384]{1,0:T(8,128)(2,1)S(1)}, bf16[2048,384]{1,0:T(8,128)(2,1)S(1)}, u32[]{:S(2)}, u32[]{:S(2)}) collective-permute-start(bf16[2048,384]{1,0:T(8,128)(2,1)S(1)} %copy-done.10), channel_id=1, source_target_pairs={{0,8},{1,9},{2,10},{3,11},{4,12},{5,13},{6,14},{7,15},{8,0},{9,1},... | collective-permute-start | bytes 4718600 | tf_op jit(solution)/shard_map/ppermute | solution.py:24
  114.9 14.9 %collective-permute-start.8 = (bf16[384,768]{1,0:T(8,128)(2,1)S(1)}, bf16[384,768]{1,0:T(8,128)(2,1)S(1)}, u32[]{:S(2)}, u32[]{:S(2)}) collective-permute-start(bf16[384,768]{1,0:T(8,128)(2,1)S(1)} %slice.87), channel_id=1, source_target_pairs={{0,16},{1,17},{2,18},{3,19},{4,20},{5,21},{6,22},{7,23},{8,24},{9,... | collective-permute-start | bytes 1769480 | tf_op jit(solution)/shard_map/ppermute | solution.py:24
  118.5 36.3 %collective-permute-start.5 = (bf16[128,1536]{1,0:T(8,128)(2,1)S(1)}, bf16[128,1536]{1,0:T(8,128)(2,1)S(1)}, u32[]{:S(2)}, u32[]{:S(2)}) collective-permute-start(bf16[128,1536]{1,0:T(8,128)(2,1)S(1)} %fusion.2), channel_id=1, source_target_pairs={{0,464},{1,465},{2,466},{3,467},{4,468},{5,469},{6,470},{7,471},{8... | collective-permute-start | bytes 1179656 | tf_op jit(solution)/shard_map/ppermute | solution.py:24
  120.8 17.3 %copy-start.5 = (bf16[128,128]{1,0:T(8,128)(2,1)S(1)}, bf16[128,128]{1,0:T(8,128)(2,1)}, u32[]{:S(2)}) copy-start(bf16[128,128]{1,0:T(8,128)(2,1)} %copy-done.4) | copy-start | bytes 98308
  120.8 17.3 %collective-permute-start.2 = (bf16[128,1536]{1,0:T(8,128)(2,1)S(1)}, bf16[128,1536]{1,0:T(8,128)(2,1)S(1)}, u32[]{:S(2)}, u32[]{:S(2)}) collective-permute-start(bf16[128,1536]{1,0:T(8,128)(2,1)S(1)} %fusion.1), channel_id=1, source_target_pairs={{0,16},{1,17},{2,18},{3,19},{4,20},{5,21},{6,22},{7,23},{8,24},{9,... | collective-permute-start | bytes 1179656 | tf_op jit(solution)/shard_map/ppermute | solution.py:24
  130.1 14.4 %collective-permute-start.11 = (bf16[96,768]{1,0:T(8,128)(2,1)S(1)}, bf16[96,768]{1,0:T(8,128)(2,1)S(1)}, u32[]{:S(2)}, u32[]{:S(2)}) collective-permute-start(bf16[96,768]{1,0:T(8,128)(2,1)S(1)} %get-tuple-element.7), channel_id=1, source_target_pairs={{0,96},{1,97},{2,98},{3,99},{4,100},{5,101},{6,102},{7,103},{8,104... | collective-permute-start | bytes 442376 | tf_op jit(solution)/shard_map/ppermute | solution.py:24
  132.0 12.5 %collective-permute-start.10 = (bf16[96,768]{1,0:T(8,128)(2,1)S(1)}, bf16[96,768]{1,0:T(8,128)(2,1)S(1)}, u32[]{:S(2)}, u32[]{:S(2)}) collective-permute-start(bf16[96,768]{1,0:T(8,128)(2,1)S(1)} %get-tuple-element.8), channel_id=1, source_target_pairs={{0,64},{1,65},{2,66},{3,67},{4,68},{5,69},{6,70},{7,71},{8,72},{9,... | collective-permute-start | bytes 442376 | tf_op jit(solution)/shard_map/ppermute | solution.py:24
  136.0 27.5 %copy-start.1 = (bf16[128,1536]{1,0:T(8,128)(2,1)S(1)}, bf16[128,1536]{1,0:T(8,128)(2,1)}, u32[]{:S(2)}) copy-start(bf16[128,1536]{1,0:T(8,128)(2,1)} %param.5) | copy-start | bytes 1179652
  136.0 27.5 %copy-start.3 = (bf16[128,128]{1,0:T(8,128)(2,1)S(1)}, bf16[128,128]{1,0:T(8,128)(2,1)}, u32[]{:S(2)}) copy-start(bf16[128,128]{1,0:T(8,128)(2,1)} %copy-done.2) | copy-start | bytes 98308
  136.0 8.5 %collective-permute-start.9 = (bf16[96,768]{1,0:T(8,128)(2,1)S(1)}, bf16[96,768]{1,0:T(8,128)(2,1)S(1)}, u32[]{:S(2)}, u32[]{:S(2)}) collective-permute-start(bf16[96,768]{1,0:T(8,128)(2,1)S(1)} %get-tuple-element.6), channel_id=1, source_target_pairs={{0,32},{1,33},{2,34},{3,35},{4,36},{5,37},{6,38},{7,39},{8,40},{9,... | collective-permute-start | bytes 442376 | tf_op jit(solution)/shard_map/ppermute | solution.py:24
  138.4 25.0 %collective-permute-start.3 = (bf16[128,1536]{1,0:T(8,128)(2,1)S(1)}, bf16[128,1536]{1,0:T(8,128)(2,1)S(1)}, u32[]{:S(2)}, u32[]{:S(2)}) collective-permute-start(bf16[128,1536]{1,0:T(8,128)(2,1)S(1)} %add_convert_fusion), channel_id=1, source_target_pairs={{0,480},{1,481},{2,482},{3,483},{4,484},{5,485},{6,486},{7,487},{8... | collective-permute-start | bytes 1179656 | tf_op jit(solution)/shard_map/ppermute | solution.py:24
  144.6 21.5 %collective-permute-start.14 = (bf16[24,768]{1,0:T(8,128)(2,1)S(1)}, bf16[24,768]{1,0:T(8,128)(2,1)S(1)}, u32[]{:S(2)}, u32[]{:S(2)}) collective-permute-start(bf16[24,768]{1,0:T(8,128)(2,1)S(1)} %get-tuple-element.12), channel_id=1, source_target_pairs={{0,384},{1,385},{2,386},{3,387},{4,388},{5,389},{6,390},{7,391},{8... | collective-permute-start | bytes 110600 | tf_op jit(solution)/shard_map/ppermute | solution.py:24
  147.8 18.3 %collective-permute-start.13 = (bf16[24,768]{1,0:T(8,128)(2,1)S(1)}, bf16[24,768]{1,0:T(8,128)(2,1)S(1)}, u32[]{:S(2)}, u32[]{:S(2)}) collective-permute-start(bf16[24,768]{1,0:T(8,128)(2,1)S(1)} %get-tuple-element.13), channel_id=1, source_target_pairs={{0,256},{1,257},{2,258},{3,259},{4,260},{5,261},{6,262},{7,263},{8... | collective-permute-start | bytes 110600 | tf_op jit(solution)/shard_map/ppermute | solution.py:24
  152.4 13.7 %collective-permute-start.12 = (bf16[24,768]{1,0:T(8,128)(2,1)S(1)}, bf16[24,768]{1,0:T(8,128)(2,1)S(1)}, u32[]{:S(2)}, u32[]{:S(2)}) collective-permute-start(bf16[24,768]{1,0:T(8,128)(2,1)S(1)} %get-tuple-element.11), channel_id=1, source_target_pairs={{0,128},{1,129},{2,130},{3,131},{4,132},{5,133},{6,134},{7,135},{8... | collective-permute-start | bytes 110600 | tf_op jit(solution)/shard_map/ppermute | solution.py:24
  166.1 4.8 %collective-permute-start.15 = (f32[12,768]{1,0:T(8,128)S(1)}, f32[12,768]{1,0:T(8,128)S(1)}, u32[]{:S(2)}, u32[]{:S(2)}) collective-permute-start(f32[12,768]{1,0:T(8,128)S(1)} %get-tuple-element.15), channel_id=1, source_target_pairs={{0,8},{1,9},{2,10},{3,11},{4,12},{5,13},{6,14},{7,15},{8,0},{9,1},... | collective-permute-start | bytes 110600 | tf_op jit(solution)/shard_map/ppermute | solution.py:24
  (5 other events, 10.8 us)
Sparse Core Ops, SparseCore 0:
  63.5 45.7 all-gather.1

commit v2 on v1

--- a/solution.py
+++ b/solution.py
@@ -19,7 +19,10 @@
         rest, z_lo = divmod(rest, Z_LO)
         rest, core = divmod(rest, CORE)
         z_hi, x = divmod(rest, X)
-        a, b, c, d, e = where(z_hi, x, core, z_lo, y)
+        target = where(z_hi, x, core, z_lo, y)
+        if target is None:
+            continue
+        a, b, c, d, e = target
         pairs.append((source, ((((a % Z_HI) * X + b % X) * CORE + c % CORE) * Z_LO + d % Z_LO) * Y + e % Y))
     return lax.ppermute(value, ("loop", "mp"), pairs)
 
@@ -35,6 +38,8 @@
 def cross(sign):
     def where(z_hi, x, core, z_lo, y):
         chip = z_hi * X + x
+        if sign > 0 and core == 1 and x == X - 1:
+            return None
         if sign > 0:
             chip += 2 * core
         else:
@@ -44,6 +49,14 @@
     return where
 
 
+def third_hop(z_hi, x, core, z_lo, y):
+    return (z_hi, 1, 0, z_lo, y) if x == 0 and core == 1 else None
+
+
+def zero_of(*values):
+    return sum(jnp.minimum(jnp.abs(v[(0,) * v.ndim].astype(jnp.float32)), 0.0) for v in values)
+
+
 def other_core(z_hi, x, core, z_lo, y):
     return z_hi, x, 1 - core, z_lo, y
 
@@ -74,10 +87,13 @@
     target = (positives[:, None] == columns).astype(jnp.float32)
     coefficient = (jax.nn.sigmoid(scores) - target).astype(jnp.bfloat16)
     image_part = SCALE_T * jnp.dot(coefficient, text_low, preferred_element_type=jnp.float32)
-    text_part = SCALE_T * lax.dot_general(
+    return (image_part, coefficient)
+
+
+def text_terms(image_low, coefficient, scale):
+    return scale * lax.dot_general(
         coefficient, image_low, (((0,), (0,)), ((), ())), preferred_element_type=jnp.float32
     )
-    return (image_part, text_part)
 
 
 def local(img_emb, txt_emb, hidden, positives):
@@ -100,10 +116,10 @@
     two_back = moved(text_low, next_chip(1))
     crossed = moved(text_low, cross(1))
     swapped = moved(two_back, other_core)
+    crossed = jnp.where((x == 1) & (core == 0), moved(two_back, third_hop), crossed)
     image_unit, image_inv = normalize(img_emb)
     image_low = image_unit.astype(bf16)
 
-    hidden_other = moved(hidden, other_z_lo)
     place = lax.broadcasted_iota(jnp.int32, (units, Z_LO * units), 1)
     block = CORE * X * Z_HI
     at_core = (place // (Z_LO * units // CORE) + core) % CORE
@@ -112,22 +128,29 @@
     unit = ((at_z * X + at_x) * CORE + at_core) * share + place % share
     here = lax.broadcasted_iota(jnp.int32, place.shape, 0) == unit
     which = (place // share) % Z_LO
-    hidden_both = jnp.dot(
-        hidden, (here & (which == 0)).astype(bf16), preferred_element_type=bf16
-    ) + jnp.dot(hidden_other, (here & (which == 1)).astype(bf16), preferred_element_type=bf16)
-    hidden_both = hidden_both.reshape(Z_LO, Y, rows, Z_LO * units).transpose(1, 0, 2, 3)
-    hidden_both = hidden_both.reshape(Z_LO * Y * rows, Z_LO * units)
+    pick = (here & (which == 0)).astype(bf16), (here & (which == 1)).astype(bf16)
+
+    def both_units(own):
+        other = moved(own, other_z_lo)
+        mixed = jnp.dot(own, pick[0], preferred_element_type=bf16) + jnp.dot(
+            other, pick[1], preferred_element_type=bf16
+        )
+        return other, mixed.reshape(Y, rows, Z_LO * units)
+
+    early, low = both_units(hidden[: Y * rows])
+    _, high = both_units(hidden[Y * rows :])
+    hidden_both = jnp.stack([low, high], axis=1).reshape(Z_LO * Y * rows, Z_LO * units)
 
     image_total = jnp.zeros(img_emb.shape, jnp.float32)
-    text_parts = []
+    coefficients = []
     far = jnp.where(core == 0, 3, 1)
     for text_block, offset in ((text_low, 0), (two_back, 2), (crossed, far), (swapped, 4 - far)):
         owner = (loop_index - offset) % groups
         first_col = (owner * splits + model_index) * rows
-        image_part, text_part = pair_terms(image_low, text_block, positives, first_col)
+        image_part, coefficient = pair_terms(image_low, text_block, positives, first_col)
         image_total = image_total + image_part
-        text_parts.append(text_part)
-    image_grad = backward_norm(image_unit, image_inv, image_total).astype(bf16)
+        coefficients.append(coefficient)
+    image_grad = backward_norm(image_unit, image_inv + zero_of(early), image_total).astype(bf16)
 
     left, right = image_grad[:, :half], image_grad[:, half:]
     first = z_lo == 0
@@ -142,6 +165,8 @@
         axis_index_groups=[list(range(Y)), list(range(Y, Z_LO * Y))],
     )
 
+    scale = SCALE_T + zero_of(theirs)
+    text_parts = [text_terms(image_low, coefficient, scale) for coefficient in coefficients]
     back = moved(text_parts[3].astype(bf16), other_core)
     back_two = moved((text_parts[1] + back.astype(jnp.float32)).astype(bf16), next_chip(-1))
     back_cross = moved(text_parts[2].astype(bf16), cross(-1))
@@ -151,6 +176,7 @@
     total = lax.dot_general(
         hidden_both, gathered, (((0,), (0,)), ((), ())), preferred_element_type=jnp.float32
     )
+    total = total * (1.0 + zero_of(back_two, back_cross))
     part = total.shape[0] // CORE
     total = total[:part] + moved(total[part:].astype(bf16), other_core).astype(jnp.float32)
     part = part // X

time: 179 us -> 179 us (level); the launches traced: 178 us -> 177 us
  starting transfers between devices: 67.1 us -> 59.5 us
  waiting for transfers between devices: 72.1 us -> 65.6 us
  matrix products: 13.9 us -> 20.3 us
  local copies, waits for them, and re-layouts: 4.92 us -> 8.2 us
  between operations: 14.8 us -> 17.4 us
    ppermute x16 -> x18, starting transfers between devices: 67.1 us -> 59.4 us  [moved(): return lax.ppermute(value, ('loop', 'mp'), pairs)]
    slice x0 -> x5, local copies, waits for them, and re-layouts: none -> 5.63 us  [the longest x4 4.05 us: zero_of(): v[(0,) * v.ndim].astype(jnp.float32)]
    ppermute x16 -> x18, waiting for transfers between devices: 69.8 us -> 65.5 us  [moved(): return lax.ppermute(value, ('loop', 'mp'), pairs)]
    unnamed x2 -> x4, matrix products: 4.34 us -> 7.98 us
    reshape x1 -> x0, local copies, waits for them, and re-layouts: 3.54 us -> none  [local(): hidden_both.reshape(Z_LO, Y, rows, Z_LO * units).transpose(1, 0, 2, 3)]
    dot_general x4, matrix products: 1.53 us -> 4.19 us  [text_terms(): lax.dot_general(coefficient, image_low, (((0,), (0,)), ((), ())), preferr...]
    another operation x0 -> x2, local copies, waits for them, and re-layouts: none -> 2.42 us  [local(): jnp.stack([low, high], axis=1).reshape(Z_LO * Y * rows, Z_LO * units)]
    all_gather x1, waiting for transfers between devices: 2.27 us -> 0.02 us  [local(): lax.all_gather(both.reshape(Z_LO * rows, half), 'mp', axis=0, tiled=True,...]
  transfers between devices with their start and end apart: 17 -> 19, of which waited for: 8 -> 8; matrix products, arithmetic and copies ran while one was open for 8% -> 14% of each run, Pallas kernels for 0% -> 0%
where the time goes in v2:
time: 179 us; the launch traced here: 177 us
  waiting for transfers between devices  65.6 us (37%)
  starting transfers between devices  59.5 us (33%)
  matrix products  20.3 us (11%)
  between operations  17.4 us (10%)
  local copies, waits for them, and re-layouts  8.2 us (5%)
  other arithmetic  5.72 us (3%)
    ppermute x18, waiting for transfers between devices, moved(): return lax.ppermute(value, ('loop', 'mp'), pairs)  65.5 us
    ppermute x18, starting transfers between devices, moved(): return lax.ppermute(value, ('loop', 'mp'), pairs)  59.4 us
    unnamed x4, matrix products  7.98 us
    dot_general x1, matrix products, local(): lax.dot_general(hidden_both, gathered, (((0,), (0,)), ((), ())), preferre...  5.57 us
    dot_general x4, matrix products, text_terms(): lax.dot_general(coefficient, image_low, (((0,), (0,)), ((), ())), preferr...  4.19 us
    slice x4, local copies, waits for them, and re-layouts, zero_of(): v[(0,) * v.ndim].astype(jnp.float32)  4.05 us
  transfers between devices with their start and end apart: 19, of which 8 were waited for; matrix products, arithmetic and copies ran while one was open for 14% of the time, Pallas kernels for 0%

profile of v2, /device:TPU:1, one launch (start us, length us, event | category | flops | bytes accessed | tf_op | source)
XLA Modules:
  0.0 176.6 jit_solution(11715824426572369692)
XLA Ops:
  8.8 5.0 %collective-permute-start.4 = (bf16[1024,384]{1,0:T(8,128)(2,1)S(1)}, bf16[1024,384]{1,0:T(8,128)(2,1)}, u32[]{:S(2)}, u32[]{:S(2)}) collective-permute-start(bf16[1024,384]{1,0:T(8,128)(2,1)S(1)} %get-tuple-element.7), channel_id=1, source_target_pairs={{0,8},{1,9},{2,10},{3,11},{4,12},{5,13},{6,14},{7,15},{8,0},{9,1},... | collective-permute-start | bytes 2359304 | tf_op jit(solution)/shard_map/ppermute | solution.py:27
  14.1 3.1 %collective-permute-start = (bf16[128,1536]{1,0:T(8,128)(2,1)S(1)}, bf16[128,1536]{1,0:T(8,128)(2,1)S(1)}, u32[]{:S(2)}, u32[]{:S(2)}) collective-permute-start(bf16[128,1536]{1,0:T(8,128)(2,1)S(1)} %fusion.45), channel_id=1, source_target_pairs={{0,32},{1,33},{2,34},{3,35},{4,36},{5,37},{6,38},{7,39},{8,40},{9,... | collective-permute-start | bytes 1179656 | tf_op jit(solution)/shard_map/ppermute | solution.py:27
  17.2 5.5 %collective-permute-start.2 = (bf16[128,1536]{1,0:T(8,128)(2,1)S(1)}, bf16[128,1536]{1,0:T(8,128)(2,1)S(1)}, u32[]{:S(2)}, u32[]{:S(2)}) collective-permute-start(bf16[128,1536]{1,0:T(8,128)(2,1)S(1)} %fusion.45), channel_id=1, source_target_pairs={{0,16},{1,17},{2,18},{3,19},{4,20},{5,21},{6,22},{7,23},{8,24},{9,... | collective-permute-start | bytes 1179656 | tf_op jit(solution)/shard_map/ppermute | solution.py:27
  23.1 34.7 %collective-permute-done = bf16[128,1536]{1,0:T(8,128)(2,1)S(1)} collective-permute-done((bf16[128,1536]{1,0:T(8,128)(2,1)S(1)}, bf16[128,1536]{1,0:T(8,128)(2,1)S(1)}, u32[]{:S(2)}, u32[]{:S(2)}) %collective-permute-start) | collective-permute-done | bytes 393248 | tf_op jit(solution)/shard_map/ppermute | solution.py:27
  59.1 2.9 %collective-permute-start.3 = (bf16[128,1536]{1,0:T(8,128)(2,1)S(1)}, bf16[128,1536]{1,0:T(8,128)(2,1)S(1)}, u32[]{:S(2)}, u32[]{:S(2)}) collective-permute-start(bf16[128,1536]{1,0:T(8,128)(2,1)S(1)} %collective-permute-done), channel_id=1, source_target_pairs={{0,16},{1,17},{2,18},{3,19},{4,20},{5,21},{6,22},{7,23},{8,24},{9,... | collective-permute-start | bytes 1179656 | tf_op jit(solution)/shard_map/ppermute | solution.py:27
  67.0 2.1 %collective-permute-start.5 = (bf16[128,768]{1,0:T(8,128)(2,1)S(1)}, bf16[128,768]{1,0:T(8,128)(2,1)S(1)}, u32[]{:S(2)}, u32[]{:S(2)}) collective-permute-start(bf16[128,768]{1,0:T(8,128)(2,1)S(1)} %get-tuple-element.12), channel_id=1, source_target_pairs={{0,8},{1,9},{2,10},{3,11},{4,12},{5,13},{6,14},{7,15},{8,0},{9,1},... | collective-permute-start | bytes 589832 | tf_op jit(solution)/shard_map/ppermute | solution.py:27
  69.0 6.5 %collective-permute-done.5 = bf16[128,768]{1,0:T(8,128)(2,1)S(1)} collective-permute-done((bf16[128,768]{1,0:T(8,128)(2,1)S(1)}, bf16[128,768]{1,0:T(8,128)(2,1)S(1)}, u32[]{:S(2)}, u32[]{:S(2)}) %collective-permute-start.5) | collective-permute-done | bytes 196640 | tf_op jit(solution)/shard_map/ppermute | solution.py:27
  76.4 2.1 %collective-permute-start.9 = (bf16[1024,384]{1,0:T(8,128)(2,1)S(1)}, bf16[1024,384]{1,0:T(8,128)(2,1)}, u32[]{:S(2)}, u32[]{:S(2)}) collective-permute-start(bf16[1024,384]{1,0:T(8,128)(2,1)S(1)} %get-tuple-element.6), channel_id=1, source_target_pairs={{0,8},{1,9},{2,10},{3,11},{4,12},{5,13},{6,14},{7,15},{8,0},{9,1},... | collective-permute-start | bytes 2359304 | tf_op jit(solution)/shard_map/ppermute | solution.py:27
  82.3 2.8 %collective-permute-start.6 = (bf16[128,1536]{1,0:T(8,128)(2,1)S(1)}, bf16[128,1536]{1,0:T(8,128)(2,1)S(1)}, u32[]{:S(2)}, u32[]{:S(2)}) collective-permute-start(bf16[128,1536]{1,0:T(8,128)(2,1)S(1)} %fusion.2), channel_id=1, source_target_pairs={{0,16},{1,17},{2,18},{3,19},{4,20},{5,21},{6,22},{7,23},{8,24},{9,... | collective-permute-start | bytes 1179656 | tf_op jit(solution)/shard_map/ppermute | solution.py:27
  85.1 3.4 %add_bitcast_fusion.1 = bf16[1024,768]{0,1:T(8,128)(2,1)} fusion(bf16[768,1024]{1,0:T(8,128)(2,1)S(1)} %convolution_convert_fusion.3, bf16[1024,384]{1,0:T(8,128)(2,1)} %collective-permute-done.4, s32[768]{0:T(1024)S(1)} %get-tuple-element.27, s32[768]{0:T(1024)S(1)} %get-tuple-element.34, pred[768]{0:T(1024)(128)(4,1)S(1)} %get-tuple-element.28, ...), kind=kOutput, calls=%fused_computation.31 | convolution fusion | flops 623837184 | bytes 3966732
  94.5 14.8 %collective-permute-done.9 = bf16[1024,384]{1,0:T(8,128)(2,1)} collective-permute-done((bf16[1024,384]{1,0:T(8,128)(2,1)S(1)}, bf16[1024,384]{1,0:T(8,128)(2,1)}, u32[]{:S(2)}, u32[]{:S(2)}) %collective-permute-start.9) | collective-permute-done | bytes 786464 | tf_op jit(solution)/shard_map/ppermute | solution.py:27
  109.3 2.5 %add_bitcast_fusion = bf16[1024,768]{0,1:T(8,128)(2,1)S(1)} fusion(bf16[768,1024]{1,0:T(8,128)(2,1)S(1)} %convolution_convert_fusion.1, bf16[1024,384]{1,0:T(8,128)(2,1)} %collective-permute-done.9, s32[768]{0:T(1024)S(1)} %get-tuple-element.27, s32[768]{0:T(1024)S(1)} %get-tuple-element.34, pred[768]{0:T(1024)(128)(4,1)S(1)} %get-tuple-element.28, ...), kind=kOutput, calls=%fused_computation.30 | convolution fusion | flops 623837184 | bytes 3966732
  114.2 2.0 %pad_maximum_fusion = bf16[8,2,128,768]{3,2,1,0:T(8,128)(2,1)} fusion(bf16[8,1,128,768]{3,2,1,0:T(8,128)(2,1)S(1)} %bitcast.32, bf16[8,1,128,768]{3,2,1,0:T(8,128)(2,1)S(1)} %bitcast.33), kind=kLoop, calls=%fused_computation | loop fusion | flops 1572864 | bytes 6291456 | tf_op jit(solution)/shard_map/stack | solution.py:142
  119.9 5.6 %convolution_multiply_fusion.4 = f32[768,768]{1,0:T(8,128)S(1)} fusion(bf16[2048,768]{1,0:T(8,128)(2,1)} %bitcast.34, bf16[2048,768]{1,0:T(8,128)(2,1)} %all-gather.2.cloned.1.call-done, f32[]{:T(128)} %bitcast.10), kind=kOutput, calls=%fused_computation.25 | convolution fusion | flops 2416508928 | bytes 8650756 | tf_op jit(solution)/shard_map/dot_general | solution.py:176
  125.6 4.8 %collective-permute-start.10 = (bf16[384,768]{1,0:T(8,128)(2,1)S(1)}, bf16[384,768]{1,0:T(8,128)(2,1)S(1)}, u32[]{:S(2)}, u32[]{:S(2)}) collective-permute-start(bf16[384,768]{1,0:T(8,128)(2,1)S(1)} %slice.119), channel_id=1, source_target_pairs={{0,16},{1,17},{2,18},{3,19},{4,20},{5,21},{6,22},{7,23},{8,24},{9,... | collective-permute-start | bytes 1769480 | tf_op jit(solution)/shard_map/ppermute | solution.py:27
  132.3 2.1 %collective-permute-start.13 = (bf16[96,768]{1,0:T(8,128)(2,1)S(1)}, bf16[96,768]{1,0:T(8,128)(2,1)S(1)}, u32[]{:S(2)}, u32[]{:S(2)}) collective-permute-start(bf16[96,768]{1,0:T(8,128)(2,1)S(1)} %get-tuple-element.9), channel_id=1, source_target_pairs={{0,96},{1,97},{2,98},{3,99},{4,100},{5,101},{6,102},{7,103},{8,104... | collective-permute-start | bytes 442376 | tf_op jit(solution)/shard_map/ppermute | solution.py:27
  134.3 1.9 %collective-permute-start.12 = (bf16[96,768]{1,0:T(8,128)(2,1)S(1)}, bf16[96,768]{1,0:T(8,128)(2,1)S(1)}, u32[]{:S(2)}, u32[]{:S(2)}) collective-permute-start(bf16[96,768]{1,0:T(8,128)(2,1)S(1)} %get-tuple-element.10), channel_id=1, source_target_pairs={{0,64},{1,65},{2,66},{3,67},{4,68},{5,69},{6,70},{7,71},{8,72},{9,... | collective-permute-start | bytes 442376 | tf_op jit(solution)/shard_map/ppermute | solution.py:27
  136.3 3.4 %collective-permute-start.11 = (bf16[96,768]{1,0:T(8,128)(2,1)S(1)}, bf16[96,768]{1,0:T(8,128)(2,1)S(1)}, u32[]{:S(2)}, u32[]{:S(2)}) collective-permute-start(bf16[96,768]{1,0:T(8,128)(2,1)S(1)} %get-tuple-element.8), channel_id=1, source_target_pairs={{0,32},{1,33},{2,34},{3,35},{4,36},{5,37},{6,38},{7,39},{8,40},{9,... | collective-permute-start | bytes 442376 | tf_op jit(solution)/shard_map/ppermute | solution.py:27
  139.6 3.2 %collective-permute-done.12 = bf16[96,768]{1,0:T(8,128)(2,1)S(1)} collective-permute-done((bf16[96,768]{1,0:T(8,128)(2,1)S(1)}, bf16[96,768]{1,0:T(8,128)(2,1)S(1)}, u32[]{:S(2)}, u32[]{:S(2)}) %collective-permute-start.12) | collective-permute-done | bytes 147488 | tf_op jit(solution)/shard_map/ppermute | solution.py:27
  142.8 3.2 %collective-permute-done.11 = bf16[96,768]{1,0:T(8,128)(2,1)S(1)} collective-permute-done((bf16[96,768]{1,0:T(8,128)(2,1)S(1)}, bf16[96,768]{1,0:T(8,128)(2,1)S(1)}, u32[]{:S(2)}, u32[]{:S(2)}) %collective-permute-start.11) | collective-permute-done | bytes 147488 | tf_op jit(solution)/shard_map/ppermute | solution.py:27
  146.1 4.4 %collective-permute-start.16 = (bf16[24,768]{1,0:T(8,128)(2,1)S(1)}, bf16[24,768]{1,0:T(8,128)(2,1)S(1)}, u32[]{:S(2)}, u32[]{:S(2)}) collective-permute-start(bf16[24,768]{1,0:T(8,128)(2,1)S(1)} %get-tuple-element.14), channel_id=1, source_target_pairs={{0,384},{1,385},{2,386},{3,387},{4,388},{5,389},{6,390},{7,391},{8... | collective-permute-start | bytes 110600 | tf_op jit(solution)/shard_map/ppermute | solution.py:27
  150.5 3.4 %collective-permute-start.15 = (bf16[24,768]{1,0:T(8,128)(2,1)S(1)}, bf16[24,768]{1,0:T(8,128)(2,1)S(1)}, u32[]{:S(2)}, u32[]{:S(2)}) collective-permute-start(bf16[24,768]{1,0:T(8,128)(2,1)S(1)} %get-tuple-element.15), channel_id=1, source_target_pairs={{0,256},{1,257},{2,258},{3,259},{4,260},{5,261},{6,262},{7,263},{8... | collective-permute-start | bytes 110600 | tf_op jit(solution)/shard_map/ppermute | solution.py:27
  153.8 4.3 %collective-permute-start.14 = (bf16[24,768]{1,0:T(8,128)(2,1)S(1)}, bf16[24,768]{1,0:T(8,128)(2,1)S(1)}, u32[]{:S(2)}, u32[]{:S(2)}) collective-permute-start(bf16[24,768]{1,0:T(8,128)(2,1)S(1)} %get-tuple-element.13), channel_id=1, source_target_pairs={{0,128},{1,129},{2,130},{3,131},{4,132},{5,133},{6,134},{7,135},{8... | collective-permute-start | bytes 110600 | tf_op jit(solution)/shard_map/ppermute | solution.py:27
  161.0 6.6 %collective-permute-start.17 = (f32[12,768]{1,0:T(8,128)S(1)}, f32[12,768]{1,0:T(8,128)S(1)}, u32[]{:S(2)}, u32[]{:S(2)}) collective-permute-start(f32[12,768]{1,0:T(8,128)S(1)} %get-tuple-element.17), channel_id=1, source_target_pairs={{0,8},{1,9},{2,10},{3,11},{4,12},{5,13},{6,14},{7,15},{8,0},{9,1},... | collective-permute-start | bytes 110600 | tf_op jit(solution)/shard_map/ppermute | solution.py:27
  (83 shorter events, 29.2 us)
Async XLA Ops:
  7.2 112.7 %all-gather.2.cloned.1.call-start = ((), (), s32[]{:S(2)}) async-start(), calls=%async_computation | async-start | bytes 3538944 | tf_op jit(solution)/shard_map/all_gather | solution.py:160
  8.8 14.1 %copy-start = (bf16[128,1536]{1,0:T(8,128)(2,1)S(1)}, bf16[128,1536]{1,0:T(8,128)(2,1)}, u32[]{:S(2)}) copy-start(bf16[128,1536]{1,0:T(8,128)(2,1)} %param.4) | copy-start | bytes 1179652
  8.8 55.1 %copy-start.6 = (s32[128]{0:T(128)S(1)}, s32[128]{0:T(128)}, u32[]{:S(2)}) copy-start(s32[128]{0:T(128)} %param.7) | copy-start | bytes 1540
  8.8 53.2 %collective-permute-start.4 = (bf16[1024,384]{1,0:T(8,128)(2,1)S(1)}, bf16[1024,384]{1,0:T(8,128)(2,1)}, u32[]{:S(2)}, u32[]{:S(2)}) collective-permute-start(bf16[1024,384]{1,0:T(8,128)(2,1)S(1)} %get-tuple-element.7), channel_id=1, source_target_pairs={{0,8},{1,9},{2,10},{3,11},{4,12},{5,13},{6,14},{7,15},{8,0},{9,1},... | collective-permute-start | bytes 2359304 | tf_op jit(solution)/shard_map/ppermute | solution.py:27
  14.1 43.6 %collective-permute-start = (bf16[128,1536]{1,0:T(8,128)(2,1)S(1)}, bf16[128,1536]{1,0:T(8,128)(2,1)S(1)}, u32[]{:S(2)}, u32[]{:S(2)}) collective-permute-start(bf16[128,1536]{1,0:T(8,128)(2,1)S(1)} %fusion.45), channel_id=1, source_target_pairs={{0,32},{1,33},{2,34},{3,35},{4,36},{5,37},{6,38},{7,39},{8,40},{9,... | collective-permute-start | bytes 1179656 | tf_op jit(solution)/shard_map/ppermute | solution.py:27
  17.2 48.5 %collective-permute-start.2 = (bf16[128,1536]{1,0:T(8,128)(2,1)S(1)}, bf16[128,1536]{1,0:T(8,128)(2,1)S(1)}, u32[]{:S(2)}, u32[]{:S(2)}) collective-permute-start(bf16[128,1536]{1,0:T(8,128)(2,1)S(1)} %fusion.45), channel_id=1, source_target_pairs={{0,16},{1,17},{2,18},{3,19},{4,20},{5,21},{6,22},{7,23},{8,24},{9,... | collective-permute-start | bytes 1179656 | tf_op jit(solution)/shard_map/ppermute | solution.py:27
  57.8 8.0 %collective-permute-start.1 = (bf16[128,1536]{1,0:T(8,128)(2,1)S(1)}, bf16[128,1536]{1,0:T(8,128)(2,1)S(1)}, u32[]{:S(2)}, u32[]{:S(2)}) collective-permute-start(bf16[128,1536]{1,0:T(8,128)(2,1)S(1)} %collective-permute-done), channel_id=1, source_target_pairs={{16,32},{17,33},{18,34},{19,35},{20,36},{21,37},{22,38},{23,39},{2... | collective-permute-start | bytes 1179656 | tf_op jit(solution)/shard_map/ppermute | solution.py:27
  59.1 5.4 %collective-permute-start.3 = (bf16[128,1536]{1,0:T(8,128)(2,1)S(1)}, bf16[128,1536]{1,0:T(8,128)(2,1)S(1)}, u32[]{:S(2)}, u32[]{:S(2)}) collective-permute-start(bf16[128,1536]{1,0:T(8,128)(2,1)S(1)} %collective-permute-done), channel_id=1, source_target_pairs={{0,16},{1,17},{2,18},{3,19},{4,20},{5,21},{6,22},{7,23},{8,24},{9,... | collective-permute-start | bytes 1179656 | tf_op jit(solution)/shard_map/ppermute | solution.py:27
  66.9 11.7 %copy-start.3 = (bf16[2048,384]{1,0:T(8,128)(2,1)S(1)}, bf16[2048,384]{1,0:T(8,128)(2,1)}, u32[]{:S(2)}) copy-start(bf16[2048,384]{1,0:T(8,128)(2,1)} %param.6) | copy-start | bytes 4718596
  67.0 8.6 %collective-permute-start.5 = (bf16[128,768]{1,0:T(8,128)(2,1)S(1)}, bf16[128,768]{1,0:T(8,128)(2,1)S(1)}, u32[]{:S(2)}, u32[]{:S(2)}) collective-permute-start(bf16[128,768]{1,0:T(8,128)(2,1)S(1)} %get-tuple-element.12), channel_id=1, source_target_pairs={{0,8},{1,9},{2,10},{3,11},{4,12},{5,13},{6,14},{7,15},{8,0},{9,1},... | collective-permute-start | bytes 589832 | tf_op jit(solution)/shard_map/ppermute | solution.py:27
  76.4 32.9 %collective-permute-start.9 = (bf16[1024,384]{1,0:T(8,128)(2,1)S(1)}, bf16[1024,384]{1,0:T(8,128)(2,1)}, u32[]{:S(2)}, u32[]{:S(2)}) collective-permute-start(bf16[1024,384]{1,0:T(8,128)(2,1)S(1)} %get-tuple-element.6), channel_id=1, source_target_pairs={{0,8},{1,9},{2,10},{3,11},{4,12},{5,13},{6,14},{7,15},{8,0},{9,1},... | collective-permute-start | bytes 2359304 | tf_op jit(solution)/shard_map/ppermute | solution.py:27
  82.3 9.2 %collective-permute-start.6 = (bf16[128,1536]{1,0:T(8,128)(2,1)S(1)}, bf16[128,1536]{1,0:T(8,128)(2,1)S(1)}, u32[]{:S(2)}, u32[]{:S(2)}) collective-permute-start(bf16[128,1536]{1,0:T(8,128)(2,1)S(1)} %fusion.2), channel_id=1, source_target_pairs={{0,16},{1,17},{2,18},{3,19},{4,20},{5,21},{6,22},{7,23},{8,24},{9,... | collective-permute-start | bytes 1179656 | tf_op jit(solution)/shard_map/ppermute | solution.py:27
  89.5 26.7 %collective-permute-start.8 = (bf16[128,1536]{1,0:T(8,128)(2,1)}, bf16[128,1536]{1,0:T(8,128)(2,1)}, u32[]{:S(2)}, u32[]{:S(2)}) collective-permute-start(bf16[128,1536]{1,0:T(8,128)(2,1)} %fusion.3), channel_id=1, source_target_pairs={{0,464},{1,465},{2,466},{3,467},{4,468},{5,469},{6,470},{7,471},{8... | collective-permute-start | bytes 1179656 | tf_op jit(solution)/shard_map/ppermute | solution.py:27
  92.6 25.5 %collective-permute-start.7 = (bf16[128,1536]{1,0:T(8,128)(2,1)}, bf16[128,1536]{1,0:T(8,128)(2,1)}, u32[]{:S(2)}, u32[]{:S(2)}) collective-permute-start(bf16[128,1536]{1,0:T(8,128)(2,1)} %add_convert_fusion), channel_id=1, source_target_pairs={{0,480},{1,481},{2,482},{3,483},{4,484},{5,485},{6,486},{7,487},{8... | collective-permute-start | bytes 1179656 | tf_op jit(solution)/shard_map/ppermute | solution.py:27
  125.6 6.5 %collective-permute-start.10 = (bf16[384,768]{1,0:T(8,128)(2,1)S(1)}, bf16[384,768]{1,0:T(8,128)(2,1)S(1)}, u32[]{:S(2)}, u32[]{:S(2)}) collective-permute-start(bf16[384,768]{1,0:T(8,128)(2,1)S(1)} %slice.119), channel_id=1, source_target_pairs={{0,16},{1,17},{2,18},{3,19},{4,20},{5,21},{6,22},{7,23},{8,24},{9,... | collective-permute-start | bytes 1769480 | tf_op jit(solution)/shard_map/ppermute | solution.py:27
  132.2 25.9 %copy-start.2 = (bf16[128,1536]{1,0:T(8,128)(2,1)S(1)}, bf16[128,1536]{1,0:T(8,128)(2,1)}, u32[]{:S(2)}) copy-start(bf16[128,1536]{1,0:T(8,128)(2,1)} %param.5) | copy-start | bytes 1179652
  132.2 25.9 %copy-start.5 = (bf16[128,128]{1,0:T(8,128)(2,1)S(1)}, bf16[128,128]{1,0:T(8,128)(2,1)}, u32[]{:S(2)}) copy-start(bf16[128,128]{1,0:T(8,128)(2,1)} %copy-done.4) | copy-start | bytes 98308
  132.3 7.4 %collective-permute-start.13 = (bf16[96,768]{1,0:T(8,128)(2,1)S(1)}, bf16[96,768]{1,0:T(8,128)(2,1)S(1)}, u32[]{:S(2)}, u32[]{:S(2)}) collective-permute-start(bf16[96,768]{1,0:T(8,128)(2,1)S(1)} %get-tuple-element.9), channel_id=1, source_target_pairs={{0,96},{1,97},{2,98},{3,99},{4,100},{5,101},{6,102},{7,103},{8,104... | collective-permute-start | bytes 442376 | tf_op jit(solution)/shard_map/ppermute | solution.py:27
  134.3 8.5 %collective-permute-start.12 = (bf16[96,768]{1,0:T(8,128)(2,1)S(1)}, bf16[96,768]{1,0:T(8,128)(2,1)S(1)}, u32[]{:S(2)}, u32[]{:S(2)}) collective-permute-start(bf16[96,768]{1,0:T(8,128)(2,1)S(1)} %get-tuple-element.10), channel_id=1, source_target_pairs={{0,64},{1,65},{2,66},{3,67},{4,68},{5,69},{6,70},{7,71},{8,72},{9,... | collective-permute-start | bytes 442376 | tf_op jit(solution)/shard_map/ppermute | solution.py:27
  136.3 9.7 %collective-permute-start.11 = (bf16[96,768]{1,0:T(8,128)(2,1)S(1)}, bf16[96,768]{1,0:T(8,128)(2,1)S(1)}, u32[]{:S(2)}, u32[]{:S(2)}) collective-permute-start(bf16[96,768]{1,0:T(8,128)(2,1)S(1)} %get-tuple-element.8), channel_id=1, source_target_pairs={{0,32},{1,33},{2,34},{3,35},{4,36},{5,37},{6,38},{7,39},{8,40},{9,... | collective-permute-start | bytes 442376 | tf_op jit(solution)/shard_map/ppermute | solution.py:27
  146.1 13.7 %collective-permute-start.16 = (bf16[24,768]{1,0:T(8,128)(2,1)S(1)}, bf16[24,768]{1,0:T(8,128)(2,1)S(1)}, u32[]{:S(2)}, u32[]{:S(2)}) collective-permute-start(bf16[24,768]{1,0:T(8,128)(2,1)S(1)} %get-tuple-element.14), channel_id=1, source_target_pairs={{0,384},{1,385},{2,386},{3,387},{4,388},{5,389},{6,390},{7,391},{8... | collective-permute-start | bytes 110600 | tf_op jit(solution)/shard_map/ppermute | solution.py:27
  150.5 9.3 %collective-permute-start.15 = (bf16[24,768]{1,0:T(8,128)(2,1)S(1)}, bf16[24,768]{1,0:T(8,128)(2,1)S(1)}, u32[]{:S(2)}, u32[]{:S(2)}) collective-permute-start(bf16[24,768]{1,0:T(8,128)(2,1)S(1)} %get-tuple-element.15), channel_id=1, source_target_pairs={{0,256},{1,257},{2,258},{3,259},{4,260},{5,261},{6,262},{7,263},{8... | collective-permute-start | bytes 110600 | tf_op jit(solution)/shard_map/ppermute | solution.py:27
  153.8 7.1 %collective-permute-start.14 = (bf16[24,768]{1,0:T(8,128)(2,1)S(1)}, bf16[24,768]{1,0:T(8,128)(2,1)S(1)}, u32[]{:S(2)}, u32[]{:S(2)}) collective-permute-start(bf16[24,768]{1,0:T(8,128)(2,1)S(1)} %get-tuple-element.13), channel_id=1, source_target_pairs={{0,128},{1,129},{2,130},{3,131},{4,132},{5,133},{6,134},{7,135},{8... | collective-permute-start | bytes 110600 | tf_op jit(solution)/shard_map/ppermute | solution.py:27
  161.0 8.1 %collective-permute-start.17 = (f32[12,768]{1,0:T(8,128)S(1)}, f32[12,768]{1,0:T(8,128)S(1)}, u32[]{:S(2)}, u32[]{:S(2)}) collective-permute-start(f32[12,768]{1,0:T(8,128)S(1)} %get-tuple-element.17), channel_id=1, source_target_pairs={{0,8},{1,9},{2,10},{3,11},{4,12},{5,13},{6,14},{7,15},{8,0},{9,1},... | collective-permute-start | bytes 110600 | tf_op jit(solution)/shard_map/ppermute | solution.py:27
  (2 other events, 7.3 us)
Sparse Core Ops, SparseCore 0:
  76.5 40.6 all-gather.1

commit v3 on v2

v3 whole, which is shorter than its diff:
```python
import math

import jax
import jax.numpy as jnp
from jax import lax
from jax.experimental import pallas as pl
from jax.experimental.pallas import tpu as pltpu
from jax.sharding import PartitionSpec as P

SCALE_T = 10.0
BIAS_T = -1.0
EPSILON = 1e-06

Z_HI, X, CORE, Z_LO, Y = 4, 4, 2, 2, 8


def moved(value, where):
    pairs = []
    for source in range(Z_HI * X * CORE * Z_LO * Y):
        rest, y = divmod(source, Y)
        rest, z_lo = divmod(rest, Z_LO)
        rest, core = divmod(rest, CORE)
        z_hi, x = divmod(rest, X)
        target = where(z_hi, x, core, z_lo, y)
        if target is None:
            continue
        a, b, c, d, e = target
        pairs.append((source, ((((a % Z_HI) * X + b % X) * CORE + c % CORE) * Z_LO + d % Z_LO) * Y + e % Y))
    return lax.ppermute(value, ("loop", "mp"), pairs)


def next_chip(by):
    def where(z_hi, x, core, z_lo, y):
        chip = z_hi * X + x + by
        return chip // X, chip % X, core, z_lo, y

    return where


def cross(z_hi, x, core, z_lo, y):
    if core == 1 and x == X - 1:
        return None
    chip = z_hi * X + x + 2 * core
    return chip // X, chip % X, 1 - core, z_lo, y


def along_x(by):
    return lambda z_hi, x, core, z_lo, y: (z_hi, x + by, core, z_lo, y)


def back_along_x(z_hi, x, core, z_lo, y):
    return z_hi, x - 2 * (1 - core), 1 - core, z_lo, y


def back_z(z_hi, x, core, z_lo, y):
    if x == X - 1 or (x == X - 2 and core == 1):
        return z_hi - 1, x, core, z_lo, y
    return None


def next_y(by):
    return lambda z_hi, x, core, z_lo, y: (z_hi, x, core, z_lo, y + by)


def third_hop(z_hi, x, core, z_lo, y):
    return (z_hi, 1, 0, z_lo, y) if x == 0 and core == 1 else None


def zero_of(value):
    return jnp.minimum(jnp.abs(value[0, 0].astype(jnp.float32)), 0.0)


def zeros_of(value, rows):
    return jnp.minimum(jnp.abs(value[:rows, :1].astype(jnp.float32)), 0.0)


def other_core(z_hi, x, core, z_lo, y):
    return z_hi, x, 1 - core, z_lo, y


def other_z_lo(z_hi, x, core, z_lo, y):
    return z_hi, x, core, 1 - z_lo, y


def normalize(values):
    widened = values.astype(jnp.float32)
    inverse = lax.rsqrt(jnp.sum(widened * widened, axis=1, keepdims=True) + EPSILON)
    return (widened * inverse, inverse)


def backward_norm(unit_rows, inverse, upstream):
    return (upstream - unit_rows * jnp.sum(unit_rows * upstream, axis=1, keepdims=True)) * inverse


def pair_terms(image_low, text_low, positives, first_col):
    scores = (
        SCALE_T
        * lax.dot_general(
            image_low, text_low, (((1,), (1,)), ((), ())), preferred_element_type=jnp.float32
        )
        + BIAS_T
    )
    columns = first_col + lax.broadcasted_iota(jnp.int32, scores.shape, 1)
    target = (positives[:, None] == columns).astype(jnp.float32)
    coefficient = (jax.nn.sigmoid(scores) - target).astype(jnp.bfloat16)
    image_part = SCALE_T * jnp.dot(coefficient, text_low, preferred_element_type=jnp.float32)
    return (image_part, coefficient)


def text_terms(image_low, coefficient, scale):
    return scale * lax.dot_general(
        coefficient, image_low, (((0,), (0,)), ((), ())), preferred_element_type=jnp.float32
    )


def weight_product(low, high, blocks, done):
    units, depth = low.shape
    both_rows, width = blocks[0].shape
    rows = both_rows // Z_LO
    tile = 256
    keep = units // CORE

    def kernel(low_ref, high_ref, *rest):
        kept_ref, sent_ref = rest[-2:]
        right = [
            jnp.concatenate([ref[z * rows : (z + 1) * rows] for ref in rest[:Y]])
            for z in range(Z_LO)
        ]
        for at in range(0, units, keep // 2):
            rows_at = slice(at, at + keep // 2)
            value = jnp.dot(low_ref[rows_at], right[0], preferred_element_type=jnp.float32)
            value += jnp.dot(high_ref[rows_at], right[1], preferred_element_type=jnp.float32)
            if at < keep:
                kept_ref[rows_at] = value
            else:
                sent_ref[at - keep : at - keep // 2] = value.astype(sent_ref.dtype)

    whole = pl.BlockSpec((units, depth), lambda n: (0, 0))
    out = pl.BlockSpec((keep, tile), lambda n: (0, n))
    return pl.pallas_call(
        kernel,
        grid=(width // tile,),
        in_specs=[whole, whole]
        + [pl.BlockSpec((both_rows, tile), lambda n: (0, n))] * len(blocks)
        + [pl.BlockSpec(memory_space=pl.ANY)] * len(done),
        out_specs=[out, out],
        out_shape=[
            jax.ShapeDtypeStruct((keep, width), jnp.float32),
            jax.ShapeDtypeStruct((keep, width), jnp.bfloat16),
        ],
        compiler_params=pltpu.CompilerParams(vmem_limit_bytes=32 * 2**20),
        cost_estimate=pl.CostEstimate(
            flops=4 * units * depth * width, bytes_accessed=12 * 2**20, transcendentals=0
        ),
    )(low, high, *blocks, *done)


def local(img_emb, txt_emb, hidden, positives):
    bf16 = jnp.bfloat16
    loop_index = lax.axis_index("loop")
    model_index = lax.axis_index("mp")
    core = loop_index % CORE
    x = (loop_index // CORE) % X
    z_hi = loop_index // (CORE * X)
    z_lo = model_index // Y
    groups = lax.axis_size("loop")
    splits = lax.axis_size("mp")
    rows, width = img_emb.shape
    half = width // Z_LO
    units = hidden.shape[1]
    share = units // groups

    text_unit, text_inv = normalize(txt_emb)
    text_low = text_unit.astype(bf16)
    image_unit, image_inv = normalize(img_emb)
    image_low = image_unit.astype(bf16)
    two_back = moved(text_low, next_chip(1))
    crossed = moved(text_low, cross)
    swapped = moved(two_back, other_core)
    crossed = jnp.where((x == 1) & (core == 0), moved(two_back, third_hop), crossed)

    place = lax.broadcasted_iota(jnp.int32, (units, Z_LO * units), 1)
    at_core = (place // (Z_LO * units // CORE) + core) % CORE
    at_chip = (place // (Z_LO * share)) % (X * Z_HI)
    unit = (at_chip * CORE + at_core) * share + place % share
    here = lax.broadcasted_iota(jnp.int32, place.shape, 0) == unit
    which = (place // share) % Z_LO
    pick = (here & (which == 0)).astype(bf16), (here & (which == 1)).astype(bf16)

    def both_units(own, before):
        own = jnp.roll(own, -rows * (model_index % Y), axis=0)
        other = moved(own + zero_of(before).astype(bf16), other_z_lo)
        units_first = (((0,), (1,)), ((), ()))
        mixed = lax.dot_general(pick[0], own, units_first, preferred_element_type=bf16)
        mixed += lax.dot_general(pick[1], other, units_first, preferred_element_type=bf16)
        return mixed, other

    image_total = jnp.zeros(img_emb.shape, jnp.float32)
    coefficients = []
    far = jnp.where(core == 0, 3, 1)
    for text_block, offset in ((text_low, 0), (two_back, 2), (crossed, far), (swapped, 4 - far)):
        owner = (loop_index - offset) % groups
        first_col = (owner * splits + model_index) * rows
        image_part, coefficient = pair_terms(image_low, text_block, positives, first_col)
        image_total = image_total + image_part
        coefficients.append(coefficient)
    low, early = both_units(hidden[: Y * rows], coefficients[0])
    image_grad = backward_norm(image_unit, image_inv + zeros_of(early, rows), image_total).astype(bf16)

    left, right = image_grad[:, :half], image_grad[:, half:]
    first = z_lo == 0
    mine = jnp.where(first, left, right)
    theirs = moved(jnp.where(first, right, left), other_z_lo)
    both = jnp.where(first, jnp.stack([mine, theirs]), jnp.stack([theirs, mine]))
    block = both.reshape(Z_LO * rows, half)
    got = [block] + [None] * (Y - 1)
    forward = backward = block
    for step in range(1, Y // 2 + 1):
        forward = got[Y - step] = moved(forward, next_y(1))
        if step < Y // 2:
            backward = got[step] = moved(backward, next_y(-1))

    scale = SCALE_T + zeros_of(image_grad, rows)
    text_parts = [text_terms(image_low, coefficient, scale) for coefficient in coefficients]
    back = moved(text_parts[3].astype(bf16), other_core)
    back_two = moved((text_parts[1] + back.astype(jnp.float32)).astype(bf16), along_x(-1))
    back_cross = moved(text_parts[2].astype(bf16), back_along_x)
    back_two, back_cross = back_two.astype(jnp.float32), back_cross.astype(jnp.float32)
    far_two, far_cross = x == X - 1, (x >= X - 2) & (core == 1)
    leaving = jnp.where(far_two, back_two, 0.0) + jnp.where(far_cross, back_cross, 0.0)
    staying = jnp.where(far_two, 0.0, back_two) + jnp.where(far_cross, 0.0, back_cross)
    back_far = moved(leaving.astype(bf16), back_z)
    text_total = text_parts[0] + staying + back_far.astype(jnp.float32)
    text_grad = backward_norm(text_unit, text_inv, text_total).astype(bf16)

    high, _ = both_units(hidden[Y * rows :], image_grad)
    kept, sent = weight_product(low, high, got, (back_far,))
    total = kept + moved(sent, other_core).astype(jnp.float32)
    part = total.shape[0]
    pieces = lax.all_to_all(
        total.astype(bf16).reshape(X * Z_HI, part // (X * Z_HI), half),
        "loop",
        0,
        0,
        tiled=True,
        axis_index_groups=[list(range(c, groups, CORE)) for c in range(CORE)],
    )
    total = jnp.sum(pieces.astype(jnp.float32), axis=0)
    total = total / math.sqrt(rows * splits * groups)
    own = total[:share]
    rest = moved(total[share:], other_z_lo)
    weight_share = jnp.where(
        first, jnp.concatenate([own, rest], axis=1), jnp.concatenate([rest, own], axis=1)
    )
    return (text_grad, weight_share)


def solution(mesh):
    in_specs = (
        P(("loop", "mp"), None),
        P(("loop", "mp"), None),
        P("loop", "mp"),
        P(("loop", "mp")),
    )
    out_specs = (P(("loop", "mp"), None), P(("mp", "loop"), None))
    return jax.shard_map(local, mesh=mesh, in_specs=in_specs, out_specs=out_specs, check_vma=False)
```

time: 179 us -> 162 us (0.905)
  waiting for transfers between devices: 65.6 us -> 42 us
  starting transfers between devices: 59.5 us -> 80.4 us
  between operations: 17.4 us -> 2.95 us
  other arithmetic: 5.72 us -> 12.9 us
  local copies, waits for them, and re-layouts: 8.2 us -> 3.51 us
  matrix products: 20.3 us -> 15.9 us
  Pallas kernels: 0 us -> 3.38 us
    ppermute x18 -> x20, waiting for transfers between devices: 65.5 us -> 24.3 us  [moved(): return lax.ppermute(value, ('loop', 'mp'), pairs)]
    all_to_all x0 -> x1, waiting for transfers between devices: none -> 17.7 us  [local(): lax.all_to_all(total.astype(bf16).reshape(X * Z_HI, part // (X * Z_HI), h...]
    ppermute x18 -> x20, starting transfers between devices: 59.4 us -> 70 us  [moved(): return lax.ppermute(value, ('loop', 'mp'), pairs)]
    all_to_all x0 -> x1, starting transfers between devices: none -> 10.3 us  [local(): lax.all_to_all(total.astype(bf16).reshape(X * Z_HI, part // (X * Z_HI), h...]
    unnamed x4 -> x2, matrix products: 7.98 us -> 3.96 us
    pallas_call x0 -> x1, Pallas kernels: none -> 3.38 us  [weight_product(): pl.pallas_call(kernel, grid=(width // tile,), in_specs=[whole, whole] + [...]
    slice x8 -> x3, local copies, waits for them, and re-layouts: 5.73 us -> 2.58 us  [the longest x1 1.53 us: local(): high, _ = both_units(hidden[Y * rows:], image_grad)]
    dot_general x4, matrix products: 4.19 us -> 1.35 us  [text_terms(): lax.dot_general(coefficient, image_low, (((0,), (0,)), ((), ())), preferr...]
  transfers between devices with their start and end apart: 19 -> 21, of which waited for: 8 -> 10; matrix products, arithmetic and copies ran while one was open for 14% -> 17% of each run, Pallas kernels for 0% -> 0%
where the time goes in v3:
time: 162 us; the launch traced here: 161 us
  starting transfers between devices  80.4 us (50%)
  waiting for transfers between devices  42 us (26%)
  matrix products  15.9 us (10%)
  other arithmetic  12.9 us (8%)
  local copies, waits for them, and re-layouts  3.51 us (2%)
  Pallas kernels  3.38 us (2%)
  between operations  2.95 us (2%)
    ppermute x20, starting transfers between devices, moved(): return lax.ppermute(value, ('loop', 'mp'), pairs)  70 us
    ppermute x20, waiting for transfers between devices, moved(): return lax.ppermute(value, ('loop', 'mp'), pairs)  24.3 us
    all_to_all x1, waiting for transfers between devices, local(): lax.all_to_all(total.astype(bf16).reshape(X * Z_HI, part // (X * Z_HI), h...  17.7 us
    all_to_all x1, starting transfers between devices, local(): lax.all_to_all(total.astype(bf16).reshape(X * Z_HI, part // (X * Z_HI), h...  10.3 us
    unnamed x2, matrix products  3.96 us
    pallas_call x1, Pallas kernels, weight_product(): pl.pallas_call(kernel, grid=(width // tile,), in_specs=[whole, whole] + [...  3.38 us
  transfers between devices with their start and end apart: 21, of which 10 were waited for; matrix products, arithmetic and copies ran while one was open for 17% of the time, Pallas kernels for 0%

profile of v3, /device:TPU:1, one launch (start us, length us, event | category | flops | bytes accessed | tf_op | source)
XLA Modules:
  0.0 161.0 jit_solution(680236165178262318)
XLA Ops:
  3.0 6.0 %collective-permute-start.2 = (bf16[128,1536]{1,0:T(8,128)(2,1)S(1)}, bf16[128,1536]{1,0:T(8,128)(2,1)S(1)}, u32[]{:S(2)}, u32[]{:S(2)}) collective-permute-start(bf16[128,1536]{1,0:T(8,128)(2,1)S(1)} %fusion.43), channel_id=1, source_target_pairs={{0,16},{1,17},{2,18},{3,19},{4,20},{5,21},{6,22},{7,23},{8,24},{9,... | collective-permute-start | bytes 1179656 | tf_op jit(solution)/shard_map/ppermute | solution.py:29
  9.1 2.2 %collective-permute-start = (bf16[128,1536]{1,0:T(8,128)(2,1)S(1)}, bf16[128,1536]{1,0:T(8,128)(2,1)}, u32[]{:S(2)}, u32[]{:S(2)}) collective-permute-start(bf16[128,1536]{1,0:T(8,128)(2,1)S(1)} %fusion.43), channel_id=1, source_target_pairs={{0,32},{1,33},{2,34},{3,35},{4,36},{5,37},{6,38},{7,39},{8,40},{9,... | collective-permute-start | bytes 1179656 | tf_op jit(solution)/shard_map/ppermute | solution.py:29
  15.7 4.0 %collective-permute-start.4 = (bf16[1024,384]{0,1:T(8,128)(2,1)S(1)}, bf16[1024,384]{0,1:T(8,128)(2,1)}, u32[]{:S(2)}, u32[]{:S(2)}) collective-permute-start(bf16[1024,384]{0,1:T(8,128)(2,1)S(1)} %broadcast_add_fusion.1), channel_id=1, source_target_pairs={{0,8},{1,9},{2,10},{3,11},{4,12},{5,13},{6,14},{7,15},{8,0},{9,1},... | collective-permute-start | bytes 2359304 | tf_op jit(solution)/shard_map/ppermute | solution.py:29
  23.4 3.0 %fusion.93 = bf16[768,1024]{1,0:T(8,128)(2,1)} fusion(s32[]{:T(128)S(6)} %select_n.186, bf16[1024,384]{0,1:T(8,128)(2,1)S(1)} %copy.27, s32[768]{0:T(1024)} %get-tuple-element.23, s32[768]{0:T(1024)} %get-tuple-element.26, pred[768]{0:T(1024)(128)(4,1)} %get-tuple-element.19, s32[768]{0:T(1024)} %get-tuple-element.24, s32[768]{0:T(1024)S(1)} %get-tuple-element.25, ...), kind=kOutput, calls=%fused_computation.153 | convolution fusion | flops 618823680 | bytes 2386952 | tf_op jit(solution)/shard_map/dot_general | solution.py:194
  26.5 2.9 %convolution_convert_fusion.1 = bf16[768,1024]{1,0:T(8,128)(2,1)} fusion(s32[]{:T(128)S(6)} %select_n.186, bf16[1024,384]{1,0:T(8,128)(2,1)S(1)} %get-tuple-element.7, s32[768]{0:T(1024)S(1)} %copy-done.8, s32[768]{0:T(1024)S(1)} %copy-done.6, pred[768]{0:T(1024)(128)(4,1)S(1)} %copy-done.22, s32[768]{0:T(1024)S(1)} %copy-done.10, ...), kind=kOutput, calls=%fused_computation.24 | convolution fusion | flops 619905024 | bytes 2386952
  31.5 10.1 %collective-permute-start.3 = (bf16[128,1536]{1,0:T(8,128)(2,1)}, bf16[128,1536]{1,0:T(8,128)(2,1)S(1)}, u32[]{:S(2)}, u32[]{:S(2)}) collective-permute-start(bf16[128,1536]{1,0:T(8,128)(2,1)} %collective-permute-done), channel_id=1, source_target_pairs={{0,16},{1,17},{2,18},{3,19},{4,20},{5,21},{6,22},{7,23},{8,24},{9,... | collective-permute-start | bytes 1179656 | tf_op jit(solution)/shard_map/ppermute | solution.py:29
  48.8 1.9 %collective-permute-start.10 = (bf16[128,768]{0,1:T(8,128)(2,1)S(1)}, bf16[128,768]{0,1:T(8,128)(2,1)S(1)}, u32[]{:S(2)}, u32[]{:S(2)}) collective-permute-start(bf16[128,768]{0,1:T(8,128)(2,1)S(1)} %get-tuple-element.10), channel_id=1, source_target_pairs={{0,8},{1,9},{2,10},{3,11},{4,12},{5,13},{6,14},{7,15},{8,0},{9,1},... | collective-permute-start | bytes 589832 | tf_op jit(solution)/shard_map/ppermute | solution.py:29
  51.0 1.9 %collective-permute-start.5 = (bf16[128,1536]{1,0:T(8,128)(2,1)S(1)}, bf16[128,1536]{1,0:T(8,128)(2,1)S(1)}, u32[]{:S(2)}, u32[]{:S(2)}) collective-permute-start(bf16[128,1536]{1,0:T(8,128)(2,1)S(1)} %fusion.2), channel_id=1, source_target_pairs={{0,16},{1,17},{2,18},{3,19},{4,20},{5,21},{6,22},{7,23},{8,24},{9,... | collective-permute-start | bytes 1179656 | tf_op jit(solution)/shard_map/ppermute | solution.py:29
  53.0 3.3 %collective-permute-done.10 = bf16[128,768]{0,1:T(8,128)(2,1)S(1)} collective-permute-done((bf16[128,768]{0,1:T(8,128)(2,1)S(1)}, bf16[128,768]{0,1:T(8,128)(2,1)S(1)}, u32[]{:S(2)}, u32[]{:S(2)}) %collective-permute-start.10) | collective-permute-done | bytes 196640 | tf_op jit(solution)/shard_map/ppermute | solution.py:29
  56.5 2.7 %collective-permute-start.14 = (bf16[256,768]{1,0:T(8,128)(2,1)S(1)}, bf16[256,768]{1,0:T(8,128)(2,1)S(1)}, u32[]{:S(2)}, u32[]{:S(2)}) collective-permute-start(bf16[256,768]{1,0:T(8,128)(2,1)S(1)} %bitcast.31), channel_id=1, source_target_pairs={{0,1},{1,2},{2,3},{3,4},{4,5},{5,6},{6,7},{7,0},{8,9},{9,10},{10,1... | collective-permute-start | bytes 1179656 | tf_op jit(solution)/shard_map/ppermute | solution.py:29
  64.2 1.9 %collective-permute-start.9 = (bf16[1024,384]{1,0:T(8,128)(2,1)S(1)}, bf16[1024,384]{1,0:T(8,128)(2,1)S(1)}, u32[]{:S(2)}, u32[]{:S(2)}) collective-permute-start(bf16[1024,384]{1,0:T(8,128)(2,1)S(1)} %broadcast_add_fusion), channel_id=1, source_target_pairs={{0,8},{1,9},{2,10},{3,11},{4,12},{5,13},{6,14},{7,15},{8,0},{9,1},... | collective-permute-start | bytes 2359304 | tf_op jit(solution)/shard_map/ppermute | solution.py:29
  66.2 3.8 %collective-permute-start.11 = (bf16[256,768]{1,0:T(8,128)(2,1)S(1)}, bf16[256,768]{1,0:T(8,128)(2,1)S(1)}, u32[]{:S(2)}, u32[]{:S(2)}) collective-permute-start(bf16[256,768]{1,0:T(8,128)(2,1)S(1)} %bitcast.32), channel_id=1, source_target_pairs={{0,7},{1,0},{2,1},{3,2},{4,3},{5,4},{6,5},{7,6},{8,15},{9,8},{10,9... | collective-permute-start | bytes 1179656 | tf_op jit(solution)/shard_map/ppermute | solution.py:29
  70.3 8.5 %collective-permute-start.6 = (bf16[128,1536]{1,0:T(8,128)(2,1)S(1)}, bf16[128,1536]{1,0:T(8,128)(2,1)S(1)}, u32[]{:S(2)}, u32[]{:S(2)}) collective-permute-start(bf16[128,1536]{1,0:T(8,128)(2,1)S(1)} %add_convert_fusion.1), channel_id=1, source_target_pairs={{0,96},{1,97},{2,98},{3,99},{4,100},{5,101},{6,102},{7,103},{8,104... | collective-permute-start | bytes 1179656 | tf_op jit(solution)/shard_map/ppermute | solution.py:29
  78.9 2.1 %collective-permute-start.15 = (bf16[256,768]{1,0:T(8,128)(2,1)S(1)}, bf16[256,768]{1,0:T(8,128)(2,1)S(1)}, u32[]{:S(2)}, u32[]{:S(2)}) collective-permute-start(bf16[256,768]{1,0:T(8,128)(2,1)S(1)} %collective-permute-done.14.rest_7_), channel_id=1, source_target_pairs={{0,1},{1,2},{2,3},{3,4},{4,5},{5,6},{6,7},{7,0},{8,9},{9,10},{10,1... | collective-permute-start | bytes 1179656 | tf_op jit(solution)/shard_map/ppermute | solution.py:29
  81.1 2.3 %convolution_add_fusion.2.low_ref = bf16[768,1024]{1,0:T(8,128)(2,1)S(1)} fusion(bf16[768,1024]{1,0:T(8,128)(2,1)S(1)} %copy-done.32, bf16[1024,384]{0,1:T(8,128)(2,1)} %collective-permute-done.4, s32[768]{0:T(1024)S(1)} %copy-done.9, s32[768]{0:T(1024)S(1)} %copy-done.7, pred[768]{0:T(1024)(128)(4,1)S(1)} %copy-done.23, s32[768]{0:T(1024)S(1)} %copy-done.11, ...), kind=kOutput, calls=%fused_computation.30 | convolution fusion | flops 618037248 | bytes 3959812 | tf_op jit(solution)/shard_map/dot_general | solution.py:195
  83.4 4.6 %collective-permute-start.12 = (bf16[256,768]{1,0:T(8,128)(2,1)S(1)}, bf16[256,768]{1,0:T(8,128)(2,1)S(1)}, u32[]{:S(2)}, u32[]{:S(2)}) collective-permute-start(bf16[256,768]{1,0:T(8,128)(2,1)S(1)} %collective-permute-done.11.rest_1_), channel_id=1, source_target_pairs={{0,7},{1,0},{2,1},{3,2},{4,3},{5,4},{6,5},{7,6},{8,15},{9,8},{10,9... | collective-permute-start | bytes 1179656 | tf_op jit(solution)/shard_map/ppermute | solution.py:29
  88.0 4.1 %collective-permute-done.15.rest_6_ = bf16[256,768]{1,0:T(8,128)(2,1)S(1)} collective-permute-done((bf16[256,768]{1,0:T(8,128)(2,1)S(1)}, bf16[256,768]{1,0:T(8,128)(2,1)S(1)}, u32[]{:S(2)}, u32[]{:S(2)}) %collective-permute-start.15) | collective-permute-done | bytes 393248 | tf_op jit(solution)/shard_map/ppermute | solution.py:29
  95.6 5.3 %collective-permute-start.13 = (bf16[256,768]{1,0:T(8,128)(2,1)S(1)}, bf16[256,768]{1,0:T(8,128)(2,1)S(1)}, u32[]{:S(2)}, u32[]{:S(2)}) collective-permute-start(bf16[256,768]{1,0:T(8,128)(2,1)S(1)} %collective-permute-done.12.rest_2_), channel_id=1, source_target_pairs={{0,7},{1,0},{2,1},{3,2},{4,3},{5,4},{6,5},{7,6},{8,15},{9,8},{10,9... | collective-permute-start | bytes 1179656 | tf_op jit(solution)/shard_map/ppermute | solution.py:29
  100.9 3.5 %collective-permute-done.16.rest_5_ = bf16[256,768]{1,0:T(8,128)(2,1)S(1)} collective-permute-done((bf16[256,768]{1,0:T(8,128)(2,1)S(1)}, bf16[256,768]{1,0:T(8,128)(2,1)S(1)}, u32[]{:S(2)}, u32[]{:S(2)}) %collective-permute-start.16) | collective-permute-done | bytes 393248 | tf_op jit(solution)/shard_map/ppermute | solution.py:29
  107.5 8.2 %collective-permute-done.17.rest_4_ = bf16[256,768]{1,0:T(8,128)(2,1)S(1)} collective-permute-done((bf16[256,768]{1,0:T(8,128)(2,1)S(1)}, bf16[256,768]{1,0:T(8,128)(2,1)S(1)}, u32[]{:S(2)}, u32[]{:S(2)}) %collective-permute-start.17) | collective-permute-done | bytes 393248 | tf_op jit(solution)/shard_map/ppermute | solution.py:29
  115.7 3.4 %shard_map.59 = (f32[384,768]{1,0:T(8,128)S(1)}, bf16[384,768]{1,0:T(8,128)(2,1)S(1)}) custom-call(bf16[768,1024]{1,0:T(8,128)(2,1)S(1)} %convolution_add_fusion.2.low_ref, bf16[768,1024]{1,0:T(8,128)(2,1)S(1)} %fusion.4.high_ref, bf16[256,768]{1,0:T(8,128)(2,1)S(1)} %bitcast.33, bf16[256,768]{1,0:T(8,128)(2,1)S(1)} %collective-permute-done.11.rest_1_, ...), custom_call_target="tpu_custom_call" | custom-call | flops 2415919104 | bytes 12582912 | tf_op jit(solution)/shard_map/pallas_call | solution.py:140
  119.1 5.2 %collective-permute-start.18 = (bf16[384,768]{1,0:T(8,128)(2,1)S(1)}, bf16[384,768]{1,0:T(8,128)(2,1)S(1)}, u32[]{:S(2)}, u32[]{:S(2)}) collective-permute-start(bf16[384,768]{1,0:T(8,128)(2,1)S(1)} %get-tuple-element.6), channel_id=1, source_target_pairs={{0,16},{1,17},{2,18},{3,19},{4,20},{5,21},{6,22},{7,23},{8,24},{9,... | collective-permute-start | bytes 1769480 | tf_op jit(solution)/shard_map/ppermute | solution.py:29
  126.8 10.3 %all-to-all-start = ((bf16[16,24,768]{2,1,0:T(8,128)(2,1)}), bf16[16,24,768]{2,1,0:T(8,128)(2,1)S(1)}, u32[]{:S(2)}, u32[]{:S(2)}) async-start(bf16[16,24,768]{2,1,0:T(8,128)(2,1)} %bitcast.8), calls=%async_computation | async-start | bytes 1179648 | tf_op jit(solution)/shard_map/all_to_all | solution.py:240
  137.7 17.7 %all-to-all-done = bf16[16,24,768]{2,1,0:T(8,128)(2,1)S(1)} async-done(((bf16[16,24,768]{2,1,0:T(8,128)(2,1)}), bf16[16,24,768]{2,1,0:T(8,128)(2,1)S(1)}, u32[]{:S(2)}, u32[]{:S(2)}) %all-to-all-start) | async-done | bytes 589856 | tf_op jit(solution)/shard_map/all_to_all | solution.py:240
  (138 shorter events, 39.1 us)
Async XLA Ops:
  3.0 43.9 %collective-permute-start.2 = (bf16[128,1536]{1,0:T(8,128)(2,1)S(1)}, bf16[128,1536]{1,0:T(8,128)(2,1)S(1)}, u32[]{:S(2)}, u32[]{:S(2)}) collective-permute-start(bf16[128,1536]{1,0:T(8,128)(2,1)S(1)} %fusion.43), channel_id=1, source_target_pairs={{0,16},{1,17},{2,18},{3,19},{4,20},{5,21},{6,22},{7,23},{8,24},{9,... | collective-permute-start | bytes 1179656 | tf_op jit(solution)/shard_map/ppermute | solution.py:29
  9.1 22.4 %collective-permute-start = (bf16[128,1536]{1,0:T(8,128)(2,1)S(1)}, bf16[128,1536]{1,0:T(8,128)(2,1)}, u32[]{:S(2)}, u32[]{:S(2)}) collective-permute-start(bf16[128,1536]{1,0:T(8,128)(2,1)S(1)} %fusion.43), channel_id=1, source_target_pairs={{0,32},{1,33},{2,34},{3,35},{4,36},{5,37},{6,38},{7,39},{8,40},{9,... | collective-permute-start | bytes 1179656 | tf_op jit(solution)/shard_map/ppermute | solution.py:29
  15.7 30.2 %collective-permute-start.4 = (bf16[1024,384]{0,1:T(8,128)(2,1)S(1)}, bf16[1024,384]{0,1:T(8,128)(2,1)}, u32[]{:S(2)}, u32[]{:S(2)}) collective-permute-start(bf16[1024,384]{0,1:T(8,128)(2,1)S(1)} %broadcast_add_fusion.1), channel_id=1, source_target_pairs={{0,8},{1,9},{2,10},{3,11},{4,12},{5,13},{6,14},{7,15},{8,0},{9,1},... | collective-permute-start | bytes 2359304 | tf_op jit(solution)/shard_map/ppermute | solution.py:29
  31.5 14.1 %collective-permute-start.3 = (bf16[128,1536]{1,0:T(8,128)(2,1)}, bf16[128,1536]{1,0:T(8,128)(2,1)S(1)}, u32[]{:S(2)}, u32[]{:S(2)}) collective-permute-start(bf16[128,1536]{1,0:T(8,128)(2,1)} %collective-permute-done), channel_id=1, source_target_pairs={{0,16},{1,17},{2,18},{3,19},{4,20},{5,21},{6,22},{7,23},{8,24},{9,... | collective-permute-start | bytes 1179656 | tf_op jit(solution)/shard_map/ppermute | solution.py:29
  41.6 6.3 %collective-permute-start.1 = (bf16[128,1536]{1,0:T(8,128)(2,1)}, bf16[128,1536]{1,0:T(8,128)(2,1)S(1)}, u32[]{:S(2)}, u32[]{:S(2)}) collective-permute-start(bf16[128,1536]{1,0:T(8,128)(2,1)} %collective-permute-done), channel_id=1, source_target_pairs={{16,32},{17,33},{18,34},{19,35},{20,36},{21,37},{22,38},{23,39},{2... | collective-permute-start | bytes 1179656 | tf_op jit(solution)/shard_map/ppermute | solution.py:29
  48.8 7.4 %collective-permute-start.10 = (bf16[128,768]{0,1:T(8,128)(2,1)S(1)}, bf16[128,768]{0,1:T(8,128)(2,1)S(1)}, u32[]{:S(2)}, u32[]{:S(2)}) collective-permute-start(bf16[128,768]{0,1:T(8,128)(2,1)S(1)} %get-tuple-element.10), channel_id=1, source_target_pairs={{0,8},{1,9},{2,10},{3,11},{4,12},{5,13},{6,14},{7,15},{8,0},{9,1},... | collective-permute-start | bytes 589832 | tf_op jit(solution)/shard_map/ppermute | solution.py:29
  51.0 19.0 %collective-permute-start.5 = (bf16[128,1536]{1,0:T(8,128)(2,1)S(1)}, bf16[128,1536]{1,0:T(8,128)(2,1)S(1)}, u32[]{:S(2)}, u32[]{:S(2)}) collective-permute-start(bf16[128,1536]{1,0:T(8,128)(2,1)S(1)} %fusion.2), channel_id=1, source_target_pairs={{0,16},{1,17},{2,18},{3,19},{4,20},{5,21},{6,22},{7,23},{8,24},{9,... | collective-permute-start | bytes 1179656 | tf_op jit(solution)/shard_map/ppermute | solution.py:29
  56.5 22.3 %collective-permute-start.14 = (bf16[256,768]{1,0:T(8,128)(2,1)S(1)}, bf16[256,768]{1,0:T(8,128)(2,1)S(1)}, u32[]{:S(2)}, u32[]{:S(2)}) collective-permute-start(bf16[256,768]{1,0:T(8,128)(2,1)S(1)} %bitcast.31), channel_id=1, source_target_pairs={{0,1},{1,2},{2,3},{3,4},{4,5},{5,6},{6,7},{7,0},{8,9},{9,10},{10,1... | collective-permute-start | bytes 1179656 | tf_op jit(solution)/shard_map/ppermute | solution.py:29
  60.7 33.3 %collective-permute-start.7 = (bf16[128,1536]{1,0:T(8,128)(2,1)S(1)}, bf16[128,1536]{1,0:T(8,128)(2,1)S(1)}, u32[]{:S(2)}, u32[]{:S(2)}) collective-permute-start(bf16[128,1536]{1,0:T(8,128)(2,1)S(1)} %fusion.3), channel_id=1, source_target_pairs={{0,80},{1,81},{2,82},{3,83},{4,84},{5,85},{6,86},{7,87},{8,88},{9,... | collective-permute-start | bytes 1179656 | tf_op jit(solution)/shard_map/ppermute | solution.py:29
  62.6 18.4 %copy-start.7 = (s32[768]{0:T(1024)S(1)}, s32[768]{0:T(1024)}, u32[]{:S(2)}) copy-start(s32[768]{0:T(1024)} %get-tuple-element.26) | copy-start | bytes 9220
  62.6 18.4 %copy-start.9 = (s32[768]{0:T(1024)S(1)}, s32[768]{0:T(1024)}, u32[]{:S(2)}) copy-start(s32[768]{0:T(1024)} %get-tuple-element.23) | copy-start | bytes 9220
  64.2 42.0 %collective-permute-start.9 = (bf16[1024,384]{1,0:T(8,128)(2,1)S(1)}, bf16[1024,384]{1,0:T(8,128)(2,1)S(1)}, u32[]{:S(2)}, u32[]{:S(2)}) collective-permute-start(bf16[1024,384]{1,0:T(8,128)(2,1)S(1)} %broadcast_add_fusion), channel_id=1, source_target_pairs={{0,8},{1,9},{2,10},{3,11},{4,12},{5,13},{6,14},{7,15},{8,0},{9,1},... | collective-permute-start | bytes 2359304 | tf_op jit(solution)/shard_map/ppermute | solution.py:29
  66.2 17.2 %collective-permute-start.11 = (bf16[256,768]{1,0:T(8,128)(2,1)S(1)}, bf16[256,768]{1,0:T(8,128)(2,1)S(1)}, u32[]{:S(2)}, u32[]{:S(2)}) collective-permute-start(bf16[256,768]{1,0:T(8,128)(2,1)S(1)} %bitcast.32), channel_id=1, source_target_pairs={{0,7},{1,0},{2,1},{3,2},{4,3},{5,4},{6,5},{7,6},{8,15},{9,8},{10,9... | collective-permute-start | bytes 1179656 | tf_op jit(solution)/shard_map/ppermute | solution.py:29
  70.3 23.7 %collective-permute-start.6 = (bf16[128,1536]{1,0:T(8,128)(2,1)S(1)}, bf16[128,1536]{1,0:T(8,128)(2,1)S(1)}, u32[]{:S(2)}, u32[]{:S(2)}) collective-permute-start(bf16[128,1536]{1,0:T(8,128)(2,1)S(1)} %add_convert_fusion.1), channel_id=1, source_target_pairs={{0,96},{1,97},{2,98},{3,99},{4,100},{5,101},{6,102},{7,103},{8,104... | collective-permute-start | bytes 1179656 | tf_op jit(solution)/shard_map/ppermute | solution.py:29
  78.9 13.2 %collective-permute-start.15 = (bf16[256,768]{1,0:T(8,128)(2,1)S(1)}, bf16[256,768]{1,0:T(8,128)(2,1)S(1)}, u32[]{:S(2)}, u32[]{:S(2)}) collective-permute-start(bf16[256,768]{1,0:T(8,128)(2,1)S(1)} %collective-permute-done.14.rest_7_), channel_id=1, source_target_pairs={{0,1},{1,2},{2,3},{3,4},{4,5},{5,6},{6,7},{7,0},{8,9},{9,10},{10,1... | collective-permute-start | bytes 1179656 | tf_op jit(solution)/shard_map/ppermute | solution.py:29
  81.1 25.2 %copy-start.33 = (bf16[768,1024]{1,0:T(8,128)(2,1)S(1)}, bf16[768,1024]{1,0:T(8,128)(2,1)}, u32[]{:S(2)}) copy-start(bf16[768,1024]{1,0:T(8,128)(2,1)} %convolution_convert_fusion.1) | copy-start | bytes 4718596
  83.4 12.1 %collective-permute-start.12 = (bf16[256,768]{1,0:T(8,128)(2,1)S(1)}, bf16[256,768]{1,0:T(8,128)(2,1)S(1)}, u32[]{:S(2)}, u32[]{:S(2)}) collective-permute-start(bf16[256,768]{1,0:T(8,128)(2,1)S(1)} %collective-permute-done.11.rest_1_), channel_id=1, source_target_pairs={{0,7},{1,0},{2,1},{3,2},{4,3},{5,4},{6,5},{7,6},{8,15},{9,8},{10,9... | collective-permute-start | bytes 1179656 | tf_op jit(solution)/shard_map/ppermute | solution.py:29
  92.1 12.3 %collective-permute-start.16 = (bf16[256,768]{1,0:T(8,128)(2,1)S(1)}, bf16[256,768]{1,0:T(8,128)(2,1)S(1)}, u32[]{:S(2)}, u32[]{:S(2)}) collective-permute-start(bf16[256,768]{1,0:T(8,128)(2,1)S(1)} %collective-permute-done.15.rest_6_), channel_id=1, source_target_pairs={{0,1},{1,2},{2,3},{3,4},{4,5},{5,6},{6,7},{7,0},{8,9},{9,10},{10,1... | collective-permute-start | bytes 1179656 | tf_op jit(solution)/shard_map/ppermute | solution.py:29
  94.2 13.2 %collective-permute-start.8 = (bf16[128,1536]{1,0:T(8,128)(2,1)S(1)}, bf16[128,1536]{1,0:T(8,128)(2,1)S(1)}, u32[]{:S(2)}, u32[]{:S(2)}) collective-permute-start(bf16[128,1536]{1,0:T(8,128)(2,1)S(1)} %fusion.61), channel_id=1, source_target_pairs={{80,464},{81,465},{82,466},{83,467},{84,468},{85,469},{86,470},{87... | collective-permute-start | bytes 1179656 | tf_op jit(solution)/shard_map/ppermute | solution.py:29
  95.6 11.9 %collective-permute-start.13 = (bf16[256,768]{1,0:T(8,128)(2,1)S(1)}, bf16[256,768]{1,0:T(8,128)(2,1)S(1)}, u32[]{:S(2)}, u32[]{:S(2)}) collective-permute-start(bf16[256,768]{1,0:T(8,128)(2,1)S(1)} %collective-permute-done.12.rest_2_), channel_id=1, source_target_pairs={{0,7},{1,0},{2,1},{3,2},{4,3},{5,4},{6,5},{7,6},{8,15},{9,8},{10,9... | collective-permute-start | bytes 1179656 | tf_op jit(solution)/shard_map/ppermute | solution.py:29
  104.3 11.3 %collective-permute-start.17 = (bf16[256,768]{1,0:T(8,128)(2,1)S(1)}, bf16[256,768]{1,0:T(8,128)(2,1)S(1)}, u32[]{:S(2)}, u32[]{:S(2)}) collective-permute-start(bf16[256,768]{1,0:T(8,128)(2,1)S(1)} %collective-permute-done.16.rest_5_), channel_id=1, source_target_pairs={{0,1},{1,2},{2,3},{3,4},{4,5},{5,6},{6,7},{7,0},{8,9},{9,10},{10,1... | collective-permute-start | bytes 1179656 | tf_op jit(solution)/shard_map/ppermute | solution.py:29
  119.1 6.8 %collective-permute-start.18 = (bf16[384,768]{1,0:T(8,128)(2,1)S(1)}, bf16[384,768]{1,0:T(8,128)(2,1)S(1)}, u32[]{:S(2)}, u32[]{:S(2)}) collective-permute-start(bf16[384,768]{1,0:T(8,128)(2,1)S(1)} %get-tuple-element.6), channel_id=1, source_target_pairs={{0,16},{1,17},{2,18},{3,19},{4,20},{5,21},{6,22},{7,23},{8,24},{9,... | collective-permute-start | bytes 1769480 | tf_op jit(solution)/shard_map/ppermute | solution.py:29
  126.8 28.6 %all-to-all-start = ((bf16[16,24,768]{2,1,0:T(8,128)(2,1)}), bf16[16,24,768]{2,1,0:T(8,128)(2,1)S(1)}, u32[]{:S(2)}, u32[]{:S(2)}) async-start(bf16[16,24,768]{2,1,0:T(8,128)(2,1)} %bitcast.8), calls=%async_computation | async-start | bytes 1179648 | tf_op jit(solution)/shard_map/all_to_all | solution.py:240
  155.6 4.8 %collective-permute-start.19 = (f32[12,768]{1,0:T(8,128)S(1)}, f32[12,768]{1,0:T(8,128)S(1)}, u32[]{:S(2)}, u32[]{:S(2)}) collective-permute-start(f32[12,768]{1,0:T(8,128)S(1)} %get-tuple-element.12), channel_id=1, source_target_pairs={{0,8},{1,9},{2,10},{3,11},{4,12},{5,13},{6,14},{7,15},{8,0},{9,1},... | collective-permute-start | bytes 110600 | tf_op jit(solution)/shard_map/ppermute | solution.py:29
  (31 other events, 252.1 us)

commit v4 on v3

--- a/solution.py
+++ b/solution.py
@@ -113,46 +113,48 @@
     )
 
 
-def weight_product(low, high, blocks, done):
-    units, depth = low.shape
-    both_rows, width = blocks[0].shape
-    rows = both_rows // Z_LO
+def weight_product(hidden_units, blocks, done):
+    units, depth = hidden_units.shape
+    rows, width = blocks[0].shape
     tile = 256
-    keep = units // CORE
-
-    def kernel(low_ref, high_ref, *rest):
-        kept_ref, sent_ref = rest[-2:]
-        right = [
-            jnp.concatenate([ref[z * rows : (z + 1) * rows] for ref in rest[:Y]])
-            for z in range(Z_LO)
-        ]
-        for at in range(0, units, keep // 2):
-            rows_at = slice(at, at + keep // 2)
-            value = jnp.dot(low_ref[rows_at], right[0], preferred_element_type=jnp.float32)
-            value += jnp.dot(high_ref[rows_at], right[1], preferred_element_type=jnp.float32)
-            if at < keep:
-                kept_ref[rows_at] = value
-            else:
-                sent_ref[at - keep : at - keep // 2] = value.astype(sent_ref.dtype)
-
-    whole = pl.BlockSpec((units, depth), lambda n: (0, 0))
+    steps = width // (2 * tile)
+    keep = 2 * units // CORE
+    share = units // (CORE * X * Z_HI * Z_LO)
+
+    def kernel(hidden_ref, *rest):
+        kept_ref, sent_ref, laid = rest[-3:]
+        left = jnp.concatenate([ref[...] for ref in rest[:Y]])
+        right = jnp.concatenate([ref[...] for ref in rest[Y : 2 * Y]])
+        step = units // CORE
+        for at in range(0, units, step):
+            lines = hidden_ref[at : at + step]
+            to = kept_ref if at == 0 else laid
+            for side, columns in enumerate((left, right)):
+                value = jnp.dot(lines, columns, preferred_element_type=jnp.float32)
+                for k in range(step // share):
+                    first = (2 * k + side) * share
+                    to[first : first + share] = value[k * share : (k + 1) * share]
+        sent_ref[...] = laid[...].astype(sent_ref.dtype)
+
     out = pl.BlockSpec((keep, tile), lambda n: (0, n))
     return pl.pallas_call(
         kernel,
-        grid=(width // tile,),
-        in_specs=[whole, whole]
-        + [pl.BlockSpec((both_rows, tile), lambda n: (0, n))] * len(blocks)
+        grid=(steps,),
+        in_specs=[pl.BlockSpec((units, depth), lambda n: (0, 0))]
+        + [pl.BlockSpec((rows, tile), lambda n: (0, n))] * Y
+        + [pl.BlockSpec((rows, tile), lambda n: (0, n + steps))] * Y
         + [pl.BlockSpec(memory_space=pl.ANY)] * len(done),
         out_specs=[out, out],
         out_shape=[
-            jax.ShapeDtypeStruct((keep, width), jnp.float32),
-            jax.ShapeDtypeStruct((keep, width), jnp.bfloat16),
+            jax.ShapeDtypeStruct((keep, width // 2), jnp.float32),
+            jax.ShapeDtypeStruct((keep, width // 2), jnp.bfloat16),
         ],
-        compiler_params=pltpu.CompilerParams(vmem_limit_bytes=32 * 2**20),
+        scratch_shapes=[pltpu.VMEM((keep, tile), jnp.float32)],
+        compiler_params=pltpu.CompilerParams(vmem_limit_bytes=40 * 2**20),
         cost_estimate=pl.CostEstimate(
-            flops=4 * units * depth * width, bytes_accessed=12 * 2**20, transcendentals=0
+            flops=2 * units * depth * width, bytes_accessed=12 * 2**20, transcendentals=0
         ),
-    )(low, high, *blocks, *done)
+    )(hidden_units, *blocks, *blocks, *done)
 
 
 def local(img_emb, txt_emb, hidden, positives):
@@ -166,7 +168,6 @@
     groups = lax.axis_size("loop")
     splits = lax.axis_size("mp")
     rows, width = img_emb.shape
-    half = width // Z_LO
     units = hidden.shape[1]
     share = units // groups
 
@@ -182,16 +183,23 @@
     place = lax.broadcasted_iota(jnp.int32, (units, Z_LO * units), 1)
     at_core = (place // (Z_LO * units // CORE) + core) % CORE
     at_chip = (place // (Z_LO * share)) % (X * Z_HI)
+    at_z_lo = (place // share) % Z_LO
     unit = (at_chip * CORE + at_core) * share + place % share
     here = lax.broadcasted_iota(jnp.int32, place.shape, 0) == unit
-    which = (place // share) % Z_LO
-    pick = (here & (which == 0)).astype(bf16), (here & (which == 1)).astype(bf16)
-
-    def both_units(own, before):
-        own = jnp.roll(own, -rows * (model_index % Y), axis=0)
-        other = moved(own + zero_of(before).astype(bf16), other_z_lo)
+    pick = (here & (at_z_lo == z_lo)).astype(bf16), (here & (at_z_lo != z_lo)).astype(bf16)
+    column_index = lax.broadcasted_iota(jnp.int32, (rows, rows), 1)
+
+    def in_ring_order(low):
+        at = jnp.where(low, 0, Y * rows)
+        return jnp.roll(lax.dynamic_slice_in_dim(hidden, at, Y * rows), -rows * (model_index % Y), 0)
+
+    first = z_lo == 0
+
+    def all_units(before):
         units_first = (((0,), (1,)), ((), ()))
+        own = in_ring_order(first) + zero_of(before).astype(bf16)
         mixed = lax.dot_general(pick[0], own, units_first, preferred_element_type=bf16)
+        other = moved(in_ring_order(~first) + zero_of(mixed).astype(bf16), other_z_lo)
         mixed += lax.dot_general(pick[1], other, units_first, preferred_element_type=bf16)
         return mixed, other
 
@@ -204,15 +212,10 @@
         image_part, coefficient = pair_terms(image_low, text_block, positives, first_col)
         image_total = image_total + image_part
         coefficients.append(coefficient)
-    low, early = both_units(hidden[: Y * rows], coefficients[0])
-    image_grad = backward_norm(image_unit, image_inv + zeros_of(early, rows), image_total).astype(bf16)
-
-    left, right = image_grad[:, :half], image_grad[:, half:]
-    first = z_lo == 0
-    mine = jnp.where(first, left, right)
-    theirs = moved(jnp.where(first, right, left), other_z_lo)
-    both = jnp.where(first, jnp.stack([mine, theirs]), jnp.stack([theirs, mine]))
-    block = both.reshape(Z_LO * rows, half)
+    hidden_units, early = all_units(coefficients[0])
+    image_grad = backward_norm(image_unit, image_inv, image_total).astype(bf16)
+
+    block = image_grad
     got = [block] + [None] * (Y - 1)
     forward = backward = block
     for step in range(1, Y // 2 + 1):
@@ -220,7 +223,7 @@
         if step < Y // 2:
             backward = got[step] = moved(backward, next_y(-1))
 
-    scale = SCALE_T + zeros_of(image_grad, rows)
+    scale = SCALE_T + zeros_of(image_grad, rows) + zeros_of(early, rows)
     text_parts = [text_terms(image_low, coefficient, scale) for coefficient in coefficients]
     back = moved(text_parts[3].astype(bf16), other_core)
     back_two = moved((text_parts[1] + back.astype(jnp.float32)).astype(bf16), along_x(-1))
@@ -233,25 +236,28 @@
     text_total = text_parts[0] + staying + back_far.astype(jnp.float32)
     text_grad = backward_norm(text_unit, text_inv, text_total).astype(bf16)
 
-    high, _ = both_units(hidden[Y * rows :], image_grad)
-    kept, sent = weight_product(low, high, got, (back_far,))
+    kept, sent = weight_product(hidden_units, got, (back_far,))
     total = kept + moved(sent, other_core).astype(jnp.float32)
-    part = total.shape[0]
+    places = X * Z_HI * Z_LO
+    peers = [
+        [
+            (chip * CORE + c) * splits + z * Y + y
+            for chip in range(X * Z_HI)
+            for z in range(Z_LO)
+        ]
+        for c in range(CORE)
+        for y in range(Y)
+    ]
     pieces = lax.all_to_all(
-        total.astype(bf16).reshape(X * Z_HI, part // (X * Z_HI), half),
-        "loop",
+        total.astype(bf16).reshape(places, 2 * share, width // 2),
+        ("loop", "mp"),
         0,
         0,
         tiled=True,
-        axis_index_groups=[list(range(c, groups, CORE)) for c in range(CORE)],
-    )
-    total = jnp.sum(pieces.astype(jnp.float32), axis=0)
-    total = total / math.sqrt(rows * splits * groups)
-    own = total[:share]
-    rest = moved(total[share:], other_z_lo)
-    weight_share = jnp.where(
-        first, jnp.concatenate([own, rest], axis=1), jnp.concatenate([rest, own], axis=1)
-    )
+        axis_index_groups=peers,
+    )
+    total = jnp.sum(pieces.astype(jnp.float32), axis=0) / math.sqrt(rows * splits * groups)
+    weight_share = jnp.concatenate([total[:share], total[share:]], axis=1)
     return (text_grad, weight_share)
 
 

time: 162 us -> 150 us (0.926)
  starting transfers between devices: 80.4 us -> 70.8 us
  waiting for transfers between devices: 42 us -> 50.4 us
  matrix products: 15.9 us -> 10.7 us
  other arithmetic: 12.9 us -> 8.68 us
  local copies, waits for them, and re-layouts: 3.51 us -> 1.39 us
    ppermute x20 -> x17, starting transfers between devices: 70 us -> 59 us  [moved(): return lax.ppermute(value, ('loop', 'mp'), pairs)]
    all_to_all x1, waiting for transfers between devices: 17.7 us -> 28.1 us  [local(): lax.all_to_all(total.astype(bf16).reshape(places, 2 * share, width // 2),...]
    dot_general x2 -> x0, matrix products: 5.32 us -> none  [the longest x1 3.01 us: both_units(): lax.dot_general(pick[0], own, units_first, preferred_element_type=bf16)]
    ppermute x20 -> x17, waiting for transfers between devices: 24.3 us -> 22.3 us  [moved(): return lax.ppermute(value, ('loop', 'mp'), pairs)]
    add x4, other arithmetic: 1.64 us -> 0.01 us  [pair_terms(): columns = first_col + lax.broadcasted_iota(jnp.int32, scores.shape, 1)]
  transfers between devices with their start and end apart: 21 -> 18, of which waited for: 10 -> 8; matrix products, arithmetic and copies ran while one was open for 17% -> 11% of each run, Pallas kernels for 0% -> 0%
where the time goes in v4:
time: 150 us; the launch traced here: 149 us
  starting transfers between devices  70.8 us (47%)
  waiting for transfers between devices  50.4 us (34%)
  matrix products  10.7 us (7%)
  other arithmetic  8.68 us (6%)
  Pallas kernels  3.81 us (3%)
  between operations  2.9 us (2%)
    ppermute x17, starting transfers between devices, moved(): return lax.ppermute(value, ('loop', 'mp'), pairs)  59 us
    all_to_all x1, waiting for transfers between devices, local(): lax.all_to_all(total.astype(bf16).reshape(places, 2 * share, width // 2),...  28.1 us
    ppermute x17, waiting for transfers between devices, moved(): return lax.ppermute(value, ('loop', 'mp'), pairs)  22.3 us
    all_to_all x1, starting transfers between devices, local(): lax.all_to_all(total.astype(bf16).reshape(places, 2 * share, width // 2),...  11.7 us
    unnamed x2, matrix products  4.51 us
    pallas_call x1, Pallas kernels, weight_product(): pl.pallas_call(kernel, grid=(steps,), in_specs=[pl.BlockSpec((units, dept...  3.81 us
  transfers between devices with their start and end apart: 18, of which 8 were waited for; matrix products, arithmetic and copies ran while one was open for 11% of the time, Pallas kernels for 0%

profile of v4, /device:TPU:1, one launch (start us, length us, event | category | flops | bytes accessed | tf_op | source)
XLA Modules:
  0.0 148.6 jit_solution(434206951247469461)
XLA Ops:
  3.1 4.0 %collective-permute-start = (bf16[128,1536]{1,0:T(8,128)(2,1)S(1)}, bf16[128,1536]{1,0:T(8,128)(2,1)}, u32[]{:S(2)}, u32[]{:S(2)}) collective-permute-start(bf16[128,1536]{1,0:T(8,128)(2,1)S(1)} %fusion.43), channel_id=1, source_target_pairs={{0,32},{1,33},{2,34},{3,35},{4,36},{5,37},{6,38},{7,39},{8,40},{9,... | collective-permute-start | bytes 1179656 | tf_op jit(solution)/shard_map/ppermute | solution.py:29
  7.1 5.2 %collective-permute-start.2 = (bf16[128,1536]{1,0:T(8,128)(2,1)S(1)}, bf16[128,1536]{1,0:T(8,128)(2,1)S(1)}, u32[]{:S(2)}, u32[]{:S(2)}) collective-permute-start(bf16[128,1536]{1,0:T(8,128)(2,1)S(1)} %fusion.43), channel_id=1, source_target_pairs={{0,16},{1,17},{2,18},{3,19},{4,20},{5,21},{6,22},{7,23},{8,24},{9,... | collective-permute-start | bytes 1179656 | tf_op jit(solution)/shard_map/ppermute | solution.py:29
  19.2 4.0 %collective-permute-start.4 = (bf16[1024,384]{1,0:T(8,128)(2,1)S(1)}, bf16[1024,384]{1,0:T(8,128)(2,1)}, u32[]{:S(2)}, u32[]{:S(2)}) collective-permute-start(bf16[1024,384]{1,0:T(8,128)(2,1)S(1)} %fusion.66), channel_id=1, source_target_pairs={{0,8},{1,9},{2,10},{3,11},{4,12},{5,13},{6,14},{7,15},{8,0},{9,1},... | collective-permute-start | bytes 2359304 | tf_op jit(solution)/shard_map/ppermute | solution.py:29
  23.6 5.7 %collective-permute-done = bf16[128,1536]{1,0:T(8,128)(2,1)} collective-permute-done((bf16[128,1536]{1,0:T(8,128)(2,1)S(1)}, bf16[128,1536]{1,0:T(8,128)(2,1)}, u32[]{:S(2)}, u32[]{:S(2)}) %collective-permute-start) | collective-permute-done | bytes 393248 | tf_op jit(solution)/shard_map/ppermute | solution.py:29
  29.3 3.9 %collective-permute-start.3 = (bf16[128,1536]{1,0:T(8,128)(2,1)}, bf16[128,1536]{1,0:T(8,128)(2,1)S(1)}, u32[]{:S(2)}, u32[]{:S(2)}) collective-permute-start(bf16[128,1536]{1,0:T(8,128)(2,1)} %collective-permute-done), channel_id=1, source_target_pairs={{0,16},{1,17},{2,18},{3,19},{4,20},{5,21},{6,22},{7,23},{8,24},{9,... | collective-permute-start | bytes 1179656 | tf_op jit(solution)/shard_map/ppermute | solution.py:29
  40.6 3.2 %collective-permute-start.12 = (bf16[128,1536]{1,0:T(8,128)(2,1)S(1)}, bf16[128,1536]{1,0:T(8,128)(2,1)S(1)}, u32[]{:S(2)}, u32[]{:S(2)}) collective-permute-start(bf16[128,1536]{1,0:T(8,128)(2,1)S(1)} %fusion.50.rest_0_.rest_8_), channel_id=1, source_target_pairs={{0,1},{1,2},{2,3},{3,4},{4,5},{5,6},{6,7},{7,0},{8,9},{9,10},{10,1... | collective-permute-start | bytes 1179656 | tf_op jit(solution)/shard_map/ppermute | solution.py:29
  45.1 1.9 %collective-permute-start.5 = (bf16[128,1536]{1,0:T(8,128)(2,1)S(1)}, bf16[128,1536]{1,0:T(8,128)(2,1)S(1)}, u32[]{:S(2)}, u32[]{:S(2)}) collective-permute-start(bf16[128,1536]{1,0:T(8,128)(2,1)S(1)} %fusion.2), channel_id=1, source_target_pairs={{0,16},{1,17},{2,18},{3,19},{4,20},{5,21},{6,22},{7,23},{8,24},{9,... | collective-permute-start | bytes 1179656 | tf_op jit(solution)/shard_map/ppermute | solution.py:29
  47.0 3.8 %collective-permute-start.9 = (bf16[128,1536]{1,0:T(8,128)(2,1)S(1)}, bf16[128,1536]{1,0:T(8,128)(2,1)S(1)}, u32[]{:S(2)}, u32[]{:S(2)}) collective-permute-start(bf16[128,1536]{1,0:T(8,128)(2,1)S(1)} %fusion.50.rest_0_.rest_8_), channel_id=1, source_target_pairs={{0,7},{1,0},{2,1},{3,2},{4,3},{5,4},{6,5},{7,6},{8,15},{9,8},{10,9... | collective-permute-start | bytes 1179656 | tf_op jit(solution)/shard_map/ppermute | solution.py:29
  51.2 2.7 %collective-permute-start.7 = (bf16[128,1536]{1,0:T(8,128)(2,1)S(1)}, bf16[128,1536]{1,0:T(8,128)(2,1)S(1)}, u32[]{:S(2)}, u32[]{:S(2)}) collective-permute-start(bf16[128,1536]{1,0:T(8,128)(2,1)S(1)} %fusion.3), channel_id=1, source_target_pairs={{0,80},{1,81},{2,82},{3,83},{4,84},{5,85},{6,86},{7,87},{8,88},{9,... | collective-permute-start | bytes 1179656 | tf_op jit(solution)/shard_map/ppermute | solution.py:29
  53.9 1.9 %collective-permute-start.13 = (bf16[128,1536]{1,0:T(8,128)(2,1)S(1)}, bf16[128,1536]{1,0:T(8,128)(2,1)S(1)}, u32[]{:S(2)}, u32[]{:S(2)}) collective-permute-start(bf16[128,1536]{1,0:T(8,128)(2,1)S(1)} %collective-permute-done.12.rest_7_.rest_15_), channel_id=1, source_target_pairs={{0,1},{1,2},{2,3},{3,4},{4,5},{5,6},{6,7},{7,0},{8,9},{9,10},{10,1... | collective-permute-start | bytes 1179656 | tf_op jit(solution)/shard_map/ppermute | solution.py:29
  56.2 8.2 %collective-permute-start.6 = (bf16[128,1536]{1,0:T(8,128)(2,1)S(1)}, bf16[128,1536]{1,0:T(8,128)(2,1)S(1)}, u32[]{:S(2)}, u32[]{:S(2)}) collective-permute-start(bf16[128,1536]{1,0:T(8,128)(2,1)S(1)} %add_convert_fusion.1), channel_id=1, source_target_pairs={{0,96},{1,97},{2,98},{3,99},{4,100},{5,101},{6,102},{7,103},{8,104... | collective-permute-start | bytes 1179656 | tf_op jit(solution)/shard_map/ppermute | solution.py:29
  64.4 4.6 %collective-permute-start.10 = (bf16[128,1536]{1,0:T(8,128)(2,1)S(1)}, bf16[128,1536]{1,0:T(8,128)(2,1)S(1)}, u32[]{:S(2)}, u32[]{:S(2)}) collective-permute-start(bf16[128,1536]{1,0:T(8,128)(2,1)S(1)} %collective-permute-done.9.rest_1_.rest_9_), channel_id=1, source_target_pairs={{0,7},{1,0},{2,1},{3,2},{4,3},{5,4},{6,5},{7,6},{8,15},{9,8},{10,9... | collective-permute-start | bytes 1179656 | tf_op jit(solution)/shard_map/ppermute | solution.py:29
  69.0 1.9 %collective-permute-start.14 = (bf16[128,1536]{1,0:T(8,128)(2,1)S(1)}, bf16[128,1536]{1,0:T(8,128)(2,1)S(1)}, u32[]{:S(2)}, u32[]{:S(2)}) collective-permute-start(bf16[128,1536]{1,0:T(8,128)(2,1)S(1)} %collective-permute-done.13.rest_6_.rest_14_), channel_id=1, source_target_pairs={{0,1},{1,2},{2,3},{3,4},{4,5},{5,6},{6,7},{7,0},{8,9},{9,10},{10,1... | collective-permute-start | bytes 1179656 | tf_op jit(solution)/shard_map/ppermute | solution.py:29
  70.9 4.5 %collective-permute-done.6 = bf16[128,1536]{1,0:T(8,128)(2,1)S(1)} collective-permute-done((bf16[128,1536]{1,0:T(8,128)(2,1)S(1)}, bf16[128,1536]{1,0:T(8,128)(2,1)S(1)}, u32[]{:S(2)}, u32[]{:S(2)}) %collective-permute-start.6) | collective-permute-done | bytes 393248 | tf_op jit(solution)/shard_map/ppermute | solution.py:29
  76.8 5.3 %collective-permute-start.11 = (bf16[128,1536]{1,0:T(8,128)(2,1)S(1)}, bf16[128,1536]{1,0:T(8,128)(2,1)S(1)}, u32[]{:S(2)}, u32[]{:S(2)}) collective-permute-start(bf16[128,1536]{1,0:T(8,128)(2,1)S(1)} %collective-permute-done.10.rest_2_.rest_10_), channel_id=1, source_target_pairs={{0,7},{1,0},{2,1},{3,2},{4,3},{5,4},{6,5},{7,6},{8,15},{9,8},{10,9... | collective-permute-start | bytes 1179656 | tf_op jit(solution)/shard_map/ppermute | solution.py:29
  82.2 1.9 %collective-permute-start.15 = (bf16[128,1536]{1,0:T(8,128)(2,1)S(1)}, bf16[128,1536]{1,0:T(8,128)(2,1)S(1)}, u32[]{:S(2)}, u32[]{:S(2)}) collective-permute-start(bf16[128,1536]{1,0:T(8,128)(2,1)S(1)} %collective-permute-done.14.rest_5_.rest_13_), channel_id=1, source_target_pairs={{0,1},{1,2},{2,3},{3,4},{4,5},{5,6},{6,7},{7,0},{8,9},{9,10},{10,1... | collective-permute-start | bytes 1179656 | tf_op jit(solution)/shard_map/ppermute | solution.py:29
  84.1 2.8 %fusion.4.hidden_ref = bf16[768,1024]{1,0:T(8,128)(2,1)S(1)} fusion(bf16[768,1024]{1,0:T(8,128)(2,1)} %copy-done.20, bf16[1024,384]{1,0:T(8,128)(2,1)} %collective-permute-done.4, s32[]{:T(128)S(6)} %select_n.136, s32[768]{0:T(1024)S(1)} %get-tuple-element.21, s32[768]{0:T(1024)} %copy-done.7, pred[768]{0:T(1024)(128)(4,1)} %copy-done.14, ...), kind=kOutput, calls=%fused_computation.31 | convolution fusion | flops 619118592 | bytes 3959816
  86.9 2.2 %collective-permute-done.11.rest_3_.rest_11_ = bf16[128,1536]{1,0:T(8,128)(2,1)S(1)} collective-permute-done((bf16[128,1536]{1,0:T(8,128)(2,1)S(1)}, bf16[128,1536]{1,0:T(8,128)(2,1)S(1)}, u32[]{:S(2)}, u32[]{:S(2)}) %collective-permute-start.11) | collective-permute-done | bytes 393248 | tf_op jit(solution)/shard_map/ppermute | solution.py:29
  89.1 5.1 %collective-permute-done.15.rest_4_.rest_12_ = bf16[128,1536]{1,0:T(8,128)(2,1)S(1)} collective-permute-done((bf16[128,1536]{1,0:T(8,128)(2,1)S(1)}, bf16[128,1536]{1,0:T(8,128)(2,1)S(1)}, u32[]{:S(2)}, u32[]{:S(2)}) %collective-permute-start.15) | collective-permute-done | bytes 393248 | tf_op jit(solution)/shard_map/ppermute | solution.py:29
  94.2 3.8 %shard_map.59 = (f32[768,768]{1,0:T(8,128)S(1)}, bf16[768,768]{1,0:T(8,128)(2,1)S(1)}) custom-call(bf16[768,1024]{1,0:T(8,128)(2,1)S(1)} %fusion.4.hidden_ref, bf16[128,1536]{1,0:T(8,128)(2,1)S(1)} %fusion.50.rest_0_.rest_8_, bf16[128,1536]{1,0:T(8,128)(2,1)S(1)} %collective-permute-done.9.rest_1_.rest_9_, ...), custom_call_target="tpu_custom_call" | custom-call | flops 2415919104 | bytes 12582912 | tf_op jit(solution)/shard_map/pallas_call | solution.py:140
  98.0 4.5 %collective-permute-start.16 = (bf16[768,768]{1,0:T(8,128)(2,1)S(1)}, bf16[768,768]{1,0:T(8,128)(2,1)S(1)}, u32[]{:S(2)}, u32[]{:S(2)}) collective-permute-start(bf16[768,768]{1,0:T(8,128)(2,1)S(1)} %get-tuple-element.6), channel_id=1, source_target_pairs={{0,16},{1,17},{2,18},{3,19},{4,20},{5,21},{6,22},{7,23},{8,24},{9,... | collective-permute-start | bytes 3538952 | tf_op jit(solution)/shard_map/ppermute | solution.py:29
  102.5 2.5 %collective-permute-done.16 = bf16[768,768]{1,0:T(8,128)(2,1)S(1)} collective-permute-done((bf16[768,768]{1,0:T(8,128)(2,1)S(1)}, bf16[768,768]{1,0:T(8,128)(2,1)S(1)}, u32[]{:S(2)}, u32[]{:S(2)}) %collective-permute-start.16) | collective-permute-done | bytes 1179680 | tf_op jit(solution)/shard_map/ppermute | solution.py:29
  106.3 11.7 %all-to-all-start = ((bf16[32,24,768]{2,1,0:T(8,128)(2,1)}), bf16[32,24,768]{2,1,0:T(8,128)(2,1)S(1)}, u32[]{:S(2)}, u32[]{:S(2)}) async-start(bf16[32,24,768]{2,1,0:T(8,128)(2,1)} %bitcast.2), calls=%async_computation | async-start | bytes 2359296 | tf_op jit(solution)/shard_map/all_to_all | solution.py:251
  119.7 28.1 %all-to-all-done = bf16[32,24,768]{2,1,0:T(8,128)(2,1)S(1)} async-done(((bf16[32,24,768]{2,1,0:T(8,128)(2,1)}), bf16[32,24,768]{2,1,0:T(8,128)(2,1)S(1)}, u32[]{:S(2)}, u32[]{:S(2)}) %all-to-all-start) | async-done | bytes 1179680 | tf_op jit(solution)/shard_map/all_to_all | solution.py:251
  (97 shorter events, 22.3 us)
Async XLA Ops:
  0.6 11.9 %copy-start = (bf16[128,1536]{1,0:T(8,128)(2,1)S(1)}, bf16[128,1536]{1,0:T(8,128)(2,1)}, u32[]{:S(2)}) copy-start(bf16[128,1536]{1,0:T(8,128)(2,1)} %param.6) | copy-start | bytes 1179652
  0.6 12.1 %copy-start.18 = (s32[128]{0:T(128)S(1)}, s32[128]{0:T(128)}, u32[]{:S(2)}) copy-start(s32[128]{0:T(128)} %param.9) | copy-start | bytes 1540
  1.9 12.5 %copy-start.2 = (bf16[2048,384]{1,0:T(8,128)(2,1)S(1)}, bf16[2048,384]{1,0:T(8,128)(2,1)}, u32[]{:S(2)}) copy-start(bf16[2048,384]{1,0:T(8,128)(2,1)} %param.8) | copy-start | bytes 4718596
  3.1 26.2 %collective-permute-start = (bf16[128,1536]{1,0:T(8,128)(2,1)S(1)}, bf16[128,1536]{1,0:T(8,128)(2,1)}, u32[]{:S(2)}, u32[]{:S(2)}) collective-permute-start(bf16[128,1536]{1,0:T(8,128)(2,1)S(1)} %fusion.43), channel_id=1, source_target_pairs={{0,32},{1,33},{2,34},{3,35},{4,36},{5,37},{6,38},{7,39},{8,40},{9,... | collective-permute-start | bytes 1179656 | tf_op jit(solution)/shard_map/ppermute | solution.py:29
  7.1 30.7 %collective-permute-start.2 = (bf16[128,1536]{1,0:T(8,128)(2,1)S(1)}, bf16[128,1536]{1,0:T(8,128)(2,1)S(1)}, u32[]{:S(2)}, u32[]{:S(2)}) collective-permute-start(bf16[128,1536]{1,0:T(8,128)(2,1)S(1)} %fusion.43), channel_id=1, source_target_pairs={{0,16},{1,17},{2,18},{3,19},{4,20},{5,21},{6,22},{7,23},{8,24},{9,... | collective-permute-start | bytes 1179656 | tf_op jit(solution)/shard_map/ppermute | solution.py:29
  17.6 16.9 %copy-start.19 = (s32[128]{0:T(128)S(1)}, s32[128]{0:T(128)}, u32[]{:S(2)}) copy-start(s32[128]{0:T(128)} %param.9) | copy-start | bytes 1540
  19.2 24.6 %collective-permute-start.4 = (bf16[1024,384]{1,0:T(8,128)(2,1)S(1)}, bf16[1024,384]{1,0:T(8,128)(2,1)}, u32[]{:S(2)}, u32[]{:S(2)}) collective-permute-start(bf16[1024,384]{1,0:T(8,128)(2,1)S(1)} %fusion.66), channel_id=1, source_target_pairs={{0,8},{1,9},{2,10},{3,11},{4,12},{5,13},{6,14},{7,15},{8,0},{9,1},... | collective-permute-start | bytes 2359304 | tf_op jit(solution)/shard_map/ppermute | solution.py:29
  29.3 7.9 %collective-permute-start.3 = (bf16[128,1536]{1,0:T(8,128)(2,1)}, bf16[128,1536]{1,0:T(8,128)(2,1)S(1)}, u32[]{:S(2)}, u32[]{:S(2)}) collective-permute-start(bf16[128,1536]{1,0:T(8,128)(2,1)} %collective-permute-done), channel_id=1, source_target_pairs={{0,16},{1,17},{2,18},{3,19},{4,20},{5,21},{6,22},{7,23},{8,24},{9,... | collective-permute-start | bytes 1179656 | tf_op jit(solution)/shard_map/ppermute | solution.py:29
  33.3 6.3 %collective-permute-start.1 = (bf16[128,1536]{1,0:T(8,128)(2,1)}, bf16[128,1536]{1,0:T(8,128)(2,1)S(1)}, u32[]{:S(2)}, u32[]{:S(2)}) collective-permute-start(bf16[128,1536]{1,0:T(8,128)(2,1)} %collective-permute-done), channel_id=1, source_target_pairs={{16,32},{17,33},{18,34},{19,35},{20,36},{21,37},{22,38},{23,39},{2... | collective-permute-start | bytes 1179656 | tf_op jit(solution)/shard_map/ppermute | solution.py:29
  40.6 13.2 %collective-permute-start.12 = (bf16[128,1536]{1,0:T(8,128)(2,1)S(1)}, bf16[128,1536]{1,0:T(8,128)(2,1)S(1)}, u32[]{:S(2)}, u32[]{:S(2)}) collective-permute-start(bf16[128,1536]{1,0:T(8,128)(2,1)S(1)} %fusion.50.rest_0_.rest_8_), channel_id=1, source_target_pairs={{0,1},{1,2},{2,3},{3,4},{4,5},{5,6},{6,7},{7,0},{8,9},{9,10},{10,1... | collective-permute-start | bytes 1179656 | tf_op jit(solution)/shard_map/ppermute | solution.py:29
  45.1 10.7 %collective-permute-start.5 = (bf16[128,1536]{1,0:T(8,128)(2,1)S(1)}, bf16[128,1536]{1,0:T(8,128)(2,1)S(1)}, u32[]{:S(2)}, u32[]{:S(2)}) collective-permute-start(bf16[128,1536]{1,0:T(8,128)(2,1)S(1)} %fusion.2), channel_id=1, source_target_pairs={{0,16},{1,17},{2,18},{3,19},{4,20},{5,21},{6,22},{7,23},{8,24},{9,... | collective-permute-start | bytes 1179656 | tf_op jit(solution)/shard_map/ppermute | solution.py:29
  47.0 17.3 %collective-permute-start.9 = (bf16[128,1536]{1,0:T(8,128)(2,1)S(1)}, bf16[128,1536]{1,0:T(8,128)(2,1)S(1)}, u32[]{:S(2)}, u32[]{:S(2)}) collective-permute-start(bf16[128,1536]{1,0:T(8,128)(2,1)S(1)} %fusion.50.rest_0_.rest_8_), channel_id=1, source_target_pairs={{0,7},{1,0},{2,1},{3,2},{4,3},{5,4},{6,5},{7,6},{8,15},{9,8},{10,9... | collective-permute-start | bytes 1179656 | tf_op jit(solution)/shard_map/ppermute | solution.py:29
  51.2 19.7 %collective-permute-start.7 = (bf16[128,1536]{1,0:T(8,128)(2,1)S(1)}, bf16[128,1536]{1,0:T(8,128)(2,1)S(1)}, u32[]{:S(2)}, u32[]{:S(2)}) collective-permute-start(bf16[128,1536]{1,0:T(8,128)(2,1)S(1)} %fusion.3), channel_id=1, source_target_pairs={{0,80},{1,81},{2,82},{3,83},{4,84},{5,85},{6,86},{7,87},{8,88},{9,... | collective-permute-start | bytes 1179656 | tf_op jit(solution)/shard_map/ppermute | solution.py:29
  53.9 15.1 %collective-permute-start.13 = (bf16[128,1536]{1,0:T(8,128)(2,1)S(1)}, bf16[128,1536]{1,0:T(8,128)(2,1)S(1)}, u32[]{:S(2)}, u32[]{:S(2)}) collective-permute-start(bf16[128,1536]{1,0:T(8,128)(2,1)S(1)} %collective-permute-done.12.rest_7_.rest_15_), channel_id=1, source_target_pairs={{0,1},{1,2},{2,3},{3,4},{4,5},{5,6},{6,7},{7,0},{8,9},{9,10},{10,1... | collective-permute-start | bytes 1179656 | tf_op jit(solution)/shard_map/ppermute | solution.py:29
  56.2 19.2 %collective-permute-start.6 = (bf16[128,1536]{1,0:T(8,128)(2,1)S(1)}, bf16[128,1536]{1,0:T(8,128)(2,1)S(1)}, u32[]{:S(2)}, u32[]{:S(2)}) collective-permute-start(bf16[128,1536]{1,0:T(8,128)(2,1)S(1)} %add_convert_fusion.1), channel_id=1, source_target_pairs={{0,96},{1,97},{2,98},{3,99},{4,100},{5,101},{6,102},{7,103},{8,104... | collective-permute-start | bytes 1179656 | tf_op jit(solution)/shard_map/ppermute | solution.py:29
  64.4 12.5 %collective-permute-start.10 = (bf16[128,1536]{1,0:T(8,128)(2,1)S(1)}, bf16[128,1536]{1,0:T(8,128)(2,1)S(1)}, u32[]{:S(2)}, u32[]{:S(2)}) collective-permute-start(bf16[128,1536]{1,0:T(8,128)(2,1)S(1)} %collective-permute-done.9.rest_1_.rest_9_), channel_id=1, source_target_pairs={{0,7},{1,0},{2,1},{3,2},{4,3},{5,4},{6,5},{7,6},{8,15},{9,8},{10,9... | collective-permute-start | bytes 1179656 | tf_op jit(solution)/shard_map/ppermute | solution.py:29
  69.0 13.2 %collective-permute-start.14 = (bf16[128,1536]{1,0:T(8,128)(2,1)S(1)}, bf16[128,1536]{1,0:T(8,128)(2,1)S(1)}, u32[]{:S(2)}, u32[]{:S(2)}) collective-permute-start(bf16[128,1536]{1,0:T(8,128)(2,1)S(1)} %collective-permute-done.13.rest_6_.rest_14_), channel_id=1, source_target_pairs={{0,1},{1,2},{2,3},{3,4},{4,5},{5,6},{6,7},{7,0},{8,9},{9,10},{10,1... | collective-permute-start | bytes 1179656 | tf_op jit(solution)/shard_map/ppermute | solution.py:29
  75.5 11.3 %collective-permute-start.8 = (bf16[128,1536]{1,0:T(8,128)(2,1)S(1)}, bf16[128,1536]{1,0:T(8,128)(2,1)S(1)}, u32[]{:S(2)}, u32[]{:S(2)}) collective-permute-start(bf16[128,1536]{1,0:T(8,128)(2,1)S(1)} %fusion.61), channel_id=1, source_target_pairs={{80,464},{81,465},{82,466},{83,467},{84,468},{85,469},{86,470},{87... | collective-permute-start | bytes 1179656 | tf_op jit(solution)/shard_map/ppermute | solution.py:29
  76.8 12.3 %collective-permute-start.11 = (bf16[128,1536]{1,0:T(8,128)(2,1)S(1)}, bf16[128,1536]{1,0:T(8,128)(2,1)S(1)}, u32[]{:S(2)}, u32[]{:S(2)}) collective-permute-start(bf16[128,1536]{1,0:T(8,128)(2,1)S(1)} %collective-permute-done.10.rest_2_.rest_10_), channel_id=1, source_target_pairs={{0,7},{1,0},{2,1},{3,2},{4,3},{5,4},{6,5},{7,6},{8,15},{9,8},{10,9... | collective-permute-start | bytes 1179656 | tf_op jit(solution)/shard_map/ppermute | solution.py:29
  82.2 12.0 %collective-permute-start.15 = (bf16[128,1536]{1,0:T(8,128)(2,1)S(1)}, bf16[128,1536]{1,0:T(8,128)(2,1)S(1)}, u32[]{:S(2)}, u32[]{:S(2)}) collective-permute-start(bf16[128,1536]{1,0:T(8,128)(2,1)S(1)} %collective-permute-done.14.rest_5_.rest_13_), channel_id=1, source_target_pairs={{0,1},{1,2},{2,3},{3,4},{4,5},{5,6},{6,7},{7,0},{8,9},{9,10},{10,1... | collective-permute-start | bytes 1179656 | tf_op jit(solution)/shard_map/ppermute | solution.py:29
  98.0 7.0 %collective-permute-start.16 = (bf16[768,768]{1,0:T(8,128)(2,1)S(1)}, bf16[768,768]{1,0:T(8,128)(2,1)S(1)}, u32[]{:S(2)}, u32[]{:S(2)}) collective-permute-start(bf16[768,768]{1,0:T(8,128)(2,1)S(1)} %get-tuple-element.6), channel_id=1, source_target_pairs={{0,16},{1,17},{2,18},{3,19},{4,20},{5,21},{6,22},{7,23},{8,24},{9,... | collective-permute-start | bytes 3538952 | tf_op jit(solution)/shard_map/ppermute | solution.py:29
  106.3 11.8 %copy-start.5 = (bf16[128,128]{1,0:T(8,128)(2,1)S(1)}, bf16[128,128]{1,0:T(8,128)(2,1)}, u32[]{:S(2)}) copy-start(bf16[128,128]{1,0:T(8,128)(2,1)} %copy-done.3) | copy-start | bytes 98308
  106.3 11.8 %copy-start.13 = (f32[128]{0:T(128)S(1)}, f32[128]{0:T(128)}, u32[]{:S(2)}) copy-start(f32[128]{0:T(128)} %copy-done.12) | copy-start | bytes 1540
  106.3 41.5 %all-to-all-start = ((bf16[32,24,768]{2,1,0:T(8,128)(2,1)}), bf16[32,24,768]{2,1,0:T(8,128)(2,1)S(1)}, u32[]{:S(2)}, u32[]{:S(2)}) async-start(bf16[32,24,768]{2,1,0:T(8,128)(2,1)} %bitcast.2), calls=%async_computation | async-start | bytes 2359296 | tf_op jit(solution)/shard_map/all_to_all | solution.py:251
  (15 other events, 53.0 us)

commit v5 on v4

--- a/solution.py
+++ b/solution.py
@@ -197,11 +197,14 @@
 
     def all_units(before):
         units_first = (((0,), (1,)), ((), ()))
-        own = in_ring_order(first) + zero_of(before).astype(bf16)
-        mixed = lax.dot_general(pick[0], own, units_first, preferred_element_type=bf16)
-        other = moved(in_ring_order(~first) + zero_of(mixed).astype(bf16), other_z_lo)
-        mixed += lax.dot_general(pick[1], other, units_first, preferred_element_type=bf16)
-        return mixed, other
+        ordered = zero_of(before).astype(bf16)
+        other = moved(in_ring_order(~first) + ordered, other_z_lo)
+        own = lax.dot_general(
+            pick[0], in_ring_order(first) + ordered, units_first, preferred_element_type=bf16
+        )
+        return own, other, own + lax.dot_general(
+            pick[1], other, units_first, preferred_element_type=bf16
+        )
 
     image_total = jnp.zeros(img_emb.shape, jnp.float32)
     coefficients = []
@@ -212,8 +215,10 @@
         image_part, coefficient = pair_terms(image_low, text_block, positives, first_col)
         image_total = image_total + image_part
         coefficients.append(coefficient)
-    hidden_units, early = all_units(coefficients[0])
-    image_grad = backward_norm(image_unit, image_inv, image_total).astype(bf16)
+    own_units, early, hidden_units = all_units(coefficients[0])
+    image_grad = backward_norm(
+        image_unit, image_inv + zeros_of(own_units, rows), image_total
+    ).astype(bf16)
 
     block = image_grad
     got = [block] + [None] * (Y - 1)

time: 150 us -> 150 us (level)
  starting transfers between devices: 70.8 us -> 65.3 us
  matrix products: 10.7 us -> 13.9 us
    ppermute x17, starting transfers between devices: 59 us -> 56.1 us  [moved(): return lax.ppermute(value, ('loop', 'mp'), pairs)]
    all_to_all x1, starting transfers between devices: 11.7 us -> 9.18 us  [local(): lax.all_to_all(total.astype(bf16).reshape(places, 2 * share, width // 2),...]
  transfers between devices with their start and end apart: 18 -> 18, of which waited for: 8 -> 8; matrix products, arithmetic and copies ran while one was open for 11% -> 14% of each run, Pallas kernels for 0% -> 0%
where the time goes in v5:
time: 150 us; the launch traced here: 148 us
  starting transfers between devices  65.3 us (44%)
  waiting for transfers between devices  51.5 us (34%)
  matrix products  13.9 us (9%)
  other arithmetic  9.62 us (6%)
  Pallas kernels  3.82 us (3%)
  between operations  2.22 us (1%)
  local copies, waits for them, and re-layouts  1.81 us (1%)
    ppermute x17, starting transfers between devices, moved(): return lax.ppermute(value, ('loop', 'mp'), pairs)  56.1 us
    all_to_all x1, waiting for transfers between devices, local(): lax.all_to_all(total.astype(bf16).reshape(places, 2 * share, width // 2),...  28.1 us
    ppermute x17, waiting for transfers between devices, moved(): return lax.ppermute(value, ('loop', 'mp'), pairs)  23.4 us
    all_to_all x1, starting transfers between devices, local(): lax.all_to_all(total.astype(bf16).reshape(places, 2 * share, width // 2),...  9.18 us
    unnamed x2, matrix products  5.71 us
    pallas_call x1, Pallas kernels, weight_product(): pl.pallas_call(kernel, grid=(steps,), in_specs=[pl.BlockSpec((units, dept...  3.82 us
    dot_general x4, matrix products, pair_terms(): lax.dot_general(image_low, text_low, (((1,), (1,)), ((), ())), preferred_...  3.39 us
    dot_general x4, matrix products, pair_terms(): jnp.dot(coefficient, text_low, preferred_element_type=jnp.float32)  3.15 us
  transfers between devices with their start and end apart: 18, of which 8 were waited for; matrix products, arithmetic and copies ran while one was open for 14% of the time, Pallas kernels for 0%

profile of v5, /device:TPU:1, one launch (start us, length us, event | category | flops | bytes accessed | tf_op | source)
XLA Modules:
  0.0 148.1 jit_solution(6585337629529922600)
XLA Ops:
  3.1 4.0 %collective-permute-start = (bf16[128,1536]{1,0:T(8,128)(2,1)S(1)}, bf16[128,1536]{1,0:T(8,128)(2,1)}, u32[]{:S(2)}, u32[]{:S(2)}) collective-permute-start(bf16[128,1536]{1,0:T(8,128)(2,1)S(1)} %fusion.43), channel_id=1, source_target_pairs={{0,32},{1,33},{2,34},{3,35},{4,36},{5,37},{6,38},{7,39},{8,40},{9,... | collective-permute-start | bytes 1179656 | tf_op jit(solution)/shard_map/ppermute | solution.py:29
  7.1 5.2 %collective-permute-start.2 = (bf16[128,1536]{1,0:T(8,128)(2,1)S(1)}, bf16[128,1536]{1,0:T(8,128)(2,1)}, u32[]{:S(2)}, u32[]{:S(2)}) collective-permute-start(bf16[128,1536]{1,0:T(8,128)(2,1)S(1)} %fusion.43), channel_id=1, source_target_pairs={{0,16},{1,17},{2,18},{3,19},{4,20},{5,21},{6,22},{7,23},{8,24},{9,... | collective-permute-start | bytes 1179656 | tf_op jit(solution)/shard_map/ppermute | solution.py:29
  16.8 4.0 %collective-permute-start.4 = (bf16[1024,384]{1,0:T(8,128)(2,1)S(1)}, bf16[1024,384]{1,0:T(8,128)(2,1)}, u32[]{:S(2)}, u32[]{:S(2)}) collective-permute-start(bf16[1024,384]{1,0:T(8,128)(2,1)S(1)} %fusion.63), channel_id=1, source_target_pairs={{0,8},{1,9},{2,10},{3,11},{4,12},{5,13},{6,14},{7,15},{8,0},{9,1},... | collective-permute-start | bytes 2359304 | tf_op jit(solution)/shard_map/ppermute | solution.py:29
  21.1 3.0 %convolution_convert_fusion.1 = bf16[768,1024]{1,0:T(8,128)(2,1)} fusion(s32[]{:T(128)S(6)} %select_n.156, bf16[1024,384]{1,0:T(8,128)(2,1)S(1)} %copy-done.3, s32[]{:T(128)S(6)} %select_n.143, s32[768]{0:T(1024)S(1)} %get-tuple-element.23, s32[768]{0:T(1024)S(1)} %get-tuple-element.26, pred[768]{0:T(1024)(128)(4,1)S(1)} %get-tuple-element.19, ...), kind=kOutput, calls=%fused_computation.26 | convolution fusion | flops 620691456 | bytes 2386958
  25.4 3.9 %collective-permute-done = bf16[128,1536]{1,0:T(8,128)(2,1)} collective-permute-done((bf16[128,1536]{1,0:T(8,128)(2,1)S(1)}, bf16[128,1536]{1,0:T(8,128)(2,1)}, u32[]{:S(2)}, u32[]{:S(2)}) %collective-permute-start) | collective-permute-done | bytes 393248 | tf_op jit(solution)/shard_map/ppermute | solution.py:29
  29.3 5.9 %collective-permute-start.3 = (bf16[128,1536]{1,0:T(8,128)(2,1)}, bf16[128,1536]{1,0:T(8,128)(2,1)S(1)}, u32[]{:S(2)}, u32[]{:S(2)}) collective-permute-start(bf16[128,1536]{1,0:T(8,128)(2,1)} %collective-permute-done), channel_id=1, source_target_pairs={{0,16},{1,17},{2,18},{3,19},{4,20},{5,21},{6,22},{7,23},{8,24},{9,... | collective-permute-start | bytes 1179656 | tf_op jit(solution)/shard_map/ppermute | solution.py:29
  44.7 2.2 %collective-permute-start.12 = (bf16[128,1536]{1,0:T(8,128)(2,1)S(1)}, bf16[128,1536]{1,0:T(8,128)(2,1)S(1)}, u32[]{:S(2)}, u32[]{:S(2)}) collective-permute-start(bf16[128,1536]{1,0:T(8,128)(2,1)S(1)} %fusion.50.rest_0_.rest_8_), channel_id=1, source_target_pairs={{0,1},{1,2},{2,3},{3,4},{4,5},{5,6},{6,7},{7,0},{8,9},{9,10},{10,1... | collective-permute-start | bytes 1179656 | tf_op jit(solution)/shard_map/ppermute | solution.py:29
  48.2 1.9 %collective-permute-start.5 = (bf16[128,1536]{1,0:T(8,128)(2,1)S(1)}, bf16[128,1536]{1,0:T(8,128)(2,1)S(1)}, u32[]{:S(2)}, u32[]{:S(2)}) collective-permute-start(bf16[128,1536]{1,0:T(8,128)(2,1)S(1)} %fusion.2), channel_id=1, source_target_pairs={{0,16},{1,17},{2,18},{3,19},{4,20},{5,21},{6,22},{7,23},{8,24},{9,... | collective-permute-start | bytes 1179656 | tf_op jit(solution)/shard_map/ppermute | solution.py:29
  50.1 4.3 %collective-permute-start.9 = (bf16[128,1536]{1,0:T(8,128)(2,1)S(1)}, bf16[128,1536]{1,0:T(8,128)(2,1)S(1)}, u32[]{:S(2)}, u32[]{:S(2)}) collective-permute-start(bf16[128,1536]{1,0:T(8,128)(2,1)S(1)} %fusion.50.rest_0_.rest_8_), channel_id=1, source_target_pairs={{0,7},{1,0},{2,1},{3,2},{4,3},{5,4},{6,5},{7,6},{8,15},{9,8},{10,9... | collective-permute-start | bytes 1179656 | tf_op jit(solution)/shard_map/ppermute | solution.py:29
  54.7 2.7 %collective-permute-start.7 = (bf16[128,1536]{1,0:T(8,128)(2,1)S(1)}, bf16[128,1536]{1,0:T(8,128)(2,1)S(1)}, u32[]{:S(2)}, u32[]{:S(2)}) collective-permute-start(bf16[128,1536]{1,0:T(8,128)(2,1)S(1)} %fusion.3), channel_id=1, source_target_pairs={{0,80},{1,81},{2,82},{3,83},{4,84},{5,85},{6,86},{7,87},{8,88},{9,... | collective-permute-start | bytes 1179656 | tf_op jit(solution)/shard_map/ppermute | solution.py:29
  57.4 1.9 %collective-permute-start.13 = (bf16[128,1536]{1,0:T(8,128)(2,1)S(1)}, bf16[128,1536]{1,0:T(8,128)(2,1)S(1)}, u32[]{:S(2)}, u32[]{:S(2)}) collective-permute-start(bf16[128,1536]{1,0:T(8,128)(2,1)S(1)} %collective-permute-done.12.rest_7_.rest_15_), channel_id=1, source_target_pairs={{0,1},{1,2},{2,3},{3,4},{4,5},{5,6},{6,7},{7,0},{8,9},{9,10},{10,1... | collective-permute-start | bytes 1179656 | tf_op jit(solution)/shard_map/ppermute | solution.py:29
  59.7 3.8 %collective-permute-start.6 = (bf16[128,1536]{1,0:T(8,128)(2,1)S(1)}, bf16[128,1536]{1,0:T(8,128)(2,1)S(1)}, u32[]{:S(2)}, u32[]{:S(2)}) collective-permute-start(bf16[128,1536]{1,0:T(8,128)(2,1)S(1)} %add_convert_fusion.1), channel_id=1, source_target_pairs={{0,96},{1,97},{2,98},{3,99},{4,100},{5,101},{6,102},{7,103},{8,104... | collective-permute-start | bytes 1179656 | tf_op jit(solution)/shard_map/ppermute | solution.py:29
  63.5 4.6 %collective-permute-start.10 = (bf16[128,1536]{1,0:T(8,128)(2,1)S(1)}, bf16[128,1536]{1,0:T(8,128)(2,1)S(1)}, u32[]{:S(2)}, u32[]{:S(2)}) collective-permute-start(bf16[128,1536]{1,0:T(8,128)(2,1)S(1)} %collective-permute-done.9.rest_1_.rest_9_), channel_id=1, source_target_pairs={{0,7},{1,0},{2,1},{3,2},{4,3},{5,4},{6,5},{7,6},{8,15},{9,8},{10,9... | collective-permute-start | bytes 1179656 | tf_op jit(solution)/shard_map/ppermute | solution.py:29
  68.1 3.1 %collective-permute-done.13.rest_6_.rest_14_ = bf16[128,1536]{1,0:T(8,128)(2,1)S(1)} collective-permute-done((bf16[128,1536]{1,0:T(8,128)(2,1)S(1)}, bf16[128,1536]{1,0:T(8,128)(2,1)S(1)}, u32[]{:S(2)}, u32[]{:S(2)}) %collective-permute-start.13) | collective-permute-done | bytes 393248 | tf_op jit(solution)/shard_map/ppermute | solution.py:29
  75.1 5.3 %collective-permute-start.11 = (bf16[128,1536]{1,0:T(8,128)(2,1)S(1)}, bf16[128,1536]{1,0:T(8,128)(2,1)S(1)}, u32[]{:S(2)}, u32[]{:S(2)}) collective-permute-start(bf16[128,1536]{1,0:T(8,128)(2,1)S(1)} %collective-permute-done.10.rest_2_.rest_10_), channel_id=1, source_target_pairs={{0,7},{1,0},{2,1},{3,2},{4,3},{5,4},{6,5},{7,6},{8,15},{9,8},{10,9... | collective-permute-start | bytes 1179656 | tf_op jit(solution)/shard_map/ppermute | solution.py:29
  80.4 3.8 %collective-permute-done.14.rest_5_.rest_13_ = bf16[128,1536]{1,0:T(8,128)(2,1)S(1)} collective-permute-done((bf16[128,1536]{1,0:T(8,128)(2,1)S(1)}, bf16[128,1536]{1,0:T(8,128)(2,1)S(1)}, u32[]{:S(2)}, u32[]{:S(2)}) %collective-permute-start.14) | collective-permute-done | bytes 393248 | tf_op jit(solution)/shard_map/ppermute | solution.py:29
  84.2 1.9 %collective-permute-start.15 = (bf16[128,1536]{1,0:T(8,128)(2,1)S(1)}, bf16[128,1536]{1,0:T(8,128)(2,1)S(1)}, u32[]{:S(2)}, u32[]{:S(2)}) collective-permute-start(bf16[128,1536]{1,0:T(8,128)(2,1)S(1)} %collective-permute-done.14.rest_5_.rest_13_), channel_id=1, source_target_pairs={{0,1},{1,2},{2,3},{3,4},{4,5},{5,6},{6,7},{7,0},{8,9},{9,10},{10,1... | collective-permute-start | bytes 1179656 | tf_op jit(solution)/shard_map/ppermute | solution.py:29
  86.1 2.8 %fusion.4.hidden_ref = bf16[768,1024]{1,0:T(8,128)(2,1)S(1)} fusion(bf16[768,1024]{1,0:T(8,128)(2,1)} %convolution_convert_fusion.1, bf16[1024,384]{1,0:T(8,128)(2,1)} %collective-permute-done.4, s32[]{:T(128)S(6)} %select_n.143, s32[768]{0:T(1024)S(1)} %get-tuple-element.23, s32[768]{0:T(1024)} %copy-done.7, pred[768]{0:T(1024)(128)(4,1)} %copy-done.14, ...), kind=kOutput, calls=%fused_computation.31 | convolution fusion | flops 619118592 | bytes 3959816
  88.9 7.3 %collective-permute-done.15.rest_4_.rest_12_ = bf16[128,1536]{1,0:T(8,128)(2,1)S(1)} collective-permute-done((bf16[128,1536]{1,0:T(8,128)(2,1)S(1)}, bf16[128,1536]{1,0:T(8,128)(2,1)S(1)}, u32[]{:S(2)}, u32[]{:S(2)}) %collective-permute-start.15) | collective-permute-done | bytes 393248 | tf_op jit(solution)/shard_map/ppermute | solution.py:29
  96.2 3.8 %shard_map.59 = (f32[768,768]{1,0:T(8,128)S(1)}, bf16[768,768]{1,0:T(8,128)(2,1)S(1)}) custom-call(bf16[768,1024]{1,0:T(8,128)(2,1)S(1)} %fusion.4.hidden_ref, bf16[128,1536]{1,0:T(8,128)(2,1)S(1)} %fusion.50.rest_0_.rest_8_, bf16[128,1536]{1,0:T(8,128)(2,1)S(1)} %collective-permute-done.9.rest_1_.rest_9_, ...), custom_call_target="tpu_custom_call" | custom-call | flops 2415919104 | bytes 12582912 | tf_op jit(solution)/shard_map/pallas_call | solution.py:140
  100.1 4.5 %collective-permute-start.16 = (bf16[768,768]{1,0:T(8,128)(2,1)S(1)}, bf16[768,768]{1,0:T(8,128)(2,1)S(1)}, u32[]{:S(2)}, u32[]{:S(2)}) collective-permute-start(bf16[768,768]{1,0:T(8,128)(2,1)S(1)} %get-tuple-element.6), channel_id=1, source_target_pairs={{0,16},{1,17},{2,18},{3,19},{4,20},{5,21},{6,22},{7,23},{8,24},{9,... | collective-permute-start | bytes 3538952 | tf_op jit(solution)/shard_map/ppermute | solution.py:29
  104.6 2.5 %collective-permute-done.16 = bf16[768,768]{1,0:T(8,128)(2,1)S(1)} collective-permute-done((bf16[768,768]{1,0:T(8,128)(2,1)S(1)}, bf16[768,768]{1,0:T(8,128)(2,1)S(1)}, u32[]{:S(2)}, u32[]{:S(2)}) %collective-permute-start.16) | collective-permute-done | bytes 1179680 | tf_op jit(solution)/shard_map/ppermute | solution.py:29
  108.3 9.2 %all-to-all-start = ((bf16[32,24,768]{2,1,0:T(8,128)(2,1)}), bf16[32,24,768]{2,1,0:T(8,128)(2,1)S(1)}, u32[]{:S(2)}, u32[]{:S(2)}) async-start(bf16[32,24,768]{2,1,0:T(8,128)(2,1)} %bitcast.2), calls=%async_computation | async-start | bytes 2359296 | tf_op jit(solution)/shard_map/all_to_all | solution.py:256
  119.2 28.1 %all-to-all-done = bf16[32,24,768]{2,1,0:T(8,128)(2,1)S(1)} async-done(((bf16[32,24,768]{2,1,0:T(8,128)(2,1)}), bf16[32,24,768]{2,1,0:T(8,128)(2,1)S(1)}, u32[]{:S(2)}, u32[]{:S(2)}) %all-to-all-start) | async-done | bytes 1179680 | tf_op jit(solution)/shard_map/all_to_all | solution.py:256
  (96 shorter events, 26.2 us)
Async XLA Ops:
  0.6 11.7 %copy-start = (bf16[128,1536]{1,0:T(8,128)(2,1)S(1)}, bf16[128,1536]{1,0:T(8,128)(2,1)}, u32[]{:S(2)}) copy-start(bf16[128,1536]{1,0:T(8,128)(2,1)} %param.6) | copy-start | bytes 1179652
  0.6 11.9 %copy-start.18 = (s32[128]{0:T(128)S(1)}, s32[128]{0:T(128)}, u32[]{:S(2)}) copy-start(s32[128]{0:T(128)} %param.9) | copy-start | bytes 1540
  1.9 10.7 %copy-start.12 = (f32[128]{0:T(128)}, f32[128]{0:T(128)S(1)}, u32[]{:S(2)}) copy-start(f32[128]{0:T(128)S(1)} %add_rsqrt_fusion) | copy-start | bytes 1540
  1.9 12.3 %copy-start.2 = (bf16[2048,384]{1,0:T(8,128)(2,1)S(1)}, bf16[2048,384]{1,0:T(8,128)(2,1)}, u32[]{:S(2)}) copy-start(bf16[2048,384]{1,0:T(8,128)(2,1)} %param.8) | copy-start | bytes 4718596
  3.1 26.2 %collective-permute-start = (bf16[128,1536]{1,0:T(8,128)(2,1)S(1)}, bf16[128,1536]{1,0:T(8,128)(2,1)}, u32[]{:S(2)}, u32[]{:S(2)}) collective-permute-start(bf16[128,1536]{1,0:T(8,128)(2,1)S(1)} %fusion.43), channel_id=1, source_target_pairs={{0,32},{1,33},{2,34},{3,35},{4,36},{5,37},{6,38},{7,39},{8,40},{9,... | collective-permute-start | bytes 1179656 | tf_op jit(solution)/shard_map/ppermute | solution.py:29
  7.1 32.8 %collective-permute-start.2 = (bf16[128,1536]{1,0:T(8,128)(2,1)S(1)}, bf16[128,1536]{1,0:T(8,128)(2,1)}, u32[]{:S(2)}, u32[]{:S(2)}) collective-permute-start(bf16[128,1536]{1,0:T(8,128)(2,1)S(1)} %fusion.43), channel_id=1, source_target_pairs={{0,16},{1,17},{2,18},{3,19},{4,20},{5,21},{6,22},{7,23},{8,24},{9,... | collective-permute-start | bytes 1179656 | tf_op jit(solution)/shard_map/ppermute | solution.py:29
  12.9 12.2 %copy-start.4 = (bf16[128,128]{1,0:T(8,128)(2,1)}, bf16[128,128]{1,0:T(8,128)(2,1)S(1)}, u32[]{:S(2)}) copy-start(bf16[128,128]{1,0:T(8,128)(2,1)S(1)} %fusion.37) | copy-start | bytes 98308
  16.8 30.2 %collective-permute-start.4 = (bf16[1024,384]{1,0:T(8,128)(2,1)S(1)}, bf16[1024,384]{1,0:T(8,128)(2,1)}, u32[]{:S(2)}, u32[]{:S(2)}) collective-permute-start(bf16[1024,384]{1,0:T(8,128)(2,1)S(1)} %fusion.63), channel_id=1, source_target_pairs={{0,8},{1,9},{2,10},{3,11},{4,12},{5,13},{6,14},{7,15},{8,0},{9,1},... | collective-permute-start | bytes 2359304 | tf_op jit(solution)/shard_map/ppermute | solution.py:29
  29.3 9.9 %collective-permute-start.3 = (bf16[128,1536]{1,0:T(8,128)(2,1)}, bf16[128,1536]{1,0:T(8,128)(2,1)S(1)}, u32[]{:S(2)}, u32[]{:S(2)}) collective-permute-start(bf16[128,1536]{1,0:T(8,128)(2,1)} %collective-permute-done), channel_id=1, source_target_pairs={{0,16},{1,17},{2,18},{3,19},{4,20},{5,21},{6,22},{7,23},{8,24},{9,... | collective-permute-start | bytes 1179656 | tf_op jit(solution)/shard_map/ppermute | solution.py:29
  35.3 6.3 %collective-permute-start.1 = (bf16[128,1536]{1,0:T(8,128)(2,1)}, bf16[128,1536]{1,0:T(8,128)(2,1)S(1)}, u32[]{:S(2)}, u32[]{:S(2)}) collective-permute-start(bf16[128,1536]{1,0:T(8,128)(2,1)} %collective-permute-done), channel_id=1, source_target_pairs={{16,32},{17,33},{18,34},{19,35},{20,36},{21,37},{22,38},{23,39},{2... | collective-permute-start | bytes 1179656 | tf_op jit(solution)/shard_map/ppermute | solution.py:29
  44.7 12.7 %collective-permute-start.12 = (bf16[128,1536]{1,0:T(8,128)(2,1)S(1)}, bf16[128,1536]{1,0:T(8,128)(2,1)S(1)}, u32[]{:S(2)}, u32[]{:S(2)}) collective-permute-start(bf16[128,1536]{1,0:T(8,128)(2,1)S(1)} %fusion.50.rest_0_.rest_8_), channel_id=1, source_target_pairs={{0,1},{1,2},{2,3},{3,4},{4,5},{5,6},{6,7},{7,0},{8,9},{9,10},{10,1... | collective-permute-start | bytes 1179656 | tf_op jit(solution)/shard_map/ppermute | solution.py:29
  48.2 11.2 %collective-permute-start.5 = (bf16[128,1536]{1,0:T(8,128)(2,1)S(1)}, bf16[128,1536]{1,0:T(8,128)(2,1)S(1)}, u32[]{:S(2)}, u32[]{:S(2)}) collective-permute-start(bf16[128,1536]{1,0:T(8,128)(2,1)S(1)} %fusion.2), channel_id=1, source_target_pairs={{0,16},{1,17},{2,18},{3,19},{4,20},{5,21},{6,22},{7,23},{8,24},{9,... | collective-permute-start | bytes 1179656 | tf_op jit(solution)/shard_map/ppermute | solution.py:29
  50.1 13.4 %collective-permute-start.9 = (bf16[128,1536]{1,0:T(8,128)(2,1)S(1)}, bf16[128,1536]{1,0:T(8,128)(2,1)S(1)}, u32[]{:S(2)}, u32[]{:S(2)}) collective-permute-start(bf16[128,1536]{1,0:T(8,128)(2,1)S(1)} %fusion.50.rest_0_.rest_8_), channel_id=1, source_target_pairs={{0,7},{1,0},{2,1},{3,2},{4,3},{5,4},{6,5},{7,6},{8,15},{9,8},{10,9... | collective-permute-start | bytes 1179656 | tf_op jit(solution)/shard_map/ppermute | solution.py:29
  54.7 18.5 %collective-permute-start.7 = (bf16[128,1536]{1,0:T(8,128)(2,1)S(1)}, bf16[128,1536]{1,0:T(8,128)(2,1)S(1)}, u32[]{:S(2)}, u32[]{:S(2)}) collective-permute-start(bf16[128,1536]{1,0:T(8,128)(2,1)S(1)} %fusion.3), channel_id=1, source_target_pairs={{0,80},{1,81},{2,82},{3,83},{4,84},{5,85},{6,86},{7,87},{8,88},{9,... | collective-permute-start | bytes 1179656 | tf_op jit(solution)/shard_map/ppermute | solution.py:29
  57.4 13.8 %collective-permute-start.13 = (bf16[128,1536]{1,0:T(8,128)(2,1)S(1)}, bf16[128,1536]{1,0:T(8,128)(2,1)S(1)}, u32[]{:S(2)}, u32[]{:S(2)}) collective-permute-start(bf16[128,1536]{1,0:T(8,128)(2,1)S(1)} %collective-permute-done.12.rest_7_.rest_15_), channel_id=1, source_target_pairs={{0,1},{1,2},{2,3},{3,4},{4,5},{5,6},{6,7},{7,0},{8,9},{9,10},{10,1... | collective-permute-start | bytes 1179656 | tf_op jit(solution)/shard_map/ppermute | solution.py:29
  59.7 13.5 %collective-permute-start.6 = (bf16[128,1536]{1,0:T(8,128)(2,1)S(1)}, bf16[128,1536]{1,0:T(8,128)(2,1)S(1)}, u32[]{:S(2)}, u32[]{:S(2)}) collective-permute-start(bf16[128,1536]{1,0:T(8,128)(2,1)S(1)} %add_convert_fusion.1), channel_id=1, source_target_pairs={{0,96},{1,97},{2,98},{3,99},{4,100},{5,101},{6,102},{7,103},{8,104... | collective-permute-start | bytes 1179656 | tf_op jit(solution)/shard_map/ppermute | solution.py:29
  63.5 11.5 %collective-permute-start.10 = (bf16[128,1536]{1,0:T(8,128)(2,1)S(1)}, bf16[128,1536]{1,0:T(8,128)(2,1)S(1)}, u32[]{:S(2)}, u32[]{:S(2)}) collective-permute-start(bf16[128,1536]{1,0:T(8,128)(2,1)S(1)} %collective-permute-done.9.rest_1_.rest_9_), channel_id=1, source_target_pairs={{0,7},{1,0},{2,1},{3,2},{4,3},{5,4},{6,5},{7,6},{8,15},{9,8},{10,9... | collective-permute-start | bytes 1179656 | tf_op jit(solution)/shard_map/ppermute | solution.py:29
  71.3 12.9 %collective-permute-start.14 = (bf16[128,1536]{1,0:T(8,128)(2,1)S(1)}, bf16[128,1536]{1,0:T(8,128)(2,1)S(1)}, u32[]{:S(2)}, u32[]{:S(2)}) collective-permute-start(bf16[128,1536]{1,0:T(8,128)(2,1)S(1)} %collective-permute-done.13.rest_6_.rest_14_), channel_id=1, source_target_pairs={{0,1},{1,2},{2,3},{3,4},{4,5},{5,6},{6,7},{7,0},{8,9},{9,10},{10,1... | collective-permute-start | bytes 1179656 | tf_op jit(solution)/shard_map/ppermute | solution.py:29
  73.4 15.5 %collective-permute-start.8 = (bf16[128,1536]{1,0:T(8,128)(2,1)S(1)}, bf16[128,1536]{1,0:T(8,128)(2,1)S(1)}, u32[]{:S(2)}, u32[]{:S(2)}) collective-permute-start(bf16[128,1536]{1,0:T(8,128)(2,1)S(1)} %fusion.61), channel_id=1, source_target_pairs={{80,464},{81,465},{82,466},{83,467},{84,468},{85,469},{86,470},{87... | collective-permute-start | bytes 1179656 | tf_op jit(solution)/shard_map/ppermute | solution.py:29
  75.1 13.9 %collective-permute-start.11 = (bf16[128,1536]{1,0:T(8,128)(2,1)S(1)}, bf16[128,1536]{1,0:T(8,128)(2,1)S(1)}, u32[]{:S(2)}, u32[]{:S(2)}) collective-permute-start(bf16[128,1536]{1,0:T(8,128)(2,1)S(1)} %collective-permute-done.10.rest_2_.rest_10_), channel_id=1, source_target_pairs={{0,7},{1,0},{2,1},{3,2},{4,3},{5,4},{6,5},{7,6},{8,15},{9,8},{10,9... | collective-permute-start | bytes 1179656 | tf_op jit(solution)/shard_map/ppermute | solution.py:29
  84.2 12.0 %collective-permute-start.15 = (bf16[128,1536]{1,0:T(8,128)(2,1)S(1)}, bf16[128,1536]{1,0:T(8,128)(2,1)S(1)}, u32[]{:S(2)}, u32[]{:S(2)}) collective-permute-start(bf16[128,1536]{1,0:T(8,128)(2,1)S(1)} %collective-permute-done.14.rest_5_.rest_13_), channel_id=1, source_target_pairs={{0,1},{1,2},{2,3},{3,4},{4,5},{5,6},{6,7},{7,0},{8,9},{9,10},{10,1... | collective-permute-start | bytes 1179656 | tf_op jit(solution)/shard_map/ppermute | solution.py:29
  100.1 7.0 %collective-permute-start.16 = (bf16[768,768]{1,0:T(8,128)(2,1)S(1)}, bf16[768,768]{1,0:T(8,128)(2,1)S(1)}, u32[]{:S(2)}, u32[]{:S(2)}) collective-permute-start(bf16[768,768]{1,0:T(8,128)(2,1)S(1)} %get-tuple-element.6), channel_id=1, source_target_pairs={{0,16},{1,17},{2,18},{3,19},{4,20},{5,21},{6,22},{7,23},{8,24},{9,... | collective-permute-start | bytes 3538952 | tf_op jit(solution)/shard_map/ppermute | solution.py:29
  108.3 9.2 %copy-start.13 = (f32[128]{0:T(128)S(1)}, f32[128]{0:T(128)}, u32[]{:S(2)}) copy-start(f32[128]{0:T(128)} %copy-done.12) | copy-start | bytes 1540
  108.3 38.9 %all-to-all-start = ((bf16[32,24,768]{2,1,0:T(8,128)(2,1)}), bf16[32,24,768]{2,1,0:T(8,128)(2,1)S(1)}, u32[]{:S(2)}, u32[]{:S(2)}) async-start(bf16[32,24,768]{2,1,0:T(8,128)(2,1)} %bitcast.2), calls=%async_computation | async-start | bytes 2359296 | tf_op jit(solution)/shard_map/all_to_all | solution.py:256
  (14 other events, 56.9 us)

commit v6 on v5

--- a/solution.py
+++ b/solution.py
@@ -113,48 +113,46 @@
     )
 
 
-def weight_product(hidden_units, blocks, done):
+def weight_product(hidden_units, blocks, after, leaving=False):
     units, depth = hidden_units.shape
     rows, width = blocks[0].shape
     tile = 256
     steps = width // (2 * tile)
-    keep = 2 * units // CORE
-    share = units // (CORE * X * Z_HI * Z_LO)
-
-    def kernel(hidden_ref, *rest):
-        kept_ref, sent_ref, laid = rest[-3:]
-        left = jnp.concatenate([ref[...] for ref in rest[:Y]])
-        right = jnp.concatenate([ref[...] for ref in rest[Y : 2 * Y]])
-        step = units // CORE
-        for at in range(0, units, step):
-            lines = hidden_ref[at : at + step]
-            to = kept_ref if at == 0 else laid
-            for side, columns in enumerate((left, right)):
-                value = jnp.dot(lines, columns, preferred_element_type=jnp.float32)
-                for k in range(step // share):
-                    first = (2 * k + side) * share
-                    to[first : first + share] = value[k * share : (k + 1) * share]
-        sent_ref[...] = laid[...].astype(sent_ref.dtype)
-
-    out = pl.BlockSpec((keep, tile), lambda n: (0, n))
+    share = units // (X * Z_HI * Z_LO)
+    count = len(blocks)
+    dtype = jnp.bfloat16 if leaving else jnp.float32
+
+    def kernel(*refs):
+        left, right = refs[1 : 1 + count], refs[1 + count : 1 + 2 * count]
+        out_ref, laid = refs[-2:]
+        lines = refs[0][...]
+        for side, columns in enumerate((left, right)):
+            value = jnp.dot(
+                lines,
+                jnp.concatenate([ref[...] for ref in columns]),
+                preferred_element_type=jnp.float32,
+            )
+            for k in range(units // share):
+                first = (2 * k + side) * share
+                laid[first : first + share] = value[k * share : (k + 1) * share]
+        out_ref[...] = laid[...].astype(dtype)
+
+    tiles = pl.BlockSpec((2 * units, tile), lambda n: (0, n))
     return pl.pallas_call(
         kernel,
         grid=(steps,),
         in_specs=[pl.BlockSpec((units, depth), lambda n: (0, 0))]
-        + [pl.BlockSpec((rows, tile), lambda n: (0, n))] * Y
-        + [pl.BlockSpec((rows, tile), lambda n: (0, n + steps))] * Y
-        + [pl.BlockSpec(memory_space=pl.ANY)] * len(done),
-        out_specs=[out, out],
-        out_shape=[
-            jax.ShapeDtypeStruct((keep, width // 2), jnp.float32),
-            jax.ShapeDtypeStruct((keep, width // 2), jnp.bfloat16),
-        ],
-        scratch_shapes=[pltpu.VMEM((keep, tile), jnp.float32)],
+        + [pl.BlockSpec((rows, tile), lambda n: (0, n))] * count
+        + [pl.BlockSpec((rows, tile), lambda n: (0, n + steps))] * count
+        + [pl.BlockSpec(memory_space=pl.ANY)] * len(after),
+        out_specs=tiles,
+        out_shape=jax.ShapeDtypeStruct((2 * units, width // 2), dtype),
+        scratch_shapes=[pltpu.VMEM((2 * units, tile), jnp.float32)],
         compiler_params=pltpu.CompilerParams(vmem_limit_bytes=40 * 2**20),
         cost_estimate=pl.CostEstimate(
-            flops=2 * units * depth * width, bytes_accessed=12 * 2**20, transcendentals=0
+            flops=2 * units * rows * count * width, bytes_accessed=6 * 2**20, transcendentals=0
         ),
-    )(hidden_units, *blocks, *blocks, *done)
+    )(hidden_units, *blocks, *blocks, *after)
 
 
 def local(img_emb, txt_emb, hidden, positives):
@@ -241,7 +239,9 @@
     text_total = text_parts[0] + staying + back_far.astype(jnp.float32)
     text_grad = backward_norm(text_unit, text_inv, text_total).astype(bf16)
 
-    kept, sent = weight_product(hidden_units, got, (back_far,))
+    mine, theirs = jnp.split(hidden_units, CORE)
+    sent = weight_product(theirs, got, (back_far,), True)
+    kept = weight_product(mine, got, ())
     total = kept + moved(sent, other_core).astype(jnp.float32)
     places = X * Z_HI * Z_LO
     peers = [

time: 150 us -> 148 us (0.987)
  waiting for transfers between devices: 51.5 us -> 48.9 us
    ppermute x17, waiting for transfers between devices: 23.4 us -> 20.8 us  [moved(): return lax.ppermute(value, ('loop', 'mp'), pairs)]
    pallas_call x1 -> x2, Pallas kernels: 3.82 us -> 4.79 us  [weight_product(): pl.pallas_call(kernel, grid=(steps,), in_specs=[pl.BlockSpec((units, dept...]
  transfers between devices with their start and end apart: 18 -> 18, of which waited for: 8 -> 7; matrix products, arithmetic and copies ran while one was open for 14% -> 14% of each run, Pallas kernels for 0% -> 2%
where the time goes in v6:
time: 148 us; the launch traced here: 147 us
  starting transfers between devices  65.3 us (44%)
  waiting for transfers between devices  48.9 us (33%)
  matrix products  13.9 us (9%)
  other arithmetic  9.62 us (6%)
  Pallas kernels  4.79 us (3%)
  between operations  2.24 us (2%)
  local copies, waits for them, and re-layouts  1.93 us (1%)
    ppermute x17, starting transfers between devices, moved(): return lax.ppermute(value, ('loop', 'mp'), pairs)  56.1 us
    all_to_all x1, waiting for transfers between devices, local(): lax.all_to_all(total.astype(bf16).reshape(places, 2 * share, width // 2),...  28.1 us
    ppermute x17, waiting for transfers between devices, moved(): return lax.ppermute(value, ('loop', 'mp'), pairs)  20.8 us
    all_to_all x1, starting transfers between devices, local(): lax.all_to_all(total.astype(bf16).reshape(places, 2 * share, width // 2),...  9.17 us
    unnamed x2, matrix products  5.71 us
    pallas_call x2, Pallas kernels, weight_product(): pl.pallas_call(kernel, grid=(steps,), in_specs=[pl.BlockSpec((units, dept...  4.79 us
    dot_general x4, matrix products, pair_terms(): lax.dot_general(image_low, text_low, (((1,), (1,)), ((), ())), preferred_...  3.39 us
    dot_general x4, matrix products, pair_terms(): jnp.dot(coefficient, text_low, preferred_element_type=jnp.float32)  3.15 us
  transfers between devices with their start and end apart: 18, of which 7 were waited for; matrix products, arithmetic and copies ran while one was open for 14% of the time, Pallas kernels for 2%

profile of v6, /device:TPU:1, one launch (start us, length us, event | category | flops | bytes accessed | tf_op | source)
XLA Modules:
  0.0 146.6 jit_solution(10918437334137132127)
XLA Ops:
  3.1 4.0 %collective-permute-start = (bf16[128,1536]{1,0:T(8,128)(2,1)S(1)}, bf16[128,1536]{1,0:T(8,128)(2,1)}, u32[]{:S(2)}, u32[]{:S(2)}) collective-permute-start(bf16[128,1536]{1,0:T(8,128)(2,1)S(1)} %fusion.43), channel_id=1, source_target_pairs={{0,32},{1,33},{2,34},{3,35},{4,36},{5,37},{6,38},{7,39},{8,40},{9,... | collective-permute-start | bytes 1179656 | tf_op jit(solution)/shard_map/ppermute | solution.py:29
  7.1 5.2 %collective-permute-start.2 = (bf16[128,1536]{1,0:T(8,128)(2,1)S(1)}, bf16[128,1536]{1,0:T(8,128)(2,1)}, u32[]{:S(2)}, u32[]{:S(2)}) collective-permute-start(bf16[128,1536]{1,0:T(8,128)(2,1)S(1)} %fusion.43), channel_id=1, source_target_pairs={{0,16},{1,17},{2,18},{3,19},{4,20},{5,21},{6,22},{7,23},{8,24},{9,... | collective-permute-start | bytes 1179656 | tf_op jit(solution)/shard_map/ppermute | solution.py:29
  16.8 4.0 %collective-permute-start.4 = (bf16[1024,384]{1,0:T(8,128)(2,1)S(1)}, bf16[1024,384]{1,0:T(8,128)(2,1)}, u32[]{:S(2)}, u32[]{:S(2)}) collective-permute-start(bf16[1024,384]{1,0:T(8,128)(2,1)S(1)} %fusion.63), channel_id=1, source_target_pairs={{0,8},{1,9},{2,10},{3,11},{4,12},{5,13},{6,14},{7,15},{8,0},{9,1},... | collective-permute-start | bytes 2359304 | tf_op jit(solution)/shard_map/ppermute | solution.py:29
  21.1 3.0 %convolution_convert_fusion.1 = bf16[768,1024]{1,0:T(8,128)(2,1)} fusion(s32[]{:T(128)S(6)} %select_n.156, bf16[1024,384]{1,0:T(8,128)(2,1)S(1)} %copy-done.3, s32[]{:T(128)S(6)} %select_n.143, s32[768]{0:T(1024)S(1)} %get-tuple-element.21, s32[768]{0:T(1024)S(1)} %get-tuple-element.24, pred[768]{0:T(1024)(128)(4,1)S(1)} %get-tuple-element.17, ...), kind=kOutput, calls=%fused_computation.26 | convolution fusion | flops 620691456 | bytes 2386958
  25.4 3.9 %collective-permute-done = bf16[128,1536]{1,0:T(8,128)(2,1)} collective-permute-done((bf16[128,1536]{1,0:T(8,128)(2,1)S(1)}, bf16[128,1536]{1,0:T(8,128)(2,1)}, u32[]{:S(2)}, u32[]{:S(2)}) %collective-permute-start) | collective-permute-done | bytes 393248 | tf_op jit(solution)/shard_map/ppermute | solution.py:29
  29.3 5.9 %collective-permute-start.3 = (bf16[128,1536]{1,0:T(8,128)(2,1)}, bf16[128,1536]{1,0:T(8,128)(2,1)S(1)}, u32[]{:S(2)}, u32[]{:S(2)}) collective-permute-start(bf16[128,1536]{1,0:T(8,128)(2,1)} %collective-permute-done), channel_id=1, source_target_pairs={{0,16},{1,17},{2,18},{3,19},{4,20},{5,21},{6,22},{7,23},{8,24},{9,... | collective-permute-start | bytes 1179656 | tf_op jit(solution)/shard_map/ppermute | solution.py:29
  44.7 2.2 %collective-permute-start.12 = (bf16[128,1536]{1,0:T(8,128)(2,1)S(1)}, bf16[128,1536]{1,0:T(8,128)(2,1)S(1)}, u32[]{:S(2)}, u32[]{:S(2)}) collective-permute-start(bf16[128,1536]{1,0:T(8,128)(2,1)S(1)} %fusion.50.refs_1_.refs_9_), channel_id=1, source_target_pairs={{0,1},{1,2},{2,3},{3,4},{4,5},{5,6},{6,7},{7,0},{8,9},{9,10},{10,1... | collective-permute-start | bytes 1179656 | tf_op jit(solution)/shard_map/ppermute | solution.py:29
  48.2 1.9 %collective-permute-start.5 = (bf16[128,1536]{1,0:T(8,128)(2,1)S(1)}, bf16[128,1536]{1,0:T(8,128)(2,1)S(1)}, u32[]{:S(2)}, u32[]{:S(2)}) collective-permute-start(bf16[128,1536]{1,0:T(8,128)(2,1)S(1)} %fusion.2), channel_id=1, source_target_pairs={{0,16},{1,17},{2,18},{3,19},{4,20},{5,21},{6,22},{7,23},{8,24},{9,... | collective-permute-start | bytes 1179656 | tf_op jit(solution)/shard_map/ppermute | solution.py:29
  50.1 4.3 %collective-permute-start.9 = (bf16[128,1536]{1,0:T(8,128)(2,1)S(1)}, bf16[128,1536]{1,0:T(8,128)(2,1)S(1)}, u32[]{:S(2)}, u32[]{:S(2)}) collective-permute-start(bf16[128,1536]{1,0:T(8,128)(2,1)S(1)} %fusion.50.refs_1_.refs_9_), channel_id=1, source_target_pairs={{0,7},{1,0},{2,1},{3,2},{4,3},{5,4},{6,5},{7,6},{8,15},{9,8},{10,9... | collective-permute-start | bytes 1179656 | tf_op jit(solution)/shard_map/ppermute | solution.py:29
  54.7 2.7 %collective-permute-start.7 = (bf16[128,1536]{1,0:T(8,128)(2,1)S(1)}, bf16[128,1536]{1,0:T(8,128)(2,1)S(1)}, u32[]{:S(2)}, u32[]{:S(2)}) collective-permute-start(bf16[128,1536]{1,0:T(8,128)(2,1)S(1)} %fusion.3), channel_id=1, source_target_pairs={{0,80},{1,81},{2,82},{3,83},{4,84},{5,85},{6,86},{7,87},{8,88},{9,... | collective-permute-start | bytes 1179656 | tf_op jit(solution)/shard_map/ppermute | solution.py:29
  57.4 1.9 %collective-permute-start.13 = (bf16[128,1536]{1,0:T(8,128)(2,1)S(1)}, bf16[128,1536]{1,0:T(8,128)(2,1)S(1)}, u32[]{:S(2)}, u32[]{:S(2)}) collective-permute-start(bf16[128,1536]{1,0:T(8,128)(2,1)S(1)} %collective-permute-done.12.refs_8_.refs_16_), channel_id=1, source_target_pairs={{0,1},{1,2},{2,3},{3,4},{4,5},{5,6},{6,7},{7,0},{8,9},{9,10},{10,1... | collective-permute-start | bytes 1179656 | tf_op jit(solution)/shard_map/ppermute | solution.py:29
  59.7 3.8 %collective-permute-start.6 = (bf16[128,1536]{1,0:T(8,128)(2,1)S(1)}, bf16[128,1536]{1,0:T(8,128)(2,1)S(1)}, u32[]{:S(2)}, u32[]{:S(2)}) collective-permute-start(bf16[128,1536]{1,0:T(8,128)(2,1)S(1)} %add_convert_fusion.1), channel_id=1, source_target_pairs={{0,96},{1,97},{2,98},{3,99},{4,100},{5,101},{6,102},{7,103},{8,104... | collective-permute-start | bytes 1179656 | tf_op jit(solution)/shard_map/ppermute | solution.py:29
  63.5 4.6 %collective-permute-start.10 = (bf16[128,1536]{1,0:T(8,128)(2,1)S(1)}, bf16[128,1536]{1,0:T(8,128)(2,1)S(1)}, u32[]{:S(2)}, u32[]{:S(2)}) collective-permute-start(bf16[128,1536]{1,0:T(8,128)(2,1)S(1)} %collective-permute-done.9.refs_2_.refs_10_), channel_id=1, source_target_pairs={{0,7},{1,0},{2,1},{3,2},{4,3},{5,4},{6,5},{7,6},{8,15},{9,8},{10,9... | collective-permute-start | bytes 1179656 | tf_op jit(solution)/shard_map/ppermute | solution.py:29
  68.1 3.1 %collective-permute-done.13.refs_7_.refs_15_ = bf16[128,1536]{1,0:T(8,128)(2,1)S(1)} collective-permute-done((bf16[128,1536]{1,0:T(8,128)(2,1)S(1)}, bf16[128,1536]{1,0:T(8,128)(2,1)S(1)}, u32[]{:S(2)}, u32[]{:S(2)}) %collective-permute-start.13) | collective-permute-done | bytes 393248 | tf_op jit(solution)/shard_map/ppermute | solution.py:29
  75.1 5.3 %collective-permute-start.11 = (bf16[128,1536]{1,0:T(8,128)(2,1)S(1)}, bf16[128,1536]{1,0:T(8,128)(2,1)S(1)}, u32[]{:S(2)}, u32[]{:S(2)}) collective-permute-start(bf16[128,1536]{1,0:T(8,128)(2,1)S(1)} %collective-permute-done.10.refs_3_.refs_11_), channel_id=1, source_target_pairs={{0,7},{1,0},{2,1},{3,2},{4,3},{5,4},{6,5},{7,6},{8,15},{9,8},{10,9... | collective-permute-start | bytes 1179656 | tf_op jit(solution)/shard_map/ppermute | solution.py:29
  80.4 3.8 %collective-permute-done.14.refs_6_.refs_14_ = bf16[128,1536]{1,0:T(8,128)(2,1)S(1)} collective-permute-done((bf16[128,1536]{1,0:T(8,128)(2,1)S(1)}, bf16[128,1536]{1,0:T(8,128)(2,1)S(1)}, u32[]{:S(2)}, u32[]{:S(2)}) %collective-permute-start.14) | collective-permute-done | bytes 393248 | tf_op jit(solution)/shard_map/ppermute | solution.py:29
  84.2 1.9 %collective-permute-start.15 = (bf16[128,1536]{1,0:T(8,128)(2,1)S(1)}, bf16[128,1536]{1,0:T(8,128)(2,1)S(1)}, u32[]{:S(2)}, u32[]{:S(2)}) collective-permute-start(bf16[128,1536]{1,0:T(8,128)(2,1)S(1)} %collective-permute-done.14.refs_6_.refs_14_), channel_id=1, source_target_pairs={{0,1},{1,2},{2,3},{3,4},{4,5},{5,6},{6,7},{7,0},{8,9},{9,10},{10,1... | collective-permute-start | bytes 1179656 | tf_op jit(solution)/shard_map/ppermute | solution.py:29
  86.1 2.8 %fusion.4 = bf16[768,1024]{1,0:T(8,128)(2,1)S(1)} fusion(bf16[768,1024]{1,0:T(8,128)(2,1)} %convolution_convert_fusion.1, bf16[1024,384]{1,0:T(8,128)(2,1)} %collective-permute-done.4, s32[]{:T(128)S(6)} %select_n.143, s32[768]{0:T(1024)S(1)} %get-tuple-element.21, s32[768]{0:T(1024)} %copy-done.7, pred[768]{0:T(1024)(128)(4,1)} %copy-done.14, ...), kind=kOutput, calls=%fused_computation.31 | convolution fusion | flops 619118592 | bytes 3959816
  89.1 7.2 %collective-permute-done.15.refs_5_.refs_13_ = bf16[128,1536]{1,0:T(8,128)(2,1)S(1)} collective-permute-done((bf16[128,1536]{1,0:T(8,128)(2,1)S(1)}, bf16[128,1536]{1,0:T(8,128)(2,1)S(1)}, u32[]{:S(2)}, u32[]{:S(2)}) %collective-permute-start.15) | collective-permute-done | bytes 393248 | tf_op jit(solution)/shard_map/ppermute | solution.py:29
  96.2 2.3 %shard_map.60 = bf16[768,768]{1,0:T(8,128)(2,1)S(1)} custom-call(bf16[384,1024]{1,0:T(8,128)(2,1)S(1)} %get-tuple-element.3.refs_0_, bf16[128,1536]{1,0:T(8,128)(2,1)S(1)} %fusion.50.refs_1_.refs_9_, bf16[128,1536]{1,0:T(8,128)(2,1)S(1)} %collective-permute-done.9.refs_2_.refs_10_, bf16[128,1536]{1,0:T(8,128)(2,1)S(1)} %collective-permute-done.10.refs_3_.refs_11_, ...), custom_call_target="tpu_custom_call" | custom-call | flops 1207959552 | bytes 6291456 | tf_op jit(solution)/shard_map/pallas_call | solution.py:141
  98.6 4.5 %collective-permute-start.16 = (bf16[768,768]{1,0:T(8,128)(2,1)S(1)}, bf16[768,768]{1,0:T(8,128)(2,1)S(1)}, u32[]{:S(2)}, u32[]{:S(2)}) collective-permute-start(bf16[768,768]{1,0:T(8,128)(2,1)S(1)} %shard_map.60), channel_id=1, source_target_pairs={{0,16},{1,17},{2,18},{3,19},{4,20},{5,21},{6,22},{7,23},{8,24},{9,... | collective-permute-start | bytes 3538952 | tf_op jit(solution)/shard_map/ppermute | solution.py:29
  103.1 2.4 %shard_map.59 = f32[768,768]{1,0:T(8,128)S(1)} custom-call(bf16[384,1024]{1,0:T(8,128)(2,1)S(1)} %get-tuple-element.4.refs_0_, bf16[128,1536]{1,0:T(8,128)(2,1)S(1)} %fusion.50.refs_1_.refs_9_, bf16[128,1536]{1,0:T(8,128)(2,1)S(1)} %collective-permute-done.9.refs_2_.refs_10_, bf16[128,1536]{1,0:T(8,128)(2,1)S(1)} %collective-permute-done.10.refs_3_.refs_11_, ...), custom_call_target="tpu_custom_call" | custom-call | flops 1207959552 | bytes 6291456 | tf_op jit(solution)/shard_map/pallas_call | solution.py:141
  106.8 9.2 %all-to-all-start = ((bf16[32,24,768]{2,1,0:T(8,128)(2,1)}), bf16[32,24,768]{2,1,0:T(8,128)(2,1)S(1)}, u32[]{:S(2)}, u32[]{:S(2)}) async-start(bf16[32,24,768]{2,1,0:T(8,128)(2,1)} %bitcast.2), calls=%async_computation | async-start | bytes 2359296 | tf_op jit(solution)/shard_map/all_to_all | solution.py:256
  117.7 28.1 %all-to-all-done = bf16[32,24,768]{2,1,0:T(8,128)(2,1)S(1)} async-done(((bf16[32,24,768]{2,1,0:T(8,128)(2,1)}), bf16[32,24,768]{2,1,0:T(8,128)(2,1)S(1)}, u32[]{:S(2)}, u32[]{:S(2)}) %all-to-all-start) | async-done | bytes 1179680 | tf_op jit(solution)/shard_map/all_to_all | solution.py:256
  (98 shorter events, 26.4 us)
Async XLA Ops:
  0.6 11.7 %copy-start = (bf16[128,1536]{1,0:T(8,128)(2,1)S(1)}, bf16[128,1536]{1,0:T(8,128)(2,1)}, u32[]{:S(2)}) copy-start(bf16[128,1536]{1,0:T(8,128)(2,1)} %param.6) | copy-start | bytes 1179652
  0.6 11.9 %copy-start.18 = (s32[128]{0:T(128)S(1)}, s32[128]{0:T(128)}, u32[]{:S(2)}) copy-start(s32[128]{0:T(128)} %param.9) | copy-start | bytes 1540
  1.9 10.7 %copy-start.12 = (f32[128]{0:T(128)}, f32[128]{0:T(128)S(1)}, u32[]{:S(2)}) copy-start(f32[128]{0:T(128)S(1)} %add_rsqrt_fusion) | copy-start | bytes 1540
  1.9 12.3 %copy-start.2 = (bf16[2048,384]{1,0:T(8,128)(2,1)S(1)}, bf16[2048,384]{1,0:T(8,128)(2,1)}, u32[]{:S(2)}) copy-start(bf16[2048,384]{1,0:T(8,128)(2,1)} %param.8) | copy-start | bytes 4718596
  3.1 26.2 %collective-permute-start = (bf16[128,1536]{1,0:T(8,128)(2,1)S(1)}, bf16[128,1536]{1,0:T(8,128)(2,1)}, u32[]{:S(2)}, u32[]{:S(2)}) collective-permute-start(bf16[128,1536]{1,0:T(8,128)(2,1)S(1)} %fusion.43), channel_id=1, source_target_pairs={{0,32},{1,33},{2,34},{3,35},{4,36},{5,37},{6,38},{7,39},{8,40},{9,... | collective-permute-start | bytes 1179656 | tf_op jit(solution)/shard_map/ppermute | solution.py:29
  7.1 32.8 %collective-permute-start.2 = (bf16[128,1536]{1,0:T(8,128)(2,1)S(1)}, bf16[128,1536]{1,0:T(8,128)(2,1)}, u32[]{:S(2)}, u32[]{:S(2)}) collective-permute-start(bf16[128,1536]{1,0:T(8,128)(2,1)S(1)} %fusion.43), channel_id=1, source_target_pairs={{0,16},{1,17},{2,18},{3,19},{4,20},{5,21},{6,22},{7,23},{8,24},{9,... | collective-permute-start | bytes 1179656 | tf_op jit(solution)/shard_map/ppermute | solution.py:29
  12.9 12.2 %copy-start.4 = (bf16[128,128]{1,0:T(8,128)(2,1)}, bf16[128,128]{1,0:T(8,128)(2,1)S(1)}, u32[]{:S(2)}) copy-start(bf16[128,128]{1,0:T(8,128)(2,1)S(1)} %fusion.37) | copy-start | bytes 98308
  16.8 30.2 %collective-permute-start.4 = (bf16[1024,384]{1,0:T(8,128)(2,1)S(1)}, bf16[1024,384]{1,0:T(8,128)(2,1)}, u32[]{:S(2)}, u32[]{:S(2)}) collective-permute-start(bf16[1024,384]{1,0:T(8,128)(2,1)S(1)} %fusion.63), channel_id=1, source_target_pairs={{0,8},{1,9},{2,10},{3,11},{4,12},{5,13},{6,14},{7,15},{8,0},{9,1},... | collective-permute-start | bytes 2359304 | tf_op jit(solution)/shard_map/ppermute | solution.py:29
  29.3 9.9 %collective-permute-start.3 = (bf16[128,1536]{1,0:T(8,128)(2,1)}, bf16[128,1536]{1,0:T(8,128)(2,1)S(1)}, u32[]{:S(2)}, u32[]{:S(2)}) collective-permute-start(bf16[128,1536]{1,0:T(8,128)(2,1)} %collective-permute-done), channel_id=1, source_target_pairs={{0,16},{1,17},{2,18},{3,19},{4,20},{5,21},{6,22},{7,23},{8,24},{9,... | collective-permute-start | bytes 1179656 | tf_op jit(solution)/shard_map/ppermute | solution.py:29
  35.3 6.3 %collective-permute-start.1 = (bf16[128,1536]{1,0:T(8,128)(2,1)}, bf16[128,1536]{1,0:T(8,128)(2,1)S(1)}, u32[]{:S(2)}, u32[]{:S(2)}) collective-permute-start(bf16[128,1536]{1,0:T(8,128)(2,1)} %collective-permute-done), channel_id=1, source_target_pairs={{16,32},{17,33},{18,34},{19,35},{20,36},{21,37},{22,38},{23,39},{2... | collective-permute-start | bytes 1179656 | tf_op jit(solution)/shard_map/ppermute | solution.py:29
  44.7 12.7 %collective-permute-start.12 = (bf16[128,1536]{1,0:T(8,128)(2,1)S(1)}, bf16[128,1536]{1,0:T(8,128)(2,1)S(1)}, u32[]{:S(2)}, u32[]{:S(2)}) collective-permute-start(bf16[128,1536]{1,0:T(8,128)(2,1)S(1)} %fusion.50.refs_1_.refs_9_), channel_id=1, source_target_pairs={{0,1},{1,2},{2,3},{3,4},{4,5},{5,6},{6,7},{7,0},{8,9},{9,10},{10,1... | collective-permute-start | bytes 1179656 | tf_op jit(solution)/shard_map/ppermute | solution.py:29
  48.2 11.2 %collective-permute-start.5 = (bf16[128,1536]{1,0:T(8,128)(2,1)S(1)}, bf16[128,1536]{1,0:T(8,128)(2,1)S(1)}, u32[]{:S(2)}, u32[]{:S(2)}) collective-permute-start(bf16[128,1536]{1,0:T(8,128)(2,1)S(1)} %fusion.2), channel_id=1, source_target_pairs={{0,16},{1,17},{2,18},{3,19},{4,20},{5,21},{6,22},{7,23},{8,24},{9,... | collective-permute-start | bytes 1179656 | tf_op jit(solution)/shard_map/ppermute | solution.py:29
  50.1 13.4 %collective-permute-start.9 = (bf16[128,1536]{1,0:T(8,128)(2,1)S(1)}, bf16[128,1536]{1,0:T(8,128)(2,1)S(1)}, u32[]{:S(2)}, u32[]{:S(2)}) collective-permute-start(bf16[128,1536]{1,0:T(8,128)(2,1)S(1)} %fusion.50.refs_1_.refs_9_), channel_id=1, source_target_pairs={{0,7},{1,0},{2,1},{3,2},{4,3},{5,4},{6,5},{7,6},{8,15},{9,8},{10,9... | collective-permute-start | bytes 1179656 | tf_op jit(solution)/shard_map/ppermute | solution.py:29
  54.7 18.5 %collective-permute-start.7 = (bf16[128,1536]{1,0:T(8,128)(2,1)S(1)}, bf16[128,1536]{1,0:T(8,128)(2,1)S(1)}, u32[]{:S(2)}, u32[]{:S(2)}) collective-permute-start(bf16[128,1536]{1,0:T(8,128)(2,1)S(1)} %fusion.3), channel_id=1, source_target_pairs={{0,80},{1,81},{2,82},{3,83},{4,84},{5,85},{6,86},{7,87},{8,88},{9,... | collective-permute-start | bytes 1179656 | tf_op jit(solution)/shard_map/ppermute | solution.py:29
  57.4 13.8 %collective-permute-start.13 = (bf16[128,1536]{1,0:T(8,128)(2,1)S(1)}, bf16[128,1536]{1,0:T(8,128)(2,1)S(1)}, u32[]{:S(2)}, u32[]{:S(2)}) collective-permute-start(bf16[128,1536]{1,0:T(8,128)(2,1)S(1)} %collective-permute-done.12.refs_8_.refs_16_), channel_id=1, source_target_pairs={{0,1},{1,2},{2,3},{3,4},{4,5},{5,6},{6,7},{7,0},{8,9},{9,10},{10,1... | collective-permute-start | bytes 1179656 | tf_op jit(solution)/shard_map/ppermute | solution.py:29
  59.7 13.5 %collective-permute-start.6 = (bf16[128,1536]{1,0:T(8,128)(2,1)S(1)}, bf16[128,1536]{1,0:T(8,128)(2,1)S(1)}, u32[]{:S(2)}, u32[]{:S(2)}) collective-permute-start(bf16[128,1536]{1,0:T(8,128)(2,1)S(1)} %add_convert_fusion.1), channel_id=1, source_target_pairs={{0,96},{1,97},{2,98},{3,99},{4,100},{5,101},{6,102},{7,103},{8,104... | collective-permute-start | bytes 1179656 | tf_op jit(solution)/shard_map/ppermute | solution.py:29
  63.5 11.5 %collective-permute-start.10 = (bf16[128,1536]{1,0:T(8,128)(2,1)S(1)}, bf16[128,1536]{1,0:T(8,128)(2,1)S(1)}, u32[]{:S(2)}, u32[]{:S(2)}) collective-permute-start(bf16[128,1536]{1,0:T(8,128)(2,1)S(1)} %collective-permute-done.9.refs_2_.refs_10_), channel_id=1, source_target_pairs={{0,7},{1,0},{2,1},{3,2},{4,3},{5,4},{6,5},{7,6},{8,15},{9,8},{10,9... | collective-permute-start | bytes 1179656 | tf_op jit(solution)/shard_map/ppermute | solution.py:29
  71.3 12.9 %collective-permute-start.14 = (bf16[128,1536]{1,0:T(8,128)(2,1)S(1)}, bf16[128,1536]{1,0:T(8,128)(2,1)S(1)}, u32[]{:S(2)}, u32[]{:S(2)}) collective-permute-start(bf16[128,1536]{1,0:T(8,128)(2,1)S(1)} %collective-permute-done.13.refs_7_.refs_15_), channel_id=1, source_target_pairs={{0,1},{1,2},{2,3},{3,4},{4,5},{5,6},{6,7},{7,0},{8,9},{9,10},{10,1... | collective-permute-start | bytes 1179656 | tf_op jit(solution)/shard_map/ppermute | solution.py:29
  73.4 15.7 %collective-permute-start.8 = (bf16[128,1536]{1,0:T(8,128)(2,1)S(1)}, bf16[128,1536]{1,0:T(8,128)(2,1)S(1)}, u32[]{:S(2)}, u32[]{:S(2)}) collective-permute-start(bf16[128,1536]{1,0:T(8,128)(2,1)S(1)} %fusion.61), channel_id=1, source_target_pairs={{80,464},{81,465},{82,466},{83,467},{84,468},{85,469},{86,470},{87... | collective-permute-start | bytes 1179656 | tf_op jit(solution)/shard_map/ppermute | solution.py:29
  75.1 14.0 %collective-permute-start.11 = (bf16[128,1536]{1,0:T(8,128)(2,1)S(1)}, bf16[128,1536]{1,0:T(8,128)(2,1)S(1)}, u32[]{:S(2)}, u32[]{:S(2)}) collective-permute-start(bf16[128,1536]{1,0:T(8,128)(2,1)S(1)} %collective-permute-done.10.refs_3_.refs_11_), channel_id=1, source_target_pairs={{0,7},{1,0},{2,1},{3,2},{4,3},{5,4},{6,5},{7,6},{8,15},{9,8},{10,9... | collective-permute-start | bytes 1179656 | tf_op jit(solution)/shard_map/ppermute | solution.py:29
  84.2 12.0 %collective-permute-start.15 = (bf16[128,1536]{1,0:T(8,128)(2,1)S(1)}, bf16[128,1536]{1,0:T(8,128)(2,1)S(1)}, u32[]{:S(2)}, u32[]{:S(2)}) collective-permute-start(bf16[128,1536]{1,0:T(8,128)(2,1)S(1)} %collective-permute-done.14.refs_6_.refs_14_), channel_id=1, source_target_pairs={{0,1},{1,2},{2,3},{3,4},{4,5},{5,6},{6,7},{7,0},{8,9},{9,10},{10,1... | collective-permute-start | bytes 1179656 | tf_op jit(solution)/shard_map/ppermute | solution.py:29
  98.6 7.0 %collective-permute-start.16 = (bf16[768,768]{1,0:T(8,128)(2,1)S(1)}, bf16[768,768]{1,0:T(8,128)(2,1)S(1)}, u32[]{:S(2)}, u32[]{:S(2)}) collective-permute-start(bf16[768,768]{1,0:T(8,128)(2,1)S(1)} %shard_map.60), channel_id=1, source_target_pairs={{0,16},{1,17},{2,18},{3,19},{4,20},{5,21},{6,22},{7,23},{8,24},{9,... | collective-permute-start | bytes 3538952 | tf_op jit(solution)/shard_map/ppermute | solution.py:29
  106.8 9.2 %copy-start.13 = (f32[128]{0:T(128)S(1)}, f32[128]{0:T(128)}, u32[]{:S(2)}) copy-start(f32[128]{0:T(128)} %copy-done.12) | copy-start | bytes 1540
  106.8 38.9 %all-to-all-start = ((bf16[32,24,768]{2,1,0:T(8,128)(2,1)}), bf16[32,24,768]{2,1,0:T(8,128)(2,1)S(1)}, u32[]{:S(2)}, u32[]{:S(2)}) async-start(bf16[32,24,768]{2,1,0:T(8,128)(2,1)} %bitcast.2), calls=%async_computation | async-start | bytes 2359296 | tf_op jit(solution)/shard_map/all_to_all | solution.py:256
  (14 other events, 56.9 us)
